TPU v7x, 128 devices: a whole 4x4x4 slice. The times are simulated.
128 devices in a mesh: scen: 32 (over z, y, x_lo), asset: 4 (over x_hi, core).
Axes of the slice: x: 4 (x_hi: 2, x_lo: 2; x = x_hi * 2 + x_lo), y: 4, z: 4, core: 2. Of those that a mesh axis runs over, the one named last changes fastest.
Arguments:
- returns: bfloat16 [196608, 6144], P('scen', 'asset'), may hold values from -1 to 1
- mean_return: float32 [6144], P('asset'), may hold values from -1 to 2
- targets: float32 [64], replicated, may hold values from 0.2 to 0.8
- weights: float32 [64, 6144], P(None, 'asset'), may hold values from 0 to 12
- threshold: float32 [64], replicated, may hold values from 0 to 1
- hinge_duals: float32 [64, 196608], P(None, 'scen'), may hold values from 0 to 1
- multiplier: float32 [64], replicated, may hold values from 0 to 0.5
Outputs:
- weights_out: float32 [64, 6144], P(None, 'asset')
- threshold_out: float32 [64], replicated
- duals_out: float32 [64, 196608], P(None, 'scen')
- multiplier_out: float32 [64], replicated
- tail_risk: float32 [64], replicated
All inputs are finite; a program needn't handle non-finite values.
Results may differ from a plain program's by a relative error of at most 0.006.
The roundings to bfloat16 on the way count: a program that leaves them out, or rounds other values in their place, can miss the bound.
Values sent between devices are 32-bit elements; how exact they have to be, the bound alone decides.
No kernel may reach another device: no remote copies, remote signals or barrier semaphores. Data moves between devices by JAX's collectives and lax.ppermute only.
A program may use at most 128 MiB of HBM per device.

v0:
```python
import math

import jax
import jax.numpy as jnp
from jax import lax
from jax.sharding import PartitionSpec as P

BISECT = 6
ITERS = 2


TAIL = 0.2
STEP_V = 1.0
STEP_T = 0.5
STEP_U = 0.5
STEP_L = 2.0


def joined(part, axis, combine):
    gathered = jax.tree.map(lambda a: lax.all_gather(a, axis), part)

    def take(source):
        return jax.tree.map(lambda a: lax.dynamic_index_in_dim(a, source, 0, False), gathered)

    return lax.fori_loop(
        1, lax.axis_size(axis), lambda source, state: combine(state, take(source)), take(0)
    )


def merge_stats(first_pair, second_pair):
    return (first_pair[0] + second_pair[0], jnp.maximum(first_pair[1], second_pair[1]))


def shared_stats(row_sums, row_maxima):
    return joined((row_sums, row_maxima), "asset", merge_stats)


def shared_sum(values):
    return lax.psum(values, "asset")


def bisect(matrix, total_cols, add_rows, stats):
    row_total, row_top = stats(jnp.sum(matrix, 1), jnp.max(matrix, 1))
    lower = row_total / total_cols - 1.0
    upper = row_top
    f_up = jnp.zeros_like(lower) - total_cols

    def excess_at(level):
        return add_rows(jnp.sum(jnp.maximum(matrix - level[:, None], 0.0), 1)) - total_cols

    def sweep_once(bounds):
        lower, upper, f_low, f_up = bounds
        middle = (lower + upper) * 0.5
        excess = excess_at(middle)
        raise_low = excess >= 0
        return (
            jnp.where(raise_low, middle, lower),
            jnp.where(raise_low, upper, middle),
            jnp.where(raise_low, excess, f_low),
            jnp.where(raise_low, f_up, excess),
        )

    def first_then_rest(index, bounds):
        return sweep_once(bounds)

    f_low = excess_at(lower)
    lower, upper, f_low, f_up = lax.fori_loop(
        0, BISECT, first_then_rest, (lower, upper, f_low, f_up)
    )
    theta = lower + f_low * (upper - lower) / (f_low - f_up)
    return jnp.maximum(matrix - theta[:, None], 0.0)


def summed(loss_part, ret_part):
    return lax.psum((loss_part, ret_part), "asset")


def loss_terms(alloc, returns, mean_return):
    loss_part = -lax.dot_general(
        alloc.astype(jnp.bfloat16),
        returns,
        (((1,), (1,)), ((), ())),
        preferred_element_type=jnp.float32,
    )
    ret_part = jnp.sum(alloc * mean_return[None, :], 1)
    return (loss_part, ret_part)


def operate(current, returns, mean_return, targets):
    weights, threshold, hinge_duals, multiplier = current
    kcount, local_cols = weights.shape
    scen_rows = returns.shape[0]
    n_scen = lax.axis_size("scen")
    n_asset = lax.axis_size("asset")
    total_cols = local_cols * n_asset
    total_rows = scen_rows * n_scen
    step_scale = math.sqrt(total_cols / total_rows)
    dual_bf = hinge_duals.astype(jnp.bfloat16)
    grad_part = jnp.dot(dual_bf, returns, preferred_element_type=jnp.float32)
    mass_part = jnp.sum(hinge_duals, 1)
    gradient, dual_mass = lax.psum((grad_part, mass_part), "scen")
    shifted = weights + STEP_V * (
        step_scale * gradient + multiplier[:, None] * mean_return[None, :]
    )
    new_weights = bisect(shifted, total_cols, shared_sum, shared_stats)
    new_threshold = threshold - STEP_T * (1.0 - dual_mass / total_rows / TAIL)
    bar_weights = 2.0 * new_weights - weights
    bar_threshold = 2.0 * new_threshold - threshold
    loss_part, ret_part = loss_terms(bar_weights, returns, mean_return)
    loss_cols, expected_sum = summed(loss_part, ret_part)
    new_duals = jnp.clip(hinge_duals + STEP_U * (loss_cols - bar_threshold[:, None]), 0.0, 1.0)
    new_multiplier = jnp.maximum(multiplier + STEP_L * (targets - expected_sum / total_cols), 0.0)
    return (new_weights, new_threshold, new_duals, new_multiplier)


def local(returns, mean_return, targets, weights, threshold, hinge_duals, multiplier):
    anchor = (weights, threshold, hinge_duals, multiplier)
    current = anchor
    for sweep in range(ITERS):
        updated = operate(current, returns, mean_return, targets)
        weight_old = (sweep + 1.0) / (sweep + 2.0)
        current = tuple(
            (
                weight_old * (2.0 * fresh_part - old_part) + start_part / (sweep + 2.0)
                for fresh_part, old_part, start_part in zip(updated, current, anchor)
            )
        )
    weights_out, threshold_out, duals_out, multiplier_out = current
    total_rows = returns.shape[0] * lax.axis_size("scen")
    loss_part, ret_part = loss_terms(weights_out, returns, mean_return)
    loss_cols, unused_sum = summed(loss_part, ret_part)
    hinge_sums = jnp.sum(jnp.maximum(loss_cols - threshold_out[:, None], 0.0), 1)
    hinge_total = lax.psum(hinge_sums, "scen")
    tail_risk = threshold_out + hinge_total / (TAIL * total_rows)
    return (weights_out, threshold_out, duals_out, multiplier_out, tail_risk)


def solution(mesh):
    in_specs = (P("scen", "asset"), P("asset"), P(), P(None, "asset"), P(), P(None, "scen"), P())
    out_specs = (P(None, "asset"), P(), P(None, "scen"), P(), P())
    return jax.shard_map(local, mesh=mesh, in_specs=in_specs, out_specs=out_specs, check_vma=False)
```

profile of v0, /device:TPU:1, one launch (start us, length us, event | category | flops | bytes accessed | tf_op | source)
XLA Modules:
  0.0 1038.7 jit_solution(2643165929812751582)
XLA Ops:
  7.3 11.0 %fusion.3 = f32[64,1536]{1,0:T(8,128)} fusion(bf16[6144,1536]{1,0:T(8,128)(2,1)} %param.15, f32[64,6144]{1,0:T(8,128)} %param.20), kind=kOutput, calls=%fused_computation.29 | convolution fusion | flops 1208352768 | bytes 20840448 | tf_op jit(solution)/shard_map/dot_general | solution.py:99
  19.6 276.9 %all-reduce.12.cloned.1.call-done = f32[64,1536]{1,0:T(8,128)} async-done(((f32[64,1536]{1,0:T(8,128)}), f32[64,1536]{1,0:T(8,128)}) %all-reduce.12.cloned.1.call-update) | async-done | bytes 393232 | tf_op jit(solution)/shard_map/psum | solution.py:101
  298.2 25.3 %all-reduce.5 = (f32[256]{0:T(256)S(1)}, f32[256]{0:T(256)S(1)}) all-reduce(f32[256]{0:T(256)S(1)} %dynamic-update-slice, f32[256]{0:T(256)S(1)} %dynamic-update-slice.1), channel_id=2, replica_groups=mesh['scen'=32,'asset'=4] {'asset'}, use_global_device_ids=true, to_apply=%add | all-reduce | flops 512 | bytes 4096
  331.2 49.5 %while.74 = (s32[]{:T(128)}, f32[64]{0:T(128)S(1)}, f32[64]{0:T(128)S(1)}, f32[64]{0:T(128)S(1)}, f32[64]{0:T(128)S(1)}, /*index=5*/f32[64,1536]{1,0:T(8,128)S(1)}, s32[]{:T(128)}, s32[]{:T(128)}) while((s32[]{:T(128)}, f32[64]{0:T(128)S(1)}, f32[64]{0:T(128)S(1)}, f32[64]{0:T(128)S(1)}, f32[64]{0:T(128)S(1)}, ...), condition=%wide.region_10.0_spmd.clone, body=%wide.region_7.10_spmd.clone.sunk | while | flops 295619 | bytes 397407 | solution.py:67
  331.4 9.6 psum.120
  341.3 7.3 psum.120
  348.9 7.5 psum.120
  364.0 9.1 psum.120
  380.7 13.3 %convolution_negate_fusion.2 = f32[64,6144]{1,0:T(8,128)} fusion(bf16[6144,1536]{1,0:T(8,128)(2,1)} %param.15, f32[64,1536]{1,0:T(8,128)S(1)} %copy-done.2, f32[64,1536]{1,0:T(8,128)S(1)} %get-tuple-element.824, f32[64]{0:T(128)S(1)} %divide_add_fusion.1), kind=kOutput, calls=%fused_computation.22 | convolution fusion | flops 1208844288 | bytes 21233920 | tf_op jit(solution)/shard_map/dot_general | solution.py:79
  395.7 65.7 %psum.107 = f32[64]{0:T(128)S(1)} all-reduce(f32[64]{0:T(128)S(1)} %reduce_sum.107), channel_id=1, replica_groups=mesh['scen'=32,'asset'=4] {'scen'}, use_global_device_ids=true, to_apply=%region_13.14 | all-reduce | flops 64 | bytes 512 | tf_op jit(solution)/shard_map/psum | solution.py:101
  461.4 11.0 %fusion.1 = f32[64,1536]{1,0:T(8,128)} fusion(bf16[6144,1536]{1,0:T(8,128)(2,1)} %param.15, f32[64,6144]{1,0:T(8,128)S(1)} %copy-done, f32[64,6144]{1,0:T(8,128)} %all-reduce.14.cloned.1.call-done, f32[64]{0:T(128)S(1)} %multiply_subtract_fusion.3), kind=kOutput, calls=%fused_computation.27 | convolution fusion | flops 1211498496 | bytes 22413568 | tf_op jit(solution)/shard_map/dot_general | solution.py:99
  472.8 22.1 %psum.109 = f32[64]{0:T(128)S(1)} all-reduce(f32[64]{0:T(128)S(1)} %multiply_reduce_fusion.1), channel_id=1, replica_groups=mesh['scen'=32,'asset'=4] {'asset'}, use_global_device_ids=true, to_apply=%region_16.17 | all-reduce | flops 64 | bytes 512 | tf_op jit(solution)/shard_map/psum | solution.py:75
  494.9 264.3 %all-reduce.16.cloned.1.call-done = f32[64,1536]{1,0:T(8,128)} async-done(((f32[64,1536]{1,0:T(8,128)}), f32[64,1536]{1,0:T(8,128)}) %all-reduce.16.cloned.1.call-update) | async-done | bytes 393232 | tf_op jit(solution)/shard_map/psum | solution.py:101
  760.9 25.3 %all-reduce.4 = (f32[256]{0:T(256)S(1)}, f32[256]{0:T(256)S(1)}) all-reduce(f32[256]{0:T(256)S(1)} %dynamic-update-slice.2, f32[256]{0:T(256)S(1)} %dynamic-update-slice.3), channel_id=4, replica_groups=mesh['scen'=32,'asset'=4] {'asset'}, use_global_device_ids=true, to_apply=%add.2 | all-reduce | flops 512 | bytes 4096
  786.7 7.4 psum.110
  794.2 49.5 %while.75 = (s32[]{:T(128)}, f32[64]{0:T(128)S(1)}, f32[64]{0:T(128)S(1)}, f32[64]{0:T(128)S(1)}, f32[64]{0:T(128)S(1)}, /*index=5*/f32[64,1536]{1,0:T(8,128)S(1)}, s32[]{:T(128)}, s32[]{:T(128)}) while((s32[]{:T(128)}, f32[64]{0:T(128)S(1)}, f32[64]{0:T(128)S(1)}, f32[64]{0:T(128)S(1)}, f32[64]{0:T(128)S(1)}, ...), condition=%wide.region_26.27_spmd.clone, body=%wide.region_23.26_spmd.clone.sunk | while | flops 295619 | bytes 397407 | solution.py:67
  794.4 9.6 psum.121
  811.8 7.5 psum.121
  827.0 9.1 psum.121
  844.6 13.4 %convolution_negate_fusion.1 = f32[64,6144]{1,0:T(8,128)} fusion(bf16[6144,1536]{1,0:T(8,128)(2,1)} %param.15, f32[64,1536]{1,0:T(8,128)S(1)} %get-tuple-element.540), kind=kOutput, calls=%fused_computation.21 | convolution fusion | flops 1208451072 | bytes 20840448 | tf_op jit(solution)/shard_map/dot_general | solution.py:79
  858.0 13.3 %convolution_negate_fusion = f32[64,6144]{1,0:T(8,128)} fusion(bf16[6144,1536]{1,0:T(8,128)(2,1)} %param.15, f32[64,1536]{1,0:T(8,128)S(1)} %multiply_add_fusion.1), kind=kOutput, calls=%fused_computation.20 | convolution fusion | flops 1208451072 | bytes 20840448 | tf_op jit(solution)/shard_map/dot_general | solution.py:79
  873.4 67.5 %psum.111 = f32[64]{0:T(128)S(1)} all-reduce(f32[64]{0:T(128)S(1)} %fusion.9), channel_id=1, replica_groups=mesh['scen'=32,'asset'=4] {'scen'}, use_global_device_ids=true, to_apply=%region_28.29 | all-reduce | flops 64 | bytes 512 | tf_op jit(solution)/shard_map/psum | solution.py:101
  940.9 21.8 %psum.113 = f32[64]{0:T(128)S(1)} all-reduce(f32[64]{0:T(128)S(1)} %copy-done.8), channel_id=1, replica_groups=mesh['scen'=32,'asset'=4] {'asset'}, use_global_device_ids=true, to_apply=%region_31.32 | all-reduce | flops 64 | bytes 512 | tf_op jit(solution)/shard_map/psum | solution.py:75
  964.9 63.3 %psum.115 = f32[64]{0:T(128)S(1)} all-reduce(f32[64]{0:T(128)S(1)} %maximum_reduce_fusion.2), channel_id=1, replica_groups=mesh['scen'=32,'asset'=4] {'scen'}, use_global_device_ids=true, to_apply=%region_34.35 | all-reduce | flops 64 | bytes 512 | tf_op jit(solution)/shard_map/psum | solution.py:133
  (125 shorter events, 62.6 us)
Async XLA Ops:
  7.2 11.2 %copy-start.11 = (u32[128]{0:T(128)S(1)}, u32[128]{0:T(128)}, u32[]{:S(2)}) copy-start(u32[128]{0:T(128)} %constant.205) | copy-start | bytes 1540
  7.2 289.3 %copy-start.4 = (f32[1536]{0:T(1024)S(1)}, f32[1536]{0:T(1024)}, u32[]{:S(2)}) copy-start(f32[1536]{0:T(1024)} %param.16) | copy-start | bytes 18436
  7.2 289.3 %copy-start.2 = (f32[64,1536]{1,0:T(8,128)S(1)}, f32[64,1536]{1,0:T(8,128)}, u32[]{:S(2)}) copy-start(f32[64,1536]{1,0:T(8,128)} %param.18) | copy-start | bytes 1179652
  7.2 289.3 %copy-start.5 = (f32[64]{0:T(128)S(1)}, f32[64]{0:T(128)}, u32[]{:S(2)}) copy-start(f32[64]{0:T(128)} %param.21) | copy-start | bytes 772
  7.2 289.2 %all-reduce.12.cloned.1.call-start = ((), (), s32[]{:S(2)}) async-start(), calls=%async_computation | async-start | bytes 786432 | tf_op jit(solution)/shard_map/psum | solution.py:101
  18.2 443.2 %all-reduce.14.cloned.1.call-start = ((), (), s32[]{:S(2)}) async-start(), calls=%async_computation.1 | async-start | bytes 3145728 | tf_op jit(solution)/shard_map/psum | solution.py:75
  394.1 1.4 copy-start
  394.1 67.3 %copy-start.9 = (f32[64]{0:T(128)S(1)}, f32[64]{0:T(128)}, u32[]{:S(2)}) copy-start(f32[64]{0:T(128)} %param.19) | copy-start | bytes 772
  394.1 365.1 %all-reduce.16.cloned.1.call-start = ((), (), s32[]{:S(2)}) async-start(), calls=%async_computation.2 | async-start | bytes 786432 | tf_op jit(solution)/shard_map/psum | solution.py:101
  461.4 33.5 %copy-start.7 = (f32[64]{0:T(128)S(1)}, f32[64]{0:T(128)}, u32[]{:S(2)}) copy-start(f32[64]{0:T(128)} %param.17) | copy-start | bytes 772
  472.5 490.7 %all-reduce.18.cloned.1.call-start = ((), (), s32[]{:S(2)}) async-start(), calls=%async_computation.3 | async-start | bytes 6291456 | tf_op jit(solution)/shard_map/psum | solution.py:75
  844.6 13.4 %copy-start.3 = (f32[64,1536]{1,0:T(8,128)}, f32[64,1536]{1,0:T(8,128)S(1)}, u32[]{:S(2)}) copy-start(f32[64,1536]{1,0:T(8,128)S(1)} %multiply_add_fusion.1) | copy-start | bytes 1179652
  871.3 1.4 copy-start.1
  872.7 68.2 %copy-start.10 = (f32[64]{0:T(128)S(1)}, f32[64]{0:T(128)}, u32[]{:S(2)}) copy-start(f32[64]{0:T(128)} %param.19) | copy-start | bytes 772
  872.7 68.2 %copy-start.8 = (f32[64]{0:T(128)S(1)}, f32[64]{0:T(128)}, u32[]{:S(2)}) copy-start(f32[64]{0:T(128)} %get-tuple-element.539) | copy-start | bytes 772
  940.9 91.3 %copy-start.6 = (f32[64]{0:T(128)}, f32[64]{0:T(128)S(1)}, u32[]{:S(2)}) copy-start(f32[64]{0:T(128)S(1)} %get-tuple-element.541) | copy-start | bytes 772
Sparse Core Ops, SparseCore 0:
  18.4 278.0 all-reduce.11
  394.2 50.1 all-reduce.13
  472.6 286.5 all-reduce.15
  871.5 76.1 all-reduce.17
where the time goes:
time: 1050 us; the launch traced here: 1040 us
  waiting for transfers between devices  541 us (52%)
  blocking collectives  402 us (38%)
  matrix products  62 us (6%)
  between operations  14.6 us (1%)
  other arithmetic  14.1 us (1%)
    psum x2, waiting for transfers between devices, operate(): gradient, dual_mass = lax.psum((grad_part, mass_part), 'scen')  541 us
    psum x2, blocking collectives, operate(): gradient, dual_mass = lax.psum((grad_part, mass_part), 'scen')  133 us
    psum x14, blocking collectives, shared_sum(): return lax.psum(values, 'asset')  111 us
    psum x1, blocking collectives, local(): hinge_total = lax.psum(hinge_sums, 'scen')  63.3 us
    unnamed x2, blocking collectives  50.6 us
    psum x2, blocking collectives, summed(): return lax.psum((loss_part, ret_part), 'asset')  43.8 us
    dot_general x3, matrix products, loss_terms(): lax.dot_general(alloc.astype(jnp.bfloat16), returns, (((1,), (1,)), ((),...  40 us
    dot_general x2, matrix products, operate(): grad_part = jnp.dot(dual_bf, returns, preferred_element_type=jnp.float32)  22 us
  transfers between devices with their start and end apart: 4, of which 2 were waited for; matrix products, arithmetic and copies ran while one was open for 0% of the time, Pallas kernels for 0%

commit v1 on v0

v1 whole, which is shorter than its diff:
```python
import math

import jax
import jax.numpy as jnp
from jax import lax
from jax.experimental import pallas as pl
from jax.experimental.pallas import tpu as pltpu
from jax.sharding import Mesh
from jax.sharding import PartitionSpec as P

BISECT = 6
TAIL = 0.2
STEP_V = 1.0
STEP_T = 0.5
STEP_U = 0.5
STEP_L = 2.0

SCEN = ("z", "y", "xl")
ASSET = ("xh", "core")
ALL = SCEN + ASSET

K = 64
HALF = 32
LANES = 128
TILE = 768

F32 = jnp.float32
BF16 = jnp.bfloat16

VMEM = pl.BlockSpec(memory_space=pltpu.VMEM)
SMEM = pl.BlockSpec(memory_space=pltpu.SMEM)
ANY = pl.BlockSpec(memory_space=pl.ANY)


def params():
    return pltpu.CompilerParams(vmem_limit_bytes=12 << 20)


def shape(*dims, dtype=F32):
    return jax.ShapeDtypeStruct(dims, dtype)


def cost(macs, nbytes):
    return pl.CostEstimate(flops=2 * macs, bytes_accessed=nbytes, transcendentals=0)


def start_of(offset):
    return pl.multiple_of(offset, LANES)


def lane_folded(values):
    total = values[:, 0:LANES]
    for j in range(1, values.shape[1] // LANES):
        total = total + values[:, j * LANES : (j + 1) * LANES]
    return total


def row_total(folded):
    return jnp.broadcast_to(jnp.sum(folded, 1, keepdims=True), folded.shape)


def diagonal(rows, first=0):
    return lax.broadcasted_iota(jnp.int32, (rows, LANES), 1) == first + lax.broadcasted_iota(
        jnp.int32, (rows, LANES), 0
    )


def in_lanes(column):
    return jnp.sum(jnp.where(diagonal(K), column, 0.0), 0, keepdims=True)[:, 0:K]


def in_rows(line):
    square = diagonal(K)[:, 0:K]
    return jnp.sum(jnp.where(square, jnp.broadcast_to(line, (K, K)), 0.0), 1, keepdims=True)


def picked(line, row):
    at = lax.broadcasted_iota(jnp.int32, line.shape, 1) == row
    return jnp.sum(jnp.where(at, line, 0.0), 1, keepdims=True)


def row_base(core_side, quarter, width):
    core = lax.axis_index("core")
    half = core if core_side else 1 - core
    return start_of((half * 2 + quarter) * width)


def scen_index():
    return (lax.axis_index("z") * 4 + lax.axis_index("y")) * 2 + lax.axis_index("xl")


def call(body, name, operands, outs, macs=0, nbytes=0, scratch=(), in_specs=None):
    single = not isinstance(outs, list)
    return pl.pallas_call(
        body,
        in_specs=in_specs or [VMEM] * len(operands),
        out_specs=VMEM if single else [VMEM] * len(outs),
        out_shape=outs,
        scratch_shapes=list(scratch),
        compiler_params=params(),
        cost_estimate=cost(macs, nbytes),
        name=name,
    )(*operands)


def pack(acc, mass, out):
    blocks = acc.shape[1] // LANES
    for j in range(blocks):
        out[:, j, :] = acc[0:HALF, j * LANES : (j + 1) * LANES]
        out[:, blocks + j, :] = acc[HALF:K, j * LANES : (j + 1) * LANES]
    out[:, 2 * blocks, :] = mass[0:HALF, :]
    out[:, 2 * blocks + 1, :] = mass[HALF:K, :]
    for j in range(2 * blocks + 2, out.shape[1]):
        out[:, j, :] = jnp.zeros((HALF, LANES), F32)


def first_gradient(duals, returns):
    rows, cols = returns.shape
    steps = rows // TILE

    def body(u, r, out, held, kept, acc, sems, dual_sems):
        copies = []
        for i in range(steps):
            at = pl.ds(i * TILE, TILE)
            mine = pltpu.make_async_copy(u.at[:, at], kept.at[:, at], dual_sems.at[i])
            block = pltpu.make_async_copy(r.at[at], held.at[at], sems.at[i])
            mine.start()
            block.start()
            copies.append((mine, block))
        folded = jnp.zeros((K, LANES), F32)
        for i in range(steps):
            copies[i][0].wait()
            part = kept[:, i * TILE : (i + 1) * TILE]
            folded = folded + lane_folded(part)
            copies[i][1].wait()
            term = jnp.dot(
                part.astype(BF16), held[pl.ds(i * TILE, TILE), :], preferred_element_type=F32
            )
            acc[...] = term if i == 0 else acc[...] + term
        pack(acc[...], row_total(folded), out)

    operands = [pltpu.with_memory_space_constraint(a, pltpu.HBM) for a in (duals, returns)]
    outs = [shape(HALF, HALF, LANES), pltpu.VMEM((rows, cols), BF16), pltpu.VMEM((K, rows), F32)]
    scratch = (
        pltpu.VMEM((K, cols), F32),
        pltpu.SemaphoreType.DMA((steps,)),
        pltpu.SemaphoreType.DMA((steps,)),
    )
    return call(
        body, "first_gradient", operands, outs, K * rows * cols, 2 * rows * cols, scratch, [ANY, ANY]
    )


def own_rows(received, state, t_old, extra, first, total_cols, total_rows):
    scale = math.sqrt(total_cols / total_rows)
    cols = state.shape[1]
    blocks = cols // LANES

    def body(got, v, t, more, out):
        s = scen_index()
        grad = jnp.sum(got[...], 0)
        out[2 * blocks : HALF, :] = jnp.zeros((HALF - 2 * blocks, LANES), F32)
        for half in range(2):
            values = v[half * HALF : (half + 1) * HALF, :]
            at = lax.broadcasted_iota(jnp.int32, values.shape, 0) == s
            old = jnp.sum(jnp.where(at, values, 0.0), 0, keepdims=True)
            for j in range(blocks):
                line = half * blocks + j
                out[line : line + 1, :] = (
                    old[:, j * LANES : (j + 1) * LANES] + STEP_V * scale * grad[line : line + 1, :]
                )
                if first:
                    out[HALF + line : HALF + line + 1, :] = more[:, j * LANES : (j + 1) * LANES]
            line = 2 * blocks + half
            out[line : line + 1, :] = picked(t[...], s + half * HALF) - STEP_T * (
                1.0 - grad[line : line + 1, :] / total_rows / TAIL
            )
        if not first:
            out[2 * blocks + 2 : 2 * blocks + 3, 0:K] = more[...]

    return call(
        body,
        "own_rows",
        (received, state, t_old, extra),
        shape(HALF + 2 * blocks if first else HALF, LANES),
        nbytes=4 * HALF * HALF * LANES,
    )


def projected(gathered, own, gathered_first, own_first, lam_old, goal, first, total_cols):
    lines = (gathered_first.shape[1] - HALF) // 2 * 2
    blocks = lines // 2

    def body(rows, mine, means, mean, lam_in, target, out, lam_out):
        s = scen_index()
        first_row = lax.broadcasted_iota(jnp.int32, (lines, LANES), 0) < blocks

        def sums(values):
            a = jnp.sum(jnp.where(first_row, values, 0.0), (0, 1), keepdims=True)
            b = jnp.sum(jnp.where(first_row, 0.0, values), (0, 1), keepdims=True)
            return jnp.concatenate([a, b], 0)

        def spread(pair):
            return jnp.where(first_row, pair[0:1, :], pair[1:2, :])

        lam = lam_in[...]
        if not first:
            ret = rows[0, lines + 2 : lines + 3, 0:K]
            for i in range(1, rows.shape[0]):
                ret = ret + rows[i, lines + 2 : lines + 3, 0:K]
            lam = jnp.maximum(lam + STEP_L * (target[...] - ret / total_cols), 0.0)
        lam_out[...] = lam
        slope = STEP_V * spread(jnp.concatenate([picked(lam, s), picked(lam, s + HALF)], 0))
        parts = [
            rows[i, 0:lines, :] + slope * means[i, HALF : HALF + lines, :]
            for i in range(rows.shape[0])
        ]
        total = parts[0]
        top = parts[0]
        for part in parts[1:]:
            total = total + part
            top = jnp.maximum(top, part)
        low = jnp.min(top, (0, 1), keepdims=True)
        top_a = jnp.max(jnp.where(first_row, top, low), (0, 1), keepdims=True)
        top_b = jnp.max(jnp.where(first_row, low, top), (0, 1), keepdims=True)
        upper = jnp.concatenate([top_a, top_b], 0)
        lower = sums(total) / total_cols - 1.0

        def excess_at(level):
            wide = spread(level)
            over = jnp.maximum(parts[0] - wide, 0.0)
            for part in parts[1:]:
                over = over + jnp.maximum(part - wide, 0.0)
            return sums(over) - total_cols

        f_low = excess_at(lower)
        f_up = jnp.zeros_like(lower) - total_cols
        for _ in range(BISECT):
            middle = (lower + upper) * 0.5
            excess = excess_at(middle)
            raise_low = excess >= 0
            lower = jnp.where(raise_low, middle, lower)
            upper = jnp.where(raise_low, upper, middle)
            f_low = jnp.where(raise_low, excess, f_low)
            f_up = jnp.where(raise_low, f_up, excess)
        theta = lower + f_low * (upper - lower) / (f_low - f_up)
        x = mine[0:lines, :] + slope * mean[HALF : HALF + lines, :]
        fresh = jnp.maximum(x - spread(theta), 0.0)
        rest = mine[lines:HALF, :]
        for i in range(HALF):
            out[i, 0:lines, :] = fresh
            out[i, lines:HALF, :] = rest

    return call(
        body,
        "projected",
        (gathered, own, gathered_first, own_first, lam_old, goal),
        [shape(HALF, HALF, LANES), shape(1, K)],
        nbytes=4 * HALF * HALF * LANES,
    )


def unpacked(received, state, start, mean_row, t_old, last):
    cols = state.shape[1]
    blocks = cols // LANES

    def body(got, v, w, m, t, fresh, bars, t_new, t_bar, ret, *mixed):
        for j in range(blocks):
            at = slice(j * LANES, (j + 1) * LANES)
            fresh[0:HALF, at] = got[:, j, :]
            fresh[HALF:K, at] = got[:, blocks + j, :]
        column = jnp.concatenate([got[:, 2 * blocks, :], got[:, 2 * blocks + 1, :]], 0)
        t_new[...] = in_lanes(column)
        t_bar[...] = 2.0 * column - in_rows(t[...])
        bar = 2.0 * fresh[...] - v[...]
        bars[0:K, :] = (-bar).astype(BF16)
        if not last:
            bars[K : 2 * K, :] = (-w[...]).astype(BF16)
        else:
            mixed[0][...] = (2.0 / 3.0) * bar + w[...] / 3.0
        ret[...] = in_lanes(row_total(lane_folded(bar * m[...])))

    outs = [
        shape(K, cols),
        shape((1 if last else 2) * K, cols, dtype=BF16),
        shape(1, K),
        shape(K, LANES),
        shape(1, K),
    ]
    if last:
        outs.append(shape(K, cols))
    return call(
        body, "unpacked", (received, state, start, mean_row, t_old), outs, nbytes=20 * K * cols
    )


def loss_part(bars, returns, side, quarter, width):
    cols = returns.shape[1]
    count = bars.shape[0] // K

    def body(b, r, *outs):
        base = row_base(side, quarter(), width)
        for i in range(width // TILE):
            at = slice(i * TILE, (i + 1) * TILE)
            block = r[pl.ds(start_of(base + i * TILE), TILE), :]
            term = lax.dot_general(
                block, b[...], (((1,), (1,)), ((), ())), preferred_element_type=F32
            ).T
            for part in range(count):
                outs[part][:, at] = term[part * K : (part + 1) * K, :]

    return call(
        body,
        "loss_part",
        (bars, returns),
        [shape(K, width)] * count,
        count * K * width * cols,
        2 * width * cols,
    )


def plus(a, b):
    def body(x, y, out):
        out[...] = x[...] + y[...]

    return call(body, "plus", (a, b), shape(*a.shape), nbytes=12 * a.size)


def own_and_other(keeps, takes):
    def body(k0, t0, k1, t1, send, keep):
        near = k0[...] + t0[...]
        far = k1[...] + t1[...]
        swap = lax.axis_index("xh") == 0
        send[...] = jnp.where(swap, far, near)
        keep[...] = jnp.where(swap, near, far)

    return call(
        body,
        "own_and_other",
        (keeps[0], takes[0], keeps[1], takes[1]),
        [shape(*keeps[0].shape)] * 2,
        nbytes=24 * keeps[0].size,
    )


def dual_step(loss, duals, t_bar):
    return jnp.clip(duals + STEP_U * (loss - t_bar[:, 0:1]), 0.0, 1.0)


def dual_rows(part, other, duals, t_bar, quarter, width):
    def body(p, o, u, t, fresh):
        base = row_base(1, quarter, width)
        fresh[...] = dual_step(p[...] + o[...], u[:, pl.ds(base, width)], t[...])

    return call(
        body, "dual_rows", (part, other, duals, t_bar), shape(K, width), nbytes=16 * K * width
    )


def gradient_part(terms, returns, before, width):
    cols = returns.shape[1]
    count = len(terms)

    def body(r, *refs):
        fed, rest = refs[:count], refs[count:]
        acc_out, folded_out = rest[-2:]
        total = rest[0][...] if before else None
        folds = rest[1][...] if before else None
        for (_, side, quarter), ref in zip(terms, fed):
            base = row_base(side, quarter, width)
            value = ref[...]
            term = jnp.dot(
                value.astype(BF16), r[pl.ds(base, width), :], preferred_element_type=F32
            )
            total = term if total is None else total + term
            fold = lane_folded(value)
            folds = fold if folds is None else folds + fold
        acc_out[...] = total
        folded_out[...] = folds

    operands = [returns] + [values for values, _, _ in terms] + list(before)
    return call(
        body,
        "gradient_part",
        operands,
        [shape(K, cols), shape(K, LANES)],
        count * K * width * cols,
        2 * count * width * cols,
    )


def gradient_end(taken, side, quarter, returns, before, width):
    cols = returns.shape[1]

    def body(r, got, acc_in, folded_in, out):
        base = row_base(side, quarter, width)
        term = acc_in[...] + jnp.dot(
            got[...].astype(BF16), r[pl.ds(base, width), :], preferred_element_type=F32
        )
        pack(term, row_total(folded_in[...] + lane_folded(got[...])), out)

    return call(
        body,
        "gradient_end",
        (returns, taken, *before),
        shape(HALF, HALF, LANES),
        K * width * cols,
        2 * width * cols,
    )


def final_duals(part, other, tails, held, start, t_new, t_old, t_start, t_bar, ret, width):
    devices = 128

    def body(p, o, la, lb, ua, ub, u0, tn, t, ts, tb, er, duals_out, t_out, sums):
        mine = lax.axis_index("xh")
        base = row_base(1, mine, width)
        loss = p[...] + o[...]
        old = jnp.where(mine == 0, ua[...], ub[...])
        fresh = dual_step(loss, old, tb[...])
        duals_out[...] = (2.0 / 3.0) * (2.0 * fresh - old) + u0[:, pl.ds(base, width)] / 3.0
        end = (2.0 / 3.0) * (2.0 * tn[...] - t[...]) + ts[...] / 3.0
        t_out[...] = end
        tail = (2.0 / 3.0) * loss + (la[...] + lb[...]) / 3.0
        over = jnp.maximum(tail - in_rows(end), 0.0)
        line = jnp.concatenate([in_lanes(row_total(lane_folded(over))), er[...]], 1)
        sums[...] = jnp.broadcast_to(line[None], (devices, 1, LANES))

    operands = (part, other, *tails, *held, start, t_new, t_old, t_start, t_bar, ret)
    return call(
        body,
        "final_duals",
        operands,
        [shape(K, width), shape(1, K), shape(devices, 1, LANES)],
        nbytes=24 * K * width,
    )


def joined(pieces, width):
    def body(far_near, near, far, own, out):
        mine = lax.axis_index("xh")
        out[:, pl.ds(row_base(0, 1 - mine, width), width)] = far_near[...]
        out[:, pl.ds(row_base(1, 1 - mine, width), width)] = near[...]
        out[:, pl.ds(row_base(0, mine, width), width)] = far[...]
        out[:, pl.ds(row_base(1, mine, width), width)] = own[...]

    return call(body, "joined", pieces, shape(K, 4 * width), nbytes=32 * K * width)


def finished(sums, t_out, lam, lam_start, goal, total_cols, total_rows):
    devices = sums.shape[0]
    copies = devices // 4

    def body(got, end, lam_old, lam_0, target, tail, lam_out):
        total = jnp.sum(got[...], 0)
        tail[...] = end[...] + total[:, 0:K] / (TAIL * total_rows)
        ret = total[:, K : 2 * K] / copies
        fresh = jnp.maximum(lam_old[...] + STEP_L * (target[...] - ret / total_cols), 0.0)
        lam_out[...] = (2.0 / 3.0) * (2.0 * fresh - lam_old[...]) + lam_0[...] / 3.0

    return call(
        body, "finished", (sums, t_out, lam, lam_start, goal), [shape(1, K)] * 2, nbytes=devices * 512
    )


def pinned(a):
    return pltpu.with_memory_space_constraint(a, pltpu.VMEM)


def across(values, axis):
    return lax.ppermute(values, axis, [(0, 1), (1, 0)])


def exchanged(payload, others):
    payload, others = lax.optimization_barrier((payload, others))
    received = lax.all_to_all(payload, SCEN, 0, 0)
    return lax.optimization_barrier((received, others))


def local(returns, mean_return, targets, weights, threshold, duals, multiplier):
    scen_rows, cols = returns.shape
    total_cols = cols * 4
    total_rows = scen_rows * 32
    width = scen_rows // 4
    mean_row = mean_return.reshape(1, cols)
    t0 = threshold.reshape(1, K)
    lam0 = multiplier.reshape(1, K)
    goal = targets.reshape(1, K)

    payload, returns, duals = first_gradient(duals, returns)
    returns = pinned(returns)
    held = (returns, duals, weights, mean_row, t0, lam0, goal)
    received, held = exchanged(payload, held)
    returns, duals, weights, mean_row, t0, lam0, goal = held
    own_first = own_rows(received, weights, t0, mean_row, True, total_cols, total_rows)
    gathered_first = lax.all_gather(own_first, ASSET)
    payload, lam0 = projected(
        gathered_first, own_first, gathered_first, own_first, lam0, goal, True, total_cols
    )
    held = (returns, duals, weights, mean_row, t0, lam0, goal, gathered_first, own_first)
    received, held = exchanged(payload, held)
    returns, duals, weights, mean_row, t0, lam0, goal, gathered_first, own_first = held
    returns = pinned(returns)
    v1, bars, t1, bar1, ret1 = unpacked(received, weights, weights, mean_row, t0, False)

    parts = []
    keep_tails = []
    take_tails = []
    for quarter in range(2):
        send, send_tail = loss_part(bars, returns, 0, lambda: quarter, width)
        take = across(send, "core")
        take_tails.append(across(send_tail, "core"))
        keep, keep_tail = loss_part(bars, returns, 1, lambda: quarter, width)
        keep_tails.append(keep_tail)
        parts.append(plus(keep, take))
    others = [across(part, "xh") for part in parts]
    send_tail, tail_a = own_and_other(keep_tails, take_tails)

    ua = dual_rows(parts[0], others[0], duals, bar1, 0, width)
    taken_a = across(ua, "core")
    sums = gradient_part([(ua, 1, 0)], returns, (), width)
    ub = dual_rows(parts[1], others[1], duals, bar1, 1, width)
    taken_b = across(ub, "core")
    sums = gradient_part([(taken_a, 0, 0), (ub, 1, 1)], returns, sums, width)
    payload = gradient_end(taken_b, 0, 1, returns, sums, width)
    tail_b = across(send_tail, "xh")

    held = (returns, duals, weights, mean_row, v1, t0, t1, lam0, goal, gathered_first, own_first)
    held = held + (ret1, ua, ub, tail_a, tail_b)
    received, held = exchanged(payload, held)
    returns, duals, weights, mean_row, v1, t0, t1, lam0, goal, gathered_first, own_first = held[:11]
    ret1, ua, ub, tail_a, tail_b = held[11:]
    own = own_rows(received, v1, t1, ret1, False, total_cols, total_rows)
    gathered = lax.all_gather(own, ASSET)
    payload, lam1 = projected(
        gathered, own, gathered_first, own_first, lam0, goal, False, total_cols
    )
    held = (returns, duals, weights, mean_row, v1, t0, t1, lam0, lam1, goal, ua, ub, tail_a, tail_b)
    received, held = exchanged(payload, held)
    returns, duals, weights, mean_row, v1, t0, t1, lam0, lam1, goal, ua, ub, tail_a, tail_b = held
    returns = pinned(returns)
    v2, bars, t2, bar2, ret2, weights_out = unpacked(received, v1, weights, mean_row, t1, True)

    def far_quarter():
        return 1 - lax.axis_index("xh")

    def own_quarter():
        return lax.axis_index("xh")

    parts = []
    for quarter in (far_quarter, own_quarter):
        (send,) = loss_part(bars, returns, 0, quarter, width)
        take = across(send, "core")
        (keep,) = loss_part(bars, returns, 1, quarter, width)
        parts.append(plus(keep, take))
    other = across(parts[0], "xh")

    quarter, t_out, sums = final_duals(
        parts[1], other, (tail_a, tail_b), (ua, ub), duals, t2, t1, t0, bar2, ret2, width
    )
    near = across(quarter, "xh")
    far = across(quarter, "core")
    far_near = across(near, "core")
    sums = lax.all_to_all(sums, ALL, 0, 0)
    duals_out = joined((far_near, near, far, quarter), width)
    tail_risk, lam_out = finished(sums, t_out, lam1, lam0, goal, total_cols, total_rows)
    return (weights_out, t_out.reshape(K), duals_out, lam_out.reshape(K), tail_risk.reshape(K))


def solution(mesh):
    split = Mesh(mesh.devices.reshape(4, 4, 2, 2, 2), ALL)
    in_specs = (P(SCEN, ASSET), P(ASSET), P(), P(None, ASSET), P(), P(None, SCEN), P())
    out_specs = (P(None, ASSET), P(), P(None, SCEN), P(), P())
    return jax.shard_map(local, mesh=split, in_specs=in_specs, out_specs=out_specs, check_vma=False)
```

time: 1050 us -> 186 us (0.18); the launches traced: 1040 us -> 186 us
  waiting for transfers between devices: 541 us -> 32.4 us
  blocking collectives: 402 us -> 96.7 us
  matrix products: 62 us -> 0 us
  Pallas kernels: 0 us -> 31.5 us
  starting transfers between devices: 0.16 us -> 23.1 us
  other arithmetic: 14.1 us -> 0 us
  between operations: 14.6 us -> 0.81 us
    psum x4 -> x0, waiting for transfers between devices: 541 us -> none  [the longest x2 541 us: operate(): gradient, dual_mass = lax.psum((grad_part, mass_part), 'scen')]
    psum x19 -> x0, blocking collectives: 351 us -> none  [the longest x2 133 us: operate(): gradient, dual_mass = lax.psum((grad_part, mass_part), 'scen')]
    all_to_all x0 -> x5, blocking collectives: none -> 79.1 us  [the longest x4 64.5 us: exchanged(): received = lax.all_to_all(payload, SCEN, 0, 0)]
    dot_general x5 -> x0, matrix products: 62 us -> none  [the longest x3 40 us: loss_terms(): lax.dot_general(alloc.astype(jnp.bfloat16), returns, (((1,), (1,)), ((),...]
    unnamed x2 -> x0, blocking collectives: 50.6 us -> none
    ppermute x0 -> x15, waiting for transfers between devices: none -> 32.4 us  [across(): return lax.ppermute(values, axis, [(0, 1), (1, 0)])]
    pallas_call x0 -> x28, Pallas kernels: none -> 31.5 us  [call(): pl.pallas_call(body, in_specs=in_specs or [VMEM] * len(operands), out_spe...]
    ppermute x0 -> x15, starting transfers between devices: none -> 23.1 us  [across(): return lax.ppermute(values, axis, [(0, 1), (1, 0)])]
  transfers between devices with their start and end apart: 4 -> 15, of which waited for: 2 -> 5; matrix products, arithmetic and copies ran while one was open for 0% -> 0% of each run, Pallas kernels for 0% -> 7%
where the time goes in v1:
time: 186 us
  blocking collectives  96.7 us (52%)
  waiting for transfers between devices  32.4 us (17%)
  Pallas kernels  31.5 us (17%)
  starting transfers between devices  23.1 us (12%)
    all_to_all x4, blocking collectives, exchanged(): received = lax.all_to_all(payload, SCEN, 0, 0)  64.5 us
    ppermute x15, waiting for transfers between devices, across(): return lax.ppermute(values, axis, [(0, 1), (1, 0)])  32.4 us
    pallas_call x28, Pallas kernels, call(): pl.pallas_call(body, in_specs=in_specs or [VMEM] * len(operands), out_spe...  31.5 us
    ppermute x15, starting transfers between devices, across(): return lax.ppermute(values, axis, [(0, 1), (1, 0)])  23.1 us
    all_to_all x1, blocking collectives, local(): sums = lax.all_to_all(sums, ALL, 0, 0)  14.6 us
    all_gather x1, blocking collectives, local(): gathered_first = lax.all_gather(own_first, ASSET)  8.83 us
    all_gather x1, blocking collectives, local(): gathered = lax.all_gather(own, ASSET)  8.75 us
  transfers between devices with their start and end apart: 15, of which 5 were waited for; matrix products, arithmetic and copies ran while one was open for 0% of the time, Pallas kernels for 7%

profile of v1, /device:TPU:1, one launch (start us, length us, event | category | flops | bytes accessed | tf_op | source)
XLA Modules:
  0.0 185.8 jit_solution(10274410679286546363)
XLA Ops:
  1.3 7.8 %first_gradient.1 = (f32[32,32,128]{2,1,0:T(8,128)S(1)}, bf16[6144,1536]{1,0:T(8,128)(2,1)S(1)}, f32[64,6144]{1,0:T(8,128)S(1)}) custom-call(f32[64,6144]{1,0:T(8,128)} %u.1, bf16[6144,1536]{1,0:T(8,128)(2,1)} %r.1), custom_call_target="tpu_custom_call" | custom-call | flops 1207959552 | bytes 18874368 | tf_op jit(solution)/shard_map/first_gradient/pallas_call | solution.py:94
  9.2 20.7 %all_to_all.25.got = f32[32,32,128]{2,1,0:T(8,128)S(1)} all-to-all(f32[32,32,128]{2,1,0:T(8,128)S(1)} %get-tuple-element.144), channel_id=1, replica_groups=mesh['z'=4,'y'=4,'xl'=2,'xh'=2,'core'=2] {'z','y','xl'}, dimensions={0} | all-to-all | bytes 1048576 | tf_op jit(solution)/shard_map/all_to_all | solution.py:476
  30.0 8.8 %all-gather = f32[224,128]{1,0:T(8,128)S(1)} all-gather(f32[56,128]{1,0:T(8,128)S(1)} %own_rows.2.mine.mean), channel_id=2, replica_groups=mesh['z'=4,'y'=4,'xl'=2,'xh'=2,'core'=2] {'xh','core'}, dimensions={0}, use_global_device_ids=true | all-gather | bytes 143360 | tf_op jit(solution)/shard_map/all_gather | solution.py:496
  40.4 14.8 %all_to_all.26.got = f32[32,32,128]{2,1,0:T(8,128)S(1)} all-to-all(f32[32,32,128]{2,1,0:T(8,128)S(1)} %get-tuple-element.162), channel_id=1, replica_groups=mesh['z'=4,'y'=4,'xl'=2,'xh'=2,'core'=2] {'z','y','xl'}, dimensions={0} | all-to-all | bytes 1048576 | tf_op jit(solution)/shard_map/all_to_all | solution.py:476
  57.0 1.7 collective-permute-start.3
  61.8 2.5 %collective-permute-start.4 = (f32[64,1536]{1,0:T(8,128)S(1)}, f32[64,1536]{1,0:T(8,128)S(1)}, u32[]{:S(2)}, u32[]{:S(2)}) collective-permute-start(f32[64,1536]{1,0:T(8,128)S(1)} %plus.5.p), channel_id=1, source_target_pairs={{0,2},{2,0},{1,3},{3,1},{4,6},{6,4},{5,7},{7,5},{8,10},{10,8},{9,1... | collective-permute-start | bytes 1179656 | tf_op jit(solution)/shard_map/ppermute | solution.py:471
  67.5 6.0 %collective-permute-done.4.o = f32[64,1536]{1,0:T(8,128)S(1)} collective-permute-done((f32[64,1536]{1,0:T(8,128)S(1)}, f32[64,1536]{1,0:T(8,128)S(1)}, u32[]{:S(2)}, u32[]{:S(2)}) %collective-permute-start.4) | collective-permute-done | bytes 393248 | tf_op jit(solution)/shard_map/ppermute | solution.py:471
  73.7 2.4 %collective-permute-start.5 = (f32[64,1536]{1,0:T(8,128)S(1)}, f32[64,1536]{1,0:T(8,128)S(1)}, u32[]{:S(2)}, u32[]{:S(2)}) collective-permute-start(f32[64,1536]{1,0:T(8,128)S(1)} %dual_rows.3.refs_0_.ua), channel_id=1, source_target_pairs={{0,1},{1,0},{2,3},{3,2},{4,5},{5,4},{6,7},{7,6},{8,9},{9,8},{10,11... | collective-permute-start | bytes 1179656 | tf_op jit(solution)/shard_map/ppermute | solution.py:471
  76.1 5.9 %collective-permute-done.1.o = f32[64,1536]{1,0:T(8,128)S(1)} collective-permute-done((f32[64,1536]{1,0:T(8,128)S(1)}, f32[64,1536]{1,0:T(8,128)S(1)}, u32[]{:S(2)}, u32[]{:S(2)}) %collective-permute-start.1) | collective-permute-done | bytes 393248 | tf_op jit(solution)/shard_map/ppermute | solution.py:471
  83.6 2.7 %collective-permute-start.8 = (f32[64,1536]{1,0:T(8,128)S(1)}, f32[64,1536]{1,0:T(8,128)S(1)}, u32[]{:S(2)}, u32[]{:S(2)}) collective-permute-start(f32[64,1536]{1,0:T(8,128)S(1)} %get-tuple-element.200), channel_id=1, source_target_pairs={{0,2},{2,0},{1,3},{3,1},{4,6},{6,4},{5,7},{7,5},{8,10},{10,8},{9,1... | collective-permute-start | bytes 1179656 | tf_op jit(solution)/shard_map/ppermute | solution.py:471
  87.3 1.7 gradient_part.3
  90.2 5.9 %collective-permute-done.8.lb = f32[64,1536]{1,0:T(8,128)S(1)} collective-permute-done((f32[64,1536]{1,0:T(8,128)S(1)}, f32[64,1536]{1,0:T(8,128)S(1)}, u32[]{:S(2)}, u32[]{:S(2)}) %collective-permute-start.8) | collective-permute-done | bytes 393248 | tf_op jit(solution)/shard_map/ppermute | solution.py:471
  96.1 14.3 %all_to_all.27.got = f32[32,32,128]{2,1,0:T(8,128)S(1)} all-to-all(f32[32,32,128]{2,1,0:T(8,128)S(1)} %gradient_end.1), channel_id=1, replica_groups=mesh['z'=4,'y'=4,'xl'=2,'xh'=2,'core'=2] {'z','y','xl'}, dimensions={0} | all-to-all | bytes 1048576 | tf_op jit(solution)/shard_map/all_to_all | solution.py:476
  110.5 8.7 %all-gather.1 = f32[128,128]{1,0:T(8,128)S(1)} all-gather(f32[32,128]{1,0:T(8,128)S(1)} %own_rows.3.mine), channel_id=3, replica_groups=mesh['z'=4,'y'=4,'xl'=2,'xh'=2,'core'=2] {'xh','core'}, dimensions={0}, use_global_device_ids=true | all-gather | bytes 81920 | tf_op jit(solution)/shard_map/all_gather | solution.py:534
  119.2 1.5 projected.3
  120.8 14.8 %all_to_all.28.got = f32[32,32,128]{2,1,0:T(8,128)S(1)} all-to-all(f32[32,32,128]{2,1,0:T(8,128)S(1)} %get-tuple-element.237), channel_id=1, replica_groups=mesh['z'=4,'y'=4,'xl'=2,'xh'=2,'core'=2] {'z','y','xl'}, dimensions={0} | all-to-all | bytes 1048576 | tf_op jit(solution)/shard_map/all_to_all | solution.py:476
  138.2 1.7 collective-permute-start.10
  142.8 2.5 %collective-permute-start.11 = (f32[64,1536]{1,0:T(8,128)S(1)}, f32[64,1536]{1,0:T(8,128)S(1)}, u32[]{:S(2)}, u32[]{:S(2)}) collective-permute-start(f32[64,1536]{1,0:T(8,128)S(1)} %plus.7), channel_id=1, source_target_pairs={{0,2},{2,0},{1,3},{3,1},{4,6},{6,4},{5,7},{7,5},{8,10},{10,8},{9,1... | collective-permute-start | bytes 1179656 | tf_op jit(solution)/shard_map/ppermute | solution.py:471
  146.9 7.8 %collective-permute-done.11.o = f32[64,1536]{1,0:T(8,128)S(1)} collective-permute-done((f32[64,1536]{1,0:T(8,128)S(1)}, f32[64,1536]{1,0:T(8,128)S(1)}, u32[]{:S(2)}, u32[]{:S(2)}) %collective-permute-start.11) | collective-permute-done | bytes 393248 | tf_op jit(solution)/shard_map/ppermute | solution.py:471
  155.5 2.4 %collective-permute-start.12 = (f32[64,1536]{1,0:T(8,128)S(1)}, f32[64,1536]{1,0:T(8,128)S(1)}, u32[]{:S(2)}, u32[]{:S(2)}) collective-permute-start(f32[64,1536]{1,0:T(8,128)S(1)} %get-tuple-element.270.own), channel_id=1, source_target_pairs={{0,2},{2,0},{1,3},{3,1},{4,6},{6,4},{5,7},{7,5},{8,10},{10,8},{9,1... | collective-permute-start | bytes 1179656 | tf_op jit(solution)/shard_map/ppermute | solution.py:471
  157.9 1.6 collective-permute-start.14
  159.5 6.7 %collective-permute-done.12.near = f32[64,1536]{1,0:T(8,128)S(1)} collective-permute-done((f32[64,1536]{1,0:T(8,128)S(1)}, f32[64,1536]{1,0:T(8,128)S(1)}, u32[]{:S(2)}, u32[]{:S(2)}) %collective-permute-start.12) | collective-permute-done | bytes 393248 | tf_op jit(solution)/shard_map/ppermute | solution.py:471
  166.2 2.3 %collective-permute-start.13 = (f32[64,1536]{1,0:T(8,128)S(1)}, f32[64,1536]{1,0:T(8,128)S(1)}, u32[]{:S(2)}, u32[]{:S(2)}) collective-permute-start(f32[64,1536]{1,0:T(8,128)S(1)} %collective-permute-done.12.near), channel_id=1, source_target_pairs={{0,1},{1,0},{2,3},{3,2},{4,5},{5,4},{6,7},{7,6},{8,9},{9,8},{10,11... | collective-permute-start | bytes 1179656 | tf_op jit(solution)/shard_map/ppermute | solution.py:471
  168.5 14.6 %all_to_all.29.got = f32[128,1,128]{2,1,0:T(1,128)S(1)} all-to-all(f32[128,1,128]{2,1,0:T(1,128)S(1)} %get-tuple-element.271), channel_id=1, replica_groups=mesh['z'=4,'y'=4,'xl'=2,'xh'=2,'core'=2] {'z','y','xl','xh','core'}, dimensions={0} | all-to-all | bytes 131072 | tf_op jit(solution)/shard_map/all_to_all | solution.py:564
  (52 shorter events, 25.0 us)
Async XLA Ops:
  1.3 28.6 %copy-start = (f32[64,1536]{1,0:T(8,128)S(1)}, f32[64,1536]{1,0:T(8,128)}, u32[]{:S(2)}) copy-start(f32[64,1536]{1,0:T(8,128)} %w.1) | copy-start | bytes 1179652
  1.3 28.6 %copy-start.1 = (f32[64]{0:T(128)S(1)}, f32[64]{0:T(128)}, u32[]{:S(2)}) copy-start(f32[64]{0:T(128)} %param.11) | copy-start | bytes 772
  9.2 29.7 %copy-start.2 = (f32[64]{0:T(128)S(1)}, f32[64]{0:T(128)}, u32[]{:S(2)}) copy-start(f32[64]{0:T(128)} %param.9) | copy-start | bytes 772
  9.2 29.7 %copy-start.3 = (f32[64]{0:T(128)S(1)}, f32[64]{0:T(128)}, u32[]{:S(2)}) copy-start(f32[64]{0:T(128)} %param.13) | copy-start | bytes 772
  57.0 4.7 %collective-permute-start.3 = (f32[64,1536]{1,0:T(8,128)S(1)}, f32[64,1536]{1,0:T(8,128)S(1)}, u32[]{:S(2)}, u32[]{:S(2)}) collective-permute-start(f32[64,1536]{1,0:T(8,128)S(1)} %get-tuple-element.183), channel_id=1, source_target_pairs={{0,1},{1,0},{2,3},{3,2},{4,5},{5,4},{6,7},{7,6},{8,9},{9,8},{10,11... | collective-permute-start | bytes 1179656 | tf_op jit(solution)/shard_map/ppermute | solution.py:471
  60.2 5.6 %collective-permute-start = (f32[64,1536]{1,0:T(8,128)S(1)}, f32[64,1536]{1,0:T(8,128)S(1)}, u32[]{:S(2)}, u32[]{:S(2)}) collective-permute-start(f32[64,1536]{1,0:T(8,128)S(1)} %get-tuple-element.179), channel_id=1, source_target_pairs={{0,1},{1,0},{2,3},{3,2},{4,5},{5,4},{6,7},{7,6},{8,9},{9,8},{10,11... | collective-permute-start | bytes 1179656 | tf_op jit(solution)/shard_map/ppermute | solution.py:471
  61.8 11.8 %collective-permute-start.4 = (f32[64,1536]{1,0:T(8,128)S(1)}, f32[64,1536]{1,0:T(8,128)S(1)}, u32[]{:S(2)}, u32[]{:S(2)}) collective-permute-start(f32[64,1536]{1,0:T(8,128)S(1)} %plus.5.p), channel_id=1, source_target_pairs={{0,2},{2,0},{1,3},{3,1},{4,6},{6,4},{5,7},{7,5},{8,10},{10,8},{9,1... | collective-permute-start | bytes 1179656 | tf_op jit(solution)/shard_map/ppermute | solution.py:471
  65.9 16.1 %collective-permute-start.1 = (f32[64,1536]{1,0:T(8,128)S(1)}, f32[64,1536]{1,0:T(8,128)S(1)}, u32[]{:S(2)}, u32[]{:S(2)}) collective-permute-start(f32[64,1536]{1,0:T(8,128)S(1)} %plus.4.p), channel_id=1, source_target_pairs={{0,2},{2,0},{1,3},{3,1},{4,6},{6,4},{5,7},{7,5},{8,10},{10,8},{9,1... | collective-permute-start | bytes 1179656 | tf_op jit(solution)/shard_map/ppermute | solution.py:471
  66.5 17.1 %collective-permute-start.6 = (f32[64,1536]{1,0:T(8,128)S(1)}, f32[64,1536]{1,0:T(8,128)S(1)}, u32[]{:S(2)}, u32[]{:S(2)}) collective-permute-start(f32[64,1536]{1,0:T(8,128)S(1)} %get-tuple-element.196), channel_id=1, source_target_pairs={{0,1},{1,0},{2,3},{3,2},{4,5},{5,4},{6,7},{7,6},{8,9},{9,8},{10,11... | collective-permute-start | bytes 1179656 | tf_op jit(solution)/shard_map/ppermute | solution.py:471
  67.5 16.0 %collective-permute-start.7 = (f32[64,1536]{1,0:T(8,128)S(1)}, f32[64,1536]{1,0:T(8,128)S(1)}, u32[]{:S(2)}, u32[]{:S(2)}) collective-permute-start(f32[64,1536]{1,0:T(8,128)S(1)} %get-tuple-element.198), channel_id=1, source_target_pairs={{0,1},{1,0},{2,3},{3,2},{4,5},{5,4},{6,7},{7,6},{8,9},{9,8},{10,11... | collective-permute-start | bytes 1179656 | tf_op jit(solution)/shard_map/ppermute | solution.py:471
  73.7 13.6 %collective-permute-start.5 = (f32[64,1536]{1,0:T(8,128)S(1)}, f32[64,1536]{1,0:T(8,128)S(1)}, u32[]{:S(2)}, u32[]{:S(2)}) collective-permute-start(f32[64,1536]{1,0:T(8,128)S(1)} %dual_rows.3.refs_0_.ua), channel_id=1, source_target_pairs={{0,1},{1,0},{2,3},{3,2},{4,5},{5,4},{6,7},{7,6},{8,9},{9,8},{10,11... | collective-permute-start | bytes 1179656 | tf_op jit(solution)/shard_map/ppermute | solution.py:471
  82.1 6.9 %collective-permute-start.2 = (f32[64,1536]{1,0:T(8,128)S(1)}, f32[64,1536]{1,0:T(8,128)S(1)}, u32[]{:S(2)}, u32[]{:S(2)}) collective-permute-start(f32[64,1536]{1,0:T(8,128)S(1)} %dual_rows.2.refs_1_.ub), channel_id=1, source_target_pairs={{0,1},{1,0},{2,3},{3,2},{4,5},{5,4},{6,7},{7,6},{8,9},{9,8},{10,11... | collective-permute-start | bytes 1179656 | tf_op jit(solution)/shard_map/ppermute | solution.py:471
  83.6 12.5 %collective-permute-start.8 = (f32[64,1536]{1,0:T(8,128)S(1)}, f32[64,1536]{1,0:T(8,128)S(1)}, u32[]{:S(2)}, u32[]{:S(2)}) collective-permute-start(f32[64,1536]{1,0:T(8,128)S(1)} %get-tuple-element.200), channel_id=1, source_target_pairs={{0,2},{2,0},{1,3},{3,1},{4,6},{6,4},{5,7},{7,5},{8,10},{10,8},{9,1... | collective-permute-start | bytes 1179656 | tf_op jit(solution)/shard_map/ppermute | solution.py:471
  138.2 4.6 %collective-permute-start.10 = (f32[64,1536]{1,0:T(8,128)S(1)}, f32[64,1536]{1,0:T(8,128)S(1)}, u32[]{:S(2)}, u32[]{:S(2)}) collective-permute-start(f32[64,1536]{1,0:T(8,128)S(1)} %loss_part.15), channel_id=1, source_target_pairs={{0,1},{1,0},{2,3},{3,2},{4,5},{5,4},{6,7},{7,6},{8,9},{9,8},{10,11... | collective-permute-start | bytes 1179656 | tf_op jit(solution)/shard_map/ppermute | solution.py:471
  141.3 5.5 %collective-permute-start.9 = (f32[64,1536]{1,0:T(8,128)S(1)}, f32[64,1536]{1,0:T(8,128)S(1)}, u32[]{:S(2)}, u32[]{:S(2)}) collective-permute-start(f32[64,1536]{1,0:T(8,128)S(1)} %loss_part.13), channel_id=1, source_target_pairs={{0,1},{1,0},{2,3},{3,2},{4,5},{5,4},{6,7},{7,6},{8,9},{9,8},{10,11... | collective-permute-start | bytes 1179656 | tf_op jit(solution)/shard_map/ppermute | solution.py:471
  142.8 11.8 %collective-permute-start.11 = (f32[64,1536]{1,0:T(8,128)S(1)}, f32[64,1536]{1,0:T(8,128)S(1)}, u32[]{:S(2)}, u32[]{:S(2)}) collective-permute-start(f32[64,1536]{1,0:T(8,128)S(1)} %plus.7), channel_id=1, source_target_pairs={{0,2},{2,0},{1,3},{3,1},{4,6},{6,4},{5,7},{7,5},{8,10},{10,8},{9,1... | collective-permute-start | bytes 1179656 | tf_op jit(solution)/shard_map/ppermute | solution.py:471
  155.5 10.8 %collective-permute-start.12 = (f32[64,1536]{1,0:T(8,128)S(1)}, f32[64,1536]{1,0:T(8,128)S(1)}, u32[]{:S(2)}, u32[]{:S(2)}) collective-permute-start(f32[64,1536]{1,0:T(8,128)S(1)} %get-tuple-element.270.own), channel_id=1, source_target_pairs={{0,2},{2,0},{1,3},{3,1},{4,6},{6,4},{5,7},{7,5},{8,10},{10,8},{9,1... | collective-permute-start | bytes 1179656 | tf_op jit(solution)/shard_map/ppermute | solution.py:471
  157.9 26.6 %collective-permute-start.14 = (f32[64,1536]{1,0:T(8,128)S(1)}, f32[64,1536]{1,0:T(8,128)S(1)}, u32[]{:S(2)}, u32[]{:S(2)}) collective-permute-start(f32[64,1536]{1,0:T(8,128)S(1)} %get-tuple-element.270.own), channel_id=1, source_target_pairs={{0,1},{1,0},{2,3},{3,2},{4,5},{5,4},{6,7},{7,6},{8,9},{9,8},{10,11... | collective-permute-start | bytes 1179656 | tf_op jit(solution)/shard_map/ppermute | solution.py:471
  166.2 18.3 %collective-permute-start.13 = (f32[64,1536]{1,0:T(8,128)S(1)}, f32[64,1536]{1,0:T(8,128)S(1)}, u32[]{:S(2)}, u32[]{:S(2)}) collective-permute-start(f32[64,1536]{1,0:T(8,128)S(1)} %collective-permute-done.12.near), channel_id=1, source_target_pairs={{0,1},{1,0},{2,3},{3,2},{4,5},{5,4},{6,7},{7,6},{8,9},{9,8},{10,11... | collective-permute-start | bytes 1179656 | tf_op jit(solution)/shard_map/ppermute | solution.py:471
  183.1 0.7 copy-start.4

commit v2 on v1

--- a/solution.py
+++ b/solution.py
@@ -41,7 +41,7 @@
 
 
 def cost(macs, nbytes):
-    return pl.CostEstimate(flops=2 * macs, bytes_accessed=nbytes, transcendentals=0)
+    return pl.CostEstimate(flops=2 * macs // 100, bytes_accessed=nbytes // 100, transcendentals=0)
 
 
 def start_of(offset):
@@ -103,22 +103,22 @@
     )(*operands)
 
 
-def pack(acc, mass, out):
+def pack(acc, out):
     blocks = acc.shape[1] // LANES
     for j in range(blocks):
         out[:, j, :] = acc[0:HALF, j * LANES : (j + 1) * LANES]
         out[:, blocks + j, :] = acc[HALF:K, j * LANES : (j + 1) * LANES]
-    out[:, 2 * blocks, :] = mass[0:HALF, :]
-    out[:, 2 * blocks + 1, :] = mass[HALF:K, :]
-    for j in range(2 * blocks + 2, out.shape[1]):
-        out[:, j, :] = jnp.zeros((HALF, LANES), F32)
+
+
+def packed_shape(cols):
+    return shape(HALF, 2 * cols // LANES, LANES)
 
 
 def first_gradient(duals, returns):
     rows, cols = returns.shape
     steps = rows // TILE
 
-    def body(u, r, out, held, kept, acc, sems, dual_sems):
+    def body(u, r, out, mass, held, kept, acc, sems, dual_sems):
         copies = []
         for i in range(steps):
             at = pl.ds(i * TILE, TILE)
@@ -137,10 +137,16 @@
                 part.astype(BF16), held[pl.ds(i * TILE, TILE), :], preferred_element_type=F32
             )
             acc[...] = term if i == 0 else acc[...] + term
-        pack(acc[...], row_total(folded), out)
+        pack(acc[...], out)
+        mass[...] = in_lanes(row_total(folded))
 
     operands = [pltpu.with_memory_space_constraint(a, pltpu.HBM) for a in (duals, returns)]
-    outs = [shape(HALF, HALF, LANES), pltpu.VMEM((rows, cols), BF16), pltpu.VMEM((K, rows), F32)]
+    outs = [
+        packed_shape(cols),
+        shape(1, K),
+        pltpu.VMEM((rows, cols), BF16),
+        pltpu.VMEM((K, rows), F32),
+    ]
     scratch = (
         pltpu.VMEM((K, cols), F32),
         pltpu.SemaphoreType.DMA((steps,)),
@@ -151,15 +157,27 @@
     )
 
 
-def own_rows(received, state, t_old, extra, first, total_cols, total_rows):
+def own_rows(received, state, extra, passed, first, total_cols, total_rows):
     scale = math.sqrt(total_cols / total_rows)
     cols = state.shape[1]
     blocks = cols // LANES
-
-    def body(got, v, t, more, out):
+    lines = 2 * blocks
+
+    def body(got, v, more, *refs):
         s = scen_index()
         grad = jnp.sum(got[...], 0)
-        out[2 * blocks : HALF, :] = jnp.zeros((HALF - 2 * blocks, LANES), F32)
+        if first:
+            out, line_out = refs
+            for j in range(blocks):
+                piece = more[pl.ds(j * LANES, LANES)].reshape(1, LANES)
+                line_out[:, j * LANES : (j + 1) * LANES] = piece
+                out[lines + j : lines + j + 1, :] = piece
+                out[lines + blocks + j : lines + blocks + j + 1, :] = piece
+        else:
+            through, out, through_out = refs
+            through_out[...] = through[...]
+            out[lines:, :] = jnp.zeros((out.shape[0] - lines, LANES), F32)
+            out[lines : lines + 1, 0:K] = more[...]
         for half in range(2):
             values = v[half * HALF : (half + 1) * HALF, :]
             at = lax.broadcasted_iota(jnp.int32, values.shape, 0) == s
@@ -169,29 +187,19 @@
                 out[line : line + 1, :] = (
                     old[:, j * LANES : (j + 1) * LANES] + STEP_V * scale * grad[line : line + 1, :]
                 )
-                if first:
-                    out[HALF + line : HALF + line + 1, :] = more[:, j * LANES : (j + 1) * LANES]
-            line = 2 * blocks + half
-            out[line : line + 1, :] = picked(t[...], s + half * HALF) - STEP_T * (
-                1.0 - grad[line : line + 1, :] / total_rows / TAIL
-            )
-        if not first:
-            out[2 * blocks + 2 : 2 * blocks + 3, 0:K] = more[...]
-
-    return call(
-        body,
-        "own_rows",
-        (received, state, t_old, extra),
-        shape(HALF + 2 * blocks if first else HALF, LANES),
-        nbytes=4 * HALF * HALF * LANES,
-    )
-
-
-def projected(gathered, own, gathered_first, own_first, lam_old, goal, first, total_cols):
-    lines = (gathered_first.shape[1] - HALF) // 2 * 2
+
+    operands = (received, state, extra) + ((passed,) if passed is not None else ())
+    outs = [shape(2 * lines, LANES), shape(1, cols)] if first else [shape(lines + 8, LANES)]
+    if passed is not None:
+        outs.append(shape(*passed.shape))
+    return call(body, "own_rows", operands, outs, nbytes=4 * HALF * lines * LANES)
+
+
+def projected(gathered, own, gathered_first, own_first, lam_old, goal, mass, first, total_cols):
+    lines = gathered_first.shape[1] // 2
     blocks = lines // 2
 
-    def body(rows, mine, means, mean, lam_in, target, out, lam_out):
+    def body(rows, mine, means, mean, lam_in, target, sums_in, out, lam_out):
         s = scen_index()
         first_row = lax.broadcasted_iota(jnp.int32, (lines, LANES), 0) < blocks
 
@@ -205,14 +213,14 @@
 
         lam = lam_in[...]
         if not first:
-            ret = rows[0, lines + 2 : lines + 3, 0:K]
+            ret = rows[0, lines : lines + 1, 0:K]
             for i in range(1, rows.shape[0]):
-                ret = ret + rows[i, lines + 2 : lines + 3, 0:K]
+                ret = ret + rows[i, lines : lines + 1, 0:K]
             lam = jnp.maximum(lam + STEP_L * (target[...] - ret / total_cols), 0.0)
         lam_out[...] = lam
         slope = STEP_V * spread(jnp.concatenate([picked(lam, s), picked(lam, s + HALF)], 0))
         parts = [
-            rows[i, 0:lines, :] + slope * means[i, HALF : HALF + lines, :]
+            rows[i, 0:lines, :] + slope * means[i, lines : 2 * lines, :]
             for i in range(rows.shape[0])
         ]
         total = parts[0]
@@ -244,9 +252,10 @@
             f_low = jnp.where(raise_low, excess, f_low)
             f_up = jnp.where(raise_low, f_up, excess)
         theta = lower + f_low * (upper - lower) / (f_low - f_up)
-        x = mine[0:lines, :] + slope * mean[HALF : HALF + lines, :]
+        x = mine[0:lines, :] + slope * mean[lines : 2 * lines, :]
         fresh = jnp.maximum(x - spread(theta), 0.0)
-        rest = mine[lines:HALF, :]
+        mass = jnp.concatenate([sums_in[...], jnp.zeros((1, LANES - K), F32)], 1)
+        rest = jnp.concatenate([mass, jnp.zeros((HALF - lines - 1, LANES), F32)], 0)
         for i in range(HALF):
             out[i, 0:lines, :] = fresh
             out[i, lines:HALF, :] = rest
@@ -254,30 +263,29 @@
     return call(
         body,
         "projected",
-        (gathered, own, gathered_first, own_first, lam_old, goal),
+        (gathered, own, gathered_first, own_first, lam_old, goal, mass),
         [shape(HALF, HALF, LANES), shape(1, K)],
         nbytes=4 * HALF * HALF * LANES,
     )
 
 
-def unpacked(received, state, start, mean_row, t_old, last):
+def unpacked(received, state, start, mean_row, t_old, last, total_rows):
     cols = state.shape[1]
     blocks = cols // LANES
 
-    def body(got, v, w, m, t, fresh, bars, t_new, t_bar, ret, *mixed):
+    def body(got, v, w, m, t, fresh, bars, t_new, t_bar, ret):
         for j in range(blocks):
             at = slice(j * LANES, (j + 1) * LANES)
             fresh[0:HALF, at] = got[:, j, :]
             fresh[HALF:K, at] = got[:, blocks + j, :]
-        column = jnp.concatenate([got[:, 2 * blocks, :], got[:, 2 * blocks + 1, :]], 0)
-        t_new[...] = in_lanes(column)
-        t_bar[...] = 2.0 * column - in_rows(t[...])
+        mass = jnp.sum(got[:, 2 * blocks, :], 0, keepdims=True)[:, 0:K]
+        t_end = t[...] - STEP_T * (1.0 - mass / total_rows / TAIL)
+        t_new[...] = t_end
+        t_bar[...] = jnp.broadcast_to(in_rows(2.0 * t_end - t[...]), (K, LANES))
         bar = 2.0 * fresh[...] - v[...]
         bars[0:K, :] = (-bar).astype(BF16)
         if not last:
             bars[K : 2 * K, :] = (-w[...]).astype(BF16)
-        else:
-            mixed[0][...] = (2.0 / 3.0) * bar + w[...] / 3.0
         ret[...] = in_lanes(row_total(lane_folded(bar * m[...])))
 
     outs = [
@@ -287,35 +295,42 @@
         shape(K, LANES),
         shape(1, K),
     ]
-    if last:
-        outs.append(shape(K, cols))
     return call(
         body, "unpacked", (received, state, start, mean_row, t_old), outs, nbytes=20 * K * cols
     )
 
 
-def loss_part(bars, returns, side, quarter, width):
+def averaged(fresh, old, start):
+    def body(new, v, w, out):
+        out[...] = (2.0 / 3.0) * (2.0 * new[...] - v[...]) + w[...] / 3.0
+
+    return call(body, "averaged", (fresh, old, start), shape(*start.shape), nbytes=16 * start.size)
+
+
+def loss_part(bars, returns, sides, quarter, width):
     cols = returns.shape[1]
     count = bars.shape[0] // K
 
     def body(b, r, *outs):
-        base = row_base(side, quarter(), width)
-        for i in range(width // TILE):
-            at = slice(i * TILE, (i + 1) * TILE)
-            block = r[pl.ds(start_of(base + i * TILE), TILE), :]
-            term = lax.dot_general(
-                block, b[...], (((1,), (1,)), ((), ())), preferred_element_type=F32
-            ).T
-            for part in range(count):
-                outs[part][:, at] = term[part * K : (part + 1) * K, :]
-
+        for index, side in enumerate(sides):
+            base = row_base(side, quarter(), width)
+            for i in range(width // TILE):
+                at = slice(i * TILE, (i + 1) * TILE)
+                block = r[pl.ds(start_of(base + i * TILE), TILE), :]
+                term = lax.dot_general(
+                    block, b[...], (((1,), (1,)), ((), ())), preferred_element_type=F32
+                ).T
+                for part in range(count):
+                    outs[index * count + part][:, at] = term[part * K : (part + 1) * K, :]
+
+    outs = [shape(K, width)] * (count * len(sides))
     return call(
         body,
         "loss_part",
         (bars, returns),
-        [shape(K, width)] * count,
-        count * K * width * cols,
-        2 * width * cols,
+        outs,
+        len(outs) * K * width * cols,
+        2 * len(sides) * width * cols,
     )
 
 
@@ -347,13 +362,18 @@
     return jnp.clip(duals + STEP_U * (loss - t_bar[:, 0:1]), 0.0, 1.0)
 
 
-def dual_rows(part, other, duals, t_bar, quarter, width):
-    def body(p, o, u, t, fresh):
-        base = row_base(1, quarter, width)
-        fresh[...] = dual_step(p[...] + o[...], u[:, pl.ds(base, width)], t[...])
-
-    return call(
-        body, "dual_rows", (part, other, duals, t_bar), shape(K, width), nbytes=16 * K * width
+def dual_rows(parts, others, duals, t_bar, width):
+    def body(pa, pb, oa, ob, u, t, ua, ub):
+        for quarter, (p, o, fresh) in enumerate(((pa, oa, ua), (pb, ob, ub))):
+            base = row_base(1, quarter, width)
+            fresh[...] = dual_step(p[...] + o[...], u[:, pl.ds(base, width)], t[...])
+
+    return call(
+        body,
+        "dual_rows",
+        (*parts, *others, duals, t_bar),
+        [shape(K, width)] * 2,
+        nbytes=32 * K * width,
     )
 
 
@@ -392,18 +412,19 @@
 def gradient_end(taken, side, quarter, returns, before, width):
     cols = returns.shape[1]
 
-    def body(r, got, acc_in, folded_in, out):
+    def body(r, got, acc_in, folded_in, out, mass):
         base = row_base(side, quarter, width)
         term = acc_in[...] + jnp.dot(
             got[...].astype(BF16), r[pl.ds(base, width), :], preferred_element_type=F32
         )
-        pack(term, row_total(folded_in[...] + lane_folded(got[...])), out)
+        pack(term, out)
+        mass[...] = in_lanes(row_total(folded_in[...] + lane_folded(got[...])))
 
     return call(
         body,
         "gradient_end",
         (returns, taken, *before),
-        shape(HALF, HALF, LANES),
+        [packed_shape(cols), shape(1, K)],
         K * width * cols,
         2 * width * cols,
     )
@@ -482,64 +503,66 @@
     total_cols = cols * 4
     total_rows = scen_rows * 32
     width = scen_rows // 4
-    mean_row = mean_return.reshape(1, cols)
     t0 = threshold.reshape(1, K)
     lam0 = multiplier.reshape(1, K)
     goal = targets.reshape(1, K)
 
-    payload, returns, duals = first_gradient(duals, returns)
+    payload, mass, returns, duals = first_gradient(duals, returns)
     returns = pinned(returns)
-    held = (returns, duals, weights, mean_row, t0, lam0, goal)
+    held = (returns, duals, weights, mean_return, t0, lam0, goal, mass)
     received, held = exchanged(payload, held)
-    returns, duals, weights, mean_row, t0, lam0, goal = held
-    own_first = own_rows(received, weights, t0, mean_row, True, total_cols, total_rows)
+    returns, duals, weights, mean_return, t0, lam0, goal, mass = held
+    own_first, mean_row = own_rows(
+        received, weights, mean_return, None, True, total_cols, total_rows
+    )
     gathered_first = lax.all_gather(own_first, ASSET)
     payload, lam0 = projected(
-        gathered_first, own_first, gathered_first, own_first, lam0, goal, True, total_cols
+        gathered_first, own_first, gathered_first, own_first, lam0, goal, mass, True, total_cols
     )
     held = (returns, duals, weights, mean_row, t0, lam0, goal, gathered_first, own_first)
     received, held = exchanged(payload, held)
     returns, duals, weights, mean_row, t0, lam0, goal, gathered_first, own_first = held
     returns = pinned(returns)
-    v1, bars, t1, bar1, ret1 = unpacked(received, weights, weights, mean_row, t0, False)
-
-    parts = []
-    keep_tails = []
-    take_tails = []
-    for quarter in range(2):
-        send, send_tail = loss_part(bars, returns, 0, lambda: quarter, width)
-        take = across(send, "core")
-        take_tails.append(across(send_tail, "core"))
-        keep, keep_tail = loss_part(bars, returns, 1, lambda: quarter, width)
-        keep_tails.append(keep_tail)
-        parts.append(plus(keep, take))
-    others = [across(part, "xh") for part in parts]
-    send_tail, tail_a = own_and_other(keep_tails, take_tails)
-
-    ua = dual_rows(parts[0], others[0], duals, bar1, 0, width)
+    v1, bars, t1, bar1, ret1 = unpacked(
+        received, weights, weights, mean_row, t0, False, total_rows
+    )
+
+    send, send_tail_a = loss_part(bars, returns, (0,), lambda: 0, width)
+    take = across(send, "core")
+    keep, keep_tail_a = loss_part(bars, returns, (1,), lambda: 0, width)
+    part_a = plus(keep, take)
+    take_tail_a = across(send_tail_a, "core")
+    part_a, bars, take_tail_a = lax.optimization_barrier((part_a, bars, take_tail_a))
+    send, send_tail_b, keep, keep_tail_b = loss_part(bars, returns, (0, 1), lambda: 1, width)
+    part_b = plus(keep, across(send, "core"))
+    take_tail_b = across(send_tail_b, "core")
+    others = (across(part_a, "xh"), across(part_b, "xh"))
+    send_tail, tail_a = own_and_other((keep_tail_a, keep_tail_b), (take_tail_a, take_tail_b))
+
+    others, send_tail = lax.optimization_barrier((others, send_tail))
+    ua, ub = dual_rows((part_a, part_b), others, duals, bar1, width)
     taken_a = across(ua, "core")
-    sums = gradient_part([(ua, 1, 0)], returns, (), width)
-    ub = dual_rows(parts[1], others[1], duals, bar1, 1, width)
     taken_b = across(ub, "core")
-    sums = gradient_part([(taken_a, 0, 0), (ub, 1, 1)], returns, sums, width)
-    payload = gradient_end(taken_b, 0, 1, returns, sums, width)
-    tail_b = across(send_tail, "xh")
+    sums = gradient_part([(ua, 1, 0), (ub, 1, 1)], returns, (), width)
+    sums = gradient_part([(taken_a, 0, 0)], returns, sums, width)
+    payload, mass = gradient_end(taken_b, 0, 1, returns, sums, width)
 
     held = (returns, duals, weights, mean_row, v1, t0, t1, lam0, goal, gathered_first, own_first)
-    held = held + (ret1, ua, ub, tail_a, tail_b)
+    held = held + (ret1, ua, ub, tail_a, send_tail, mass)
     received, held = exchanged(payload, held)
     returns, duals, weights, mean_row, v1, t0, t1, lam0, goal, gathered_first, own_first = held[:11]
-    ret1, ua, ub, tail_a, tail_b = held[11:]
-    own = own_rows(received, v1, t1, ret1, False, total_cols, total_rows)
+    ret1, ua, ub, tail_a, send_tail, mass = held[11:]
+    own, send_tail = own_rows(received, v1, ret1, send_tail, False, total_cols, total_rows)
+    tail_b = across(send_tail, "xh")
     gathered = lax.all_gather(own, ASSET)
     payload, lam1 = projected(
-        gathered, own, gathered_first, own_first, lam0, goal, False, total_cols
+        gathered, own, gathered_first, own_first, lam0, goal, mass, False, total_cols
     )
     held = (returns, duals, weights, mean_row, v1, t0, t1, lam0, lam1, goal, ua, ub, tail_a, tail_b)
     received, held = exchanged(payload, held)
     returns, duals, weights, mean_row, v1, t0, t1, lam0, lam1, goal, ua, ub, tail_a, tail_b = held
     returns = pinned(returns)
-    v2, bars, t2, bar2, ret2, weights_out = unpacked(received, v1, weights, mean_row, t1, True)
+    v2, bars, t2, bar2, ret2 = unpacked(received, v1, weights, mean_row, t1, True, total_rows)
 
     def far_quarter():
         return 1 - lax.axis_index("xh")
@@ -547,22 +570,28 @@
     def own_quarter():
         return lax.axis_index("xh")
 
-    parts = []
-    for quarter in (far_quarter, own_quarter):
-        (send,) = loss_part(bars, returns, 0, quarter, width)
-        take = across(send, "core")
-        (keep,) = loss_part(bars, returns, 1, quarter, width)
-        parts.append(plus(keep, take))
+    (send,) = loss_part(bars, returns, (0,), far_quarter, width)
+    take = across(send, "core")
+    (keep,) = loss_part(bars, returns, (1,), far_quarter, width)
+    part_a = plus(keep, take)
+    part_a, bars, v2 = lax.optimization_barrier((part_a, bars, v2))
+    send, keep = loss_part(bars, returns, (0, 1), own_quarter, width)
+    part_b = plus(keep, across(send, "core"))
+    parts = (part_a, part_b)
     other = across(parts[0], "xh")
+    weights_out = averaged(v2, v1, weights)
+    part, weights_out = lax.optimization_barrier((parts[1], weights_out))
 
     quarter, t_out, sums = final_duals(
-        parts[1], other, (tail_a, tail_b), (ua, ub), duals, t2, t1, t0, bar2, ret2, width
+        part, other, (tail_a, tail_b), (ua, ub), duals, t2, t1, t0, bar2, ret2, width
     )
     near = across(quarter, "xh")
     far = across(quarter, "core")
+    sums = lax.all_to_all(sums, ALL, 0, 0)
+    near, far, sums = lax.optimization_barrier((near, far, sums))
     far_near = across(near, "core")
-    sums = lax.all_to_all(sums, ALL, 0, 0)
     duals_out = joined((far_near, near, far, quarter), width)
+    sums, duals_out = lax.optimization_barrier((sums, duals_out))
     tail_risk, lam_out = finished(sums, t_out, lam1, lam0, goal, total_cols, total_rows)
     return (weights_out, t_out.reshape(K), duals_out, lam_out.reshape(K), tail_risk.reshape(K))
 

time: 186 us -> 173 us (0.930)
  waiting for transfers between devices: 32.4 us -> 26.7 us
  starting transfers between devices: 23.1 us -> 18.9 us
    ppermute x15, waiting for transfers between devices: 32.4 us -> 26.7 us  [across(): return lax.ppermute(values, axis, [(0, 1), (1, 0)])]
    ppermute x15, starting transfers between devices: 23.1 us -> 18.9 us  [across(): return lax.ppermute(values, axis, [(0, 1), (1, 0)])]
    all_gather x1, blocking collectives: 8.75 us -> 11.6 us  [local(): gathered = lax.all_gather(own, ASSET)]
    all_to_all x4, blocking collectives: 64.5 us -> 62.6 us  [exchanged(): received = lax.all_to_all(payload, SCEN, 0, 0)]
    all_to_all x1, blocking collectives: 14.6 us -> 12.7 us  [local(): sums = lax.all_to_all(sums, ALL, 0, 0)]
    pallas_call x28 -> x26, Pallas kernels: 31.5 us -> 30.9 us  [call(): pl.pallas_call(body, in_specs=in_specs or [VMEM] * len(operands), out_spe...]
  transfers between devices with their start and end apart: 15 -> 15, of which waited for: 5 -> 5; matrix products, arithmetic and copies ran while one was open for 0% -> 0% of each run, Pallas kernels for 7% -> 5%
where the time goes in v2:
time: 173 us
  blocking collectives  95.5 us (55%)
  Pallas kernels  30.9 us (18%)
  waiting for transfers between devices  26.7 us (15%)
  starting transfers between devices  18.9 us (11%)
    all_to_all x4, blocking collectives, exchanged(): received = lax.all_to_all(payload, SCEN, 0, 0)  62.6 us
    pallas_call x26, Pallas kernels, call(): pl.pallas_call(body, in_specs=in_specs or [VMEM] * len(operands), out_spe...  30.9 us
    ppermute x15, waiting for transfers between devices, across(): return lax.ppermute(values, axis, [(0, 1), (1, 0)])  26.7 us
    ppermute x15, starting transfers between devices, across(): return lax.ppermute(values, axis, [(0, 1), (1, 0)])  18.9 us
    all_to_all x1, blocking collectives, local(): sums = lax.all_to_all(sums, ALL, 0, 0)  12.7 us
    all_gather x1, blocking collectives, local(): gathered = lax.all_gather(own, ASSET)  11.6 us
    all_gather x1, blocking collectives, local(): gathered_first = lax.all_gather(own_first, ASSET)  8.54 us
  transfers between devices with their start and end apart: 15, of which 5 were waited for; matrix products, arithmetic and copies ran while one was open for 0% of the time, Pallas kernels for 5%

profile of v2, /device:TPU:1, one launch (start us, length us, event | category | flops | bytes accessed | tf_op | source)
XLA Modules:
  0.0 172.8 jit_solution(1186647850824160739)
XLA Ops:
  0.7 7.8 %first_gradient.1 = (f32[32,24,128]{2,1,0:T(8,128)S(1)}, f32[1,64]{1,0:T(1,128)S(1)}, bf16[6144,1536]{1,0:T(8,128)(2,1)S(1)}, f32[64,6144]{1,0:T(8,128)S(1)}) custom-call(f32[64,6144]{1,0:T(8,128)} %u.1, bf16[6144,1536]{1,0:T(8,128)(2,1)} %r.1), custom_call_target="tpu_custom_call" | custom-call | flops 12079595 | bytes 188743 | tf_op jit(solution)/shard_map/first_gradient/pallas_call | solution.py:94
  8.5 19.6 %all_to_all.25.got = f32[32,24,128]{2,1,0:T(8,128)S(1)} all-to-all(f32[32,24,128]{2,1,0:T(8,128)S(1)} %get-tuple-element.176), channel_id=1, replica_groups=mesh['z'=4,'y'=4,'xl'=2,'xh'=2,'core'=2] {'z','y','xl'}, dimensions={0} | all-to-all | bytes 786432 | tf_op jit(solution)/shard_map/all_to_all | solution.py:497
  28.2 8.5 %all-gather = f32[192,128]{1,0:T(8,128)S(1)} all-gather(f32[48,128]{1,0:T(8,128)S(1)} %get-tuple-element.271.mine.mean), channel_id=2, replica_groups=mesh['z'=4,'y'=4,'xl'=2,'xh'=2,'core'=2] {'xh','core'}, dimensions={0}, use_global_device_ids=true | all-gather | bytes 122880 | tf_op jit(solution)/shard_map/all_gather | solution.py:518
  36.7 1.6 projected.2
  38.3 14.8 %all_to_all.26.got = f32[32,32,128]{2,1,0:T(8,128)S(1)} all-to-all(f32[32,32,128]{2,1,0:T(8,128)S(1)} %get-tuple-element.198), channel_id=1, replica_groups=mesh['z'=4,'y'=4,'xl'=2,'xh'=2,'core'=2] {'z','y','xl'}, dimensions={0} | all-to-all | bytes 1048576 | tf_op jit(solution)/shard_map/all_to_all | solution.py:497
  53.5 1.5 loss_part.7
  55.0 1.7 collective-permute-start
  56.7 1.5 loss_part.6
  58.5 2.7 %loss_part.8 = (f32[64,1536]{1,0:T(8,128)S(1)}, f32[64,1536]{1,0:T(8,128)S(1)}, f32[64,1536]{1,0:T(8,128)S(1)}, f32[64,1536]{1,0:T(8,128)S(1)}) custom-call(bf16[128,1536]{1,0:T(8,128)(2,1)S(1)} %get-tuple-element.218.b, bf16[6144,1536]{1,0:T(8,128)(2,1)S(1)} %get-tuple-element.308.r), custom_call_target="tpu_custom_call" | custom-call | flops 12079595 | bytes 94371 | tf_op jit(solution)/shard_map/loss_part/pallas_call | solution.py:94
  61.8 2.4 %collective-permute-start.3 = (f32[64,1536]{1,0:T(8,128)S(1)}, f32[64,1536]{1,0:T(8,128)S(1)}, u32[]{:S(2)}, u32[]{:S(2)}) collective-permute-start(f32[64,1536]{1,0:T(8,128)S(1)} %plus.4.pa), channel_id=1, source_target_pairs={{0,2},{2,0},{1,3},{3,1},{4,6},{6,4},{5,7},{7,5},{8,10},{10,8},{9,1... | collective-permute-start | bytes 1179656 | tf_op jit(solution)/shard_map/ppermute | solution.py:492
  65.7 8.0 %collective-permute-done.3.oa = f32[64,1536]{1,0:T(8,128)S(1)} collective-permute-done((f32[64,1536]{1,0:T(8,128)S(1)}, f32[64,1536]{1,0:T(8,128)S(1)}, u32[]{:S(2)}, u32[]{:S(2)}) %collective-permute-start.3) | collective-permute-done | bytes 393248 | tf_op jit(solution)/shard_map/ppermute | solution.py:492
  73.7 8.4 %collective-permute-done.4.ob = f32[64,1536]{1,0:T(8,128)S(1)} collective-permute-done((f32[64,1536]{1,0:T(8,128)S(1)}, f32[64,1536]{1,0:T(8,128)S(1)}, u32[]{:S(2)}, u32[]{:S(2)}) %collective-permute-start.4) | collective-permute-done | bytes 393248 | tf_op jit(solution)/shard_map/ppermute | solution.py:492
  83.7 1.7 %gradient_part.2 = (f32[64,1536]{1,0:T(8,128)S(1)}, f32[64,128]{1,0:T(8,128)S(1)}) custom-call(bf16[6144,1536]{1,0:T(8,128)(2,1)S(1)} %get-tuple-element.308.r, f32[64,1536]{1,0:T(8,128)S(1)} %get-tuple-element.319.refs_0_.ua, f32[64,1536]{1,0:T(8,128)S(1)} %get-tuple-element.320.refs_1_.ub), custom_call_target="tpu_custom_call" | custom-call | flops 6039797 | bytes 94371 | tf_op jit(solution)/shard_map/gradient_part/pallas_call | solution.py:94
  87.5 13.1 %all_to_all.27.got = f32[32,24,128]{2,1,0:T(8,128)S(1)} all-to-all(f32[32,24,128]{2,1,0:T(8,128)S(1)} %get-tuple-element.247), channel_id=1, replica_groups=mesh['z'=4,'y'=4,'xl'=2,'xh'=2,'core'=2] {'z','y','xl'}, dimensions={0} | all-to-all | bytes 786432 | tf_op jit(solution)/shard_map/all_to_all | solution.py:497
  100.7 2.5 %collective-permute-start.8 = (f32[64,1536]{1,0:T(8,128)S(1)}, f32[64,1536]{1,0:T(8,128)S(1)}, u32[]{:S(2)}, u32[]{:S(2)}) collective-permute-start(f32[64,1536]{1,0:T(8,128)S(1)} %get-tuple-element.286), channel_id=1, source_target_pairs={{0,2},{2,0},{1,3},{3,1},{4,6},{6,4},{5,7},{7,5},{8,10},{10,8},{9,1... | collective-permute-start | bytes 1179656 | tf_op jit(solution)/shard_map/ppermute | solution.py:492
  103.2 11.6 %all-gather.1 = f32[128,128]{1,0:T(8,128)S(1)} all-gather(f32[32,128]{1,0:T(8,128)S(1)} %get-tuple-element.269.mine), channel_id=3, replica_groups=mesh['z'=4,'y'=4,'xl'=2,'xh'=2,'core'=2] {'xh','core'}, dimensions={0}, use_global_device_ids=true | all-gather | bytes 81920 | tf_op jit(solution)/shard_map/all_gather | solution.py:557
  114.9 1.6 projected.3
  116.4 15.0 %all_to_all.28.got = f32[32,32,128]{2,1,0:T(8,128)S(1)} all-to-all(f32[32,32,128]{2,1,0:T(8,128)S(1)} %get-tuple-element.287), channel_id=1, replica_groups=mesh['z'=4,'y'=4,'xl'=2,'xh'=2,'core'=2] {'z','y','xl'}, dimensions={0} | all-to-all | bytes 1048576 | tf_op jit(solution)/shard_map/all_to_all | solution.py:497
  133.2 1.6 collective-permute-start.9
  136.4 2.7 %loss_part.11 = (f32[64,1536]{1,0:T(8,128)S(1)}, f32[64,1536]{1,0:T(8,128)S(1)}) custom-call(bf16[64,1536]{1,0:T(8,128)(2,1)S(1)} %get-tuple-element.310.b, bf16[6144,1536]{1,0:T(8,128)(2,1)S(1)} %get-tuple-element.308.r), custom_call_target="tpu_custom_call" | custom-call | flops 6039797 | bytes 94371 | tf_op jit(solution)/shard_map/loss_part/pallas_call | solution.py:94
  139.4 2.4 %collective-permute-start.11 = (f32[64,1536]{1,0:T(8,128)S(1)}, f32[64,1536]{1,0:T(8,128)S(1)}, u32[]{:S(2)}, u32[]{:S(2)}) collective-permute-start(f32[64,1536]{1,0:T(8,128)S(1)} %plus.6), channel_id=1, source_target_pairs={{0,2},{2,0},{1,3},{3,1},{4,6},{6,4},{5,7},{7,5},{8,10},{10,8},{9,1... | collective-permute-start | bytes 1179656 | tf_op jit(solution)/shard_map/ppermute | solution.py:492
  142.7 8.7 %collective-permute-done.11.o = f32[64,1536]{1,0:T(8,128)S(1)} collective-permute-done((f32[64,1536]{1,0:T(8,128)S(1)}, f32[64,1536]{1,0:T(8,128)S(1)}, u32[]{:S(2)}, u32[]{:S(2)}) %collective-permute-start.11) | collective-permute-done | bytes 393248 | tf_op jit(solution)/shard_map/ppermute | solution.py:492
  152.3 2.5 %collective-permute-start.12 = (f32[64,1536]{1,0:T(8,128)S(1)}, f32[64,1536]{1,0:T(8,128)S(1)}, u32[]{:S(2)}, u32[]{:S(2)}) collective-permute-start(f32[64,1536]{1,0:T(8,128)S(1)} %get-tuple-element.327.own), channel_id=1, source_target_pairs={{0,2},{2,0},{1,3},{3,1},{4,6},{6,4},{5,7},{7,5},{8,10},{10,8},{9,1... | collective-permute-start | bytes 1179656 | tf_op jit(solution)/shard_map/ppermute | solution.py:492
  156.0 12.7 %all_to_all.29.got = f32[128,1,128]{2,1,0:T(1,128)S(1)} all-to-all(f32[128,1,128]{2,1,0:T(1,128)S(1)} %get-tuple-element.328), channel_id=1, replica_groups=mesh['z'=4,'y'=4,'xl'=2,'xh'=2,'core'=2] {'z','y','xl','xh','core'}, dimensions={0} | all-to-all | bytes 131072 | tf_op jit(solution)/shard_map/all_to_all | solution.py:590
  (51 shorter events, 17.4 us)
Async XLA Ops:
  0.6 27.5 %copy-start = (f32[64,1536]{1,0:T(8,128)S(1)}, f32[64,1536]{1,0:T(8,128)}, u32[]{:S(2)}) copy-start(f32[64,1536]{1,0:T(8,128)} %w.2) | copy-start | bytes 1179652
  0.6 27.5 %copy-start.1 = (f32[1536]{0:T(1024)S(1)}, f32[1536]{0:T(1024)}, u32[]{:S(2)}) copy-start(f32[1536]{0:T(1024)} %more) | copy-start | bytes 18436
  8.4 28.3 %copy-start.2 = (f32[64]{0:T(128)S(1)}, f32[64]{0:T(128)}, u32[]{:S(2)}) copy-start(f32[64]{0:T(128)} %param.9) | copy-start | bytes 772
  8.4 28.3 %copy-start.4 = (f32[64]{0:T(128)S(1)}, f32[64]{0:T(128)}, u32[]{:S(2)}) copy-start(f32[64]{0:T(128)} %param.13) | copy-start | bytes 772
  8.4 44.7 %copy-start.3 = (f32[64]{0:T(128)S(1)}, f32[64]{0:T(128)}, u32[]{:S(2)}) copy-start(f32[64]{0:T(128)} %param.11) | copy-start | bytes 772
  55.0 3.2 %collective-permute-start = (f32[64,1536]{1,0:T(8,128)S(1)}, f32[64,1536]{1,0:T(8,128)S(1)}, u32[]{:S(2)}, u32[]{:S(2)}) collective-permute-start(f32[64,1536]{1,0:T(8,128)S(1)} %get-tuple-element.215), channel_id=1, source_target_pairs={{0,1},{1,0},{2,3},{3,2},{4,5},{5,4},{6,7},{7,6},{8,9},{9,8},{10,11... | collective-permute-start | bytes 1179656 | tf_op jit(solution)/shard_map/ppermute | solution.py:492
  56.6 1.9 %collective-permute-start.1 = (f32[64,1536]{1,0:T(8,128)S(1)}, f32[64,1536]{1,0:T(8,128)S(1)}, u32[]{:S(2)}, u32[]{:S(2)}) collective-permute-start(f32[64,1536]{1,0:T(8,128)S(1)} %get-tuple-element.216), channel_id=1, source_target_pairs={{0,1},{1,0},{2,3},{3,2},{4,5},{5,4},{6,7},{7,6},{8,9},{9,8},{10,11... | collective-permute-start | bytes 1179656 | tf_op jit(solution)/shard_map/ppermute | solution.py:492
  61.2 3.0 %collective-permute-start.2 = (f32[64,1536]{1,0:T(8,128)S(1)}, f32[64,1536]{1,0:T(8,128)S(1)}, u32[]{:S(2)}, u32[]{:S(2)}) collective-permute-start(f32[64,1536]{1,0:T(8,128)S(1)} %get-tuple-element.220), channel_id=1, source_target_pairs={{0,1},{1,0},{2,3},{3,2},{4,5},{5,4},{6,7},{7,6},{8,9},{9,8},{10,11... | collective-permute-start | bytes 1179656 | tf_op jit(solution)/shard_map/ppermute | solution.py:492
  61.7 3.9 %collective-permute-start.5 = (f32[64,1536]{1,0:T(8,128)S(1)}, f32[64,1536]{1,0:T(8,128)S(1)}, u32[]{:S(2)}, u32[]{:S(2)}) collective-permute-start(f32[64,1536]{1,0:T(8,128)S(1)} %get-tuple-element.224), channel_id=1, source_target_pairs={{0,1},{1,0},{2,3},{3,2},{4,5},{5,4},{6,7},{7,6},{8,9},{9,8},{10,11... | collective-permute-start | bytes 1179656 | tf_op jit(solution)/shard_map/ppermute | solution.py:492
  61.8 11.8 %collective-permute-start.3 = (f32[64,1536]{1,0:T(8,128)S(1)}, f32[64,1536]{1,0:T(8,128)S(1)}, u32[]{:S(2)}, u32[]{:S(2)}) collective-permute-start(f32[64,1536]{1,0:T(8,128)S(1)} %plus.4.pa), channel_id=1, source_target_pairs={{0,2},{2,0},{1,3},{3,1},{4,6},{6,4},{5,7},{7,5},{8,10},{10,8},{9,1... | collective-permute-start | bytes 1179656 | tf_op jit(solution)/shard_map/ppermute | solution.py:492
  64.3 17.8 %collective-permute-start.4 = (f32[64,1536]{1,0:T(8,128)S(1)}, f32[64,1536]{1,0:T(8,128)S(1)}, u32[]{:S(2)}, u32[]{:S(2)}) collective-permute-start(f32[64,1536]{1,0:T(8,128)S(1)} %plus.5.pb), channel_id=1, source_target_pairs={{0,2},{2,0},{1,3},{3,1},{4,6},{6,4},{5,7},{7,5},{8,10},{10,8},{9,1... | collective-permute-start | bytes 1179656 | tf_op jit(solution)/shard_map/ppermute | solution.py:492
  82.3 3.1 %collective-permute-start.7 = (f32[64,1536]{1,0:T(8,128)S(1)}, f32[64,1536]{1,0:T(8,128)S(1)}, u32[]{:S(2)}, u32[]{:S(2)}) collective-permute-start(f32[64,1536]{1,0:T(8,128)S(1)} %get-tuple-element.319.refs_0_.ua), channel_id=1, source_target_pairs={{0,1},{1,0},{2,3},{3,2},{4,5},{5,4},{6,7},{7,6},{8,9},{9,8},{10,11... | collective-permute-start | bytes 1179656 | tf_op jit(solution)/shard_map/ppermute | solution.py:492
  83.6 2.8 %collective-permute-start.6 = (f32[64,1536]{1,0:T(8,128)S(1)}, f32[64,1536]{1,0:T(8,128)S(1)}, u32[]{:S(2)}, u32[]{:S(2)}) collective-permute-start(f32[64,1536]{1,0:T(8,128)S(1)} %get-tuple-element.320.refs_1_.ub), channel_id=1, source_target_pairs={{0,1},{1,0},{2,3},{3,2},{4,5},{5,4},{6,7},{7,6},{8,9},{9,8},{10,11... | collective-permute-start | bytes 1179656 | tf_op jit(solution)/shard_map/ppermute | solution.py:492
  100.7 15.7 %collective-permute-start.8 = (f32[64,1536]{1,0:T(8,128)S(1)}, f32[64,1536]{1,0:T(8,128)S(1)}, u32[]{:S(2)}, u32[]{:S(2)}) collective-permute-start(f32[64,1536]{1,0:T(8,128)S(1)} %get-tuple-element.286), channel_id=1, source_target_pairs={{0,2},{2,0},{1,3},{3,1},{4,6},{6,4},{5,7},{7,5},{8,10},{10,8},{9,1... | collective-permute-start | bytes 1179656 | tf_op jit(solution)/shard_map/ppermute | solution.py:492
  133.2 3.1 %collective-permute-start.9 = (f32[64,1536]{1,0:T(8,128)S(1)}, f32[64,1536]{1,0:T(8,128)S(1)}, u32[]{:S(2)}, u32[]{:S(2)}) collective-permute-start(f32[64,1536]{1,0:T(8,128)S(1)} %loss_part.10), channel_id=1, source_target_pairs={{0,1},{1,0},{2,3},{3,2},{4,5},{5,4},{6,7},{7,6},{8,9},{9,8},{10,11... | collective-permute-start | bytes 1179656 | tf_op jit(solution)/shard_map/ppermute | solution.py:492
  139.1 3.6 %collective-permute-start.10 = (f32[64,1536]{1,0:T(8,128)S(1)}, f32[64,1536]{1,0:T(8,128)S(1)}, u32[]{:S(2)}, u32[]{:S(2)}) collective-permute-start(f32[64,1536]{1,0:T(8,128)S(1)} %get-tuple-element.312), channel_id=1, source_target_pairs={{0,1},{1,0},{2,3},{3,2},{4,5},{5,4},{6,7},{7,6},{8,9},{9,8},{10,11... | collective-permute-start | bytes 1179656 | tf_op jit(solution)/shard_map/ppermute | solution.py:492
  139.4 12.0 %collective-permute-start.11 = (f32[64,1536]{1,0:T(8,128)S(1)}, f32[64,1536]{1,0:T(8,128)S(1)}, u32[]{:S(2)}, u32[]{:S(2)}) collective-permute-start(f32[64,1536]{1,0:T(8,128)S(1)} %plus.6), channel_id=1, source_target_pairs={{0,2},{2,0},{1,3},{3,1},{4,6},{6,4},{5,7},{7,5},{8,10},{10,8},{9,1... | collective-permute-start | bytes 1179656 | tf_op jit(solution)/shard_map/ppermute | solution.py:492
  152.3 16.5 %collective-permute-start.12 = (f32[64,1536]{1,0:T(8,128)S(1)}, f32[64,1536]{1,0:T(8,128)S(1)}, u32[]{:S(2)}, u32[]{:S(2)}) collective-permute-start(f32[64,1536]{1,0:T(8,128)S(1)} %get-tuple-element.327.own), channel_id=1, source_target_pairs={{0,2},{2,0},{1,3},{3,1},{4,6},{6,4},{5,7},{7,5},{8,10},{10,8},{9,1... | collective-permute-start | bytes 1179656 | tf_op jit(solution)/shard_map/ppermute | solution.py:492
  154.7 14.0 %collective-permute-start.13 = (f32[64,1536]{1,0:T(8,128)S(1)}, f32[64,1536]{1,0:T(8,128)S(1)}, u32[]{:S(2)}, u32[]{:S(2)}) collective-permute-start(f32[64,1536]{1,0:T(8,128)S(1)} %get-tuple-element.327.own), channel_id=1, source_target_pairs={{0,1},{1,0},{2,3},{3,2},{4,5},{5,4},{6,7},{7,6},{8,9},{9,8},{10,11... | collective-permute-start | bytes 1179656 | tf_op jit(solution)/shard_map/ppermute | solution.py:492
  168.7 3.3 %copy-start.5 = (f32[1,64]{1,0:T(1,128)S(1)}, f32[1,64]{1,0:T(1,128)}, u32[]{:S(2)}) copy-start(f32[1,64]{1,0:T(1,128)} %get-tuple-element.326.end) | copy-start | bytes 772
  168.7 2.0 %collective-permute-start.14 = (f32[64,1536]{1,0:T(8,128)S(1)}, f32[64,1536]{1,0:T(8,128)S(1)}, u32[]{:S(2)}, u32[]{:S(2)}) collective-permute-start(f32[64,1536]{1,0:T(8,128)S(1)} %collective-permute-done.12.near), channel_id=1, source_target_pairs={{0,1},{1,0},{2,3},{3,2},{4,5},{5,4},{6,7},{7,6},{8,9},{9,8},{10,11... | collective-permute-start | bytes 1179656 | tf_op jit(solution)/shard_map/ppermute | solution.py:492

commit v3 on v2

--- a/solution.py
+++ b/solution.py
@@ -89,12 +89,15 @@
     return (lax.axis_index("z") * 4 + lax.axis_index("y")) * 2 + lax.axis_index("xl")
 
 
-def call(body, name, operands, outs, macs=0, nbytes=0, scratch=(), in_specs=None):
+def call(
+    body, name, operands, outs, macs=0, nbytes=0, scratch=(), in_specs=None, out_specs=None, aliases=None
+):
     single = not isinstance(outs, list)
     return pl.pallas_call(
         body,
         in_specs=in_specs or [VMEM] * len(operands),
-        out_specs=VMEM if single else [VMEM] * len(outs),
+        out_specs=out_specs or (VMEM if single else [VMEM] * len(outs)),
+        input_output_aliases=aliases or {},
         out_shape=outs,
         scratch_shapes=list(scratch),
         compiler_params=params(),
@@ -255,16 +258,16 @@
         x = mine[0:lines, :] + slope * mean[lines : 2 * lines, :]
         fresh = jnp.maximum(x - spread(theta), 0.0)
         mass = jnp.concatenate([sums_in[...], jnp.zeros((1, LANES - K), F32)], 1)
-        rest = jnp.concatenate([mass, jnp.zeros((HALF - lines - 1, LANES), F32)], 0)
         for i in range(HALF):
-            out[i, 0:lines, :] = fresh
-            out[i, lines:HALF, :] = rest
+            for half in range(2):
+                out[i, 0:blocks, half, :] = fresh[half * blocks : (half + 1) * blocks, :]
+                out[i, blocks : blocks + 1, half, :] = mass
 
     return call(
         body,
         "projected",
         (gathered, own, gathered_first, own_first, lam_old, goal, mass),
-        [shape(HALF, HALF, LANES), shape(1, K)],
+        [shape(HALF, blocks + 1, 2, LANES), shape(1, K)],
         nbytes=4 * HALF * HALF * LANES,
     )
 
@@ -276,9 +279,9 @@
     def body(got, v, w, m, t, fresh, bars, t_new, t_bar, ret):
         for j in range(blocks):
             at = slice(j * LANES, (j + 1) * LANES)
-            fresh[0:HALF, at] = got[:, j, :]
-            fresh[HALF:K, at] = got[:, blocks + j, :]
-        mass = jnp.sum(got[:, 2 * blocks, :], 0, keepdims=True)[:, 0:K]
+            fresh[0:HALF, at] = got[:, j, 0, :]
+            fresh[HALF:K, at] = got[:, j, 1, :]
+        mass = jnp.sum(got[:, blocks, 0, :], 0, keepdims=True)[:, 0:K]
         t_end = t[...] - STEP_T * (1.0 - mass / total_rows / TAIL)
         t_new[...] = t_end
         t_bar[...] = jnp.broadcast_to(in_rows(2.0 * t_end - t[...]), (K, LANES))
@@ -362,19 +365,12 @@
     return jnp.clip(duals + STEP_U * (loss - t_bar[:, 0:1]), 0.0, 1.0)
 
 
-def dual_rows(parts, others, duals, t_bar, width):
-    def body(pa, pb, oa, ob, u, t, ua, ub):
-        for quarter, (p, o, fresh) in enumerate(((pa, oa, ua), (pb, ob, ub))):
-            base = row_base(1, quarter, width)
-            fresh[...] = dual_step(p[...] + o[...], u[:, pl.ds(base, width)], t[...])
-
-    return call(
-        body,
-        "dual_rows",
-        (*parts, *others, duals, t_bar),
-        [shape(K, width)] * 2,
-        nbytes=32 * K * width,
-    )
+def dual_row(part, other, duals, t_bar, quarter, width):
+    def body(p, o, u, t, fresh):
+        base = row_base(1, quarter, width)
+        fresh[...] = dual_step(p[...] + o[...], u[:, pl.ds(base, width)], t[...])
+
+    return call(body, "dual_row", (part, other, duals, t_bar), shape(K, width), nbytes=16 * K * width)
 
 
 def gradient_part(terms, returns, before, width):
@@ -458,14 +454,47 @@
 
 
 def joined(pieces, width):
-    def body(far_near, near, far, own, out):
+    def body(near, far, own, out, sems):
         mine = lax.axis_index("xh")
-        out[:, pl.ds(row_base(0, 1 - mine, width), width)] = far_near[...]
-        out[:, pl.ds(row_base(1, 1 - mine, width), width)] = near[...]
-        out[:, pl.ds(row_base(0, mine, width), width)] = far[...]
-        out[:, pl.ds(row_base(1, mine, width), width)] = own[...]
-
-    return call(body, "joined", pieces, shape(K, 4 * width), nbytes=32 * K * width)
+        places = ((1, 1 - mine, near), (0, mine, far), (1, mine, own))
+        copies = []
+        for i, (side, quarter, ref) in enumerate(places):
+            to = out.at[:, pl.ds(row_base(side, quarter, width), width)]
+            copies.append(pltpu.make_async_copy(ref, to, sems.at[i]))
+        for copy in copies:
+            copy.start()
+        for copy in copies:
+            copy.wait()
+
+    return call(
+        body,
+        "joined",
+        pieces,
+        pltpu.HBM((K, 4 * width), F32),
+        nbytes=24 * K * width,
+        scratch=(pltpu.SemaphoreType.DMA((3,)),),
+        out_specs=ANY,
+    )
+
+
+def completed(duals_out, last, width):
+    def body(before, piece, out, sem):
+        to = out.at[:, pl.ds(row_base(0, 1 - lax.axis_index("xh"), width), width)]
+        copy = pltpu.make_async_copy(piece, to, sem)
+        copy.start()
+        copy.wait()
+
+    return call(
+        body,
+        "completed",
+        (duals_out, last),
+        pltpu.HBM(duals_out.shape, F32),
+        nbytes=8 * K * width,
+        scratch=(pltpu.SemaphoreType.DMA,),
+        in_specs=[ANY, VMEM],
+        out_specs=ANY,
+        aliases={0: 0},
+    )
 
 
 def finished(sums, t_out, lam, lam_start, goal, total_cols, total_rows):
@@ -490,6 +519,14 @@
 
 def across(values, axis):
     return lax.ppermute(values, axis, [(0, 1), (1, 0)])
+
+
+def plus_gathered(a, both):
+    def body(x, y, out):
+        core = lax.axis_index("core")
+        out[...] = x[...] + y[1 - core]
+
+    return call(body, "plus", (a, both), shape(*a.shape), nbytes=12 * a.size)
 
 
 def exchanged(payload, others):
@@ -534,14 +571,15 @@
     take_tail_a = across(send_tail_a, "core")
     part_a, bars, take_tail_a = lax.optimization_barrier((part_a, bars, take_tail_a))
     send, send_tail_b, keep, keep_tail_b = loss_part(bars, returns, (0, 1), lambda: 1, width)
-    part_b = plus(keep, across(send, "core"))
+    part_b = plus_gathered(keep, lax.all_gather(send, "core"))
     take_tail_b = across(send_tail_b, "core")
     others = (across(part_a, "xh"), across(part_b, "xh"))
     send_tail, tail_a = own_and_other((keep_tail_a, keep_tail_b), (take_tail_a, take_tail_b))
 
-    others, send_tail = lax.optimization_barrier((others, send_tail))
-    ua, ub = dual_rows((part_a, part_b), others, duals, bar1, width)
+    ua = dual_row(part_a, others[0], duals, bar1, 0, width)
     taken_a = across(ua, "core")
+    ub = dual_row(part_b, others[1], duals, bar1, 1, width)
+    ub, send_tail = lax.optimization_barrier((ub, send_tail))
     taken_b = across(ub, "core")
     sums = gradient_part([(ua, 1, 0), (ub, 1, 1)], returns, (), width)
     sums = gradient_part([(taken_a, 0, 0)], returns, sums, width)
@@ -576,7 +614,7 @@
     part_a = plus(keep, take)
     part_a, bars, v2 = lax.optimization_barrier((part_a, bars, v2))
     send, keep = loss_part(bars, returns, (0, 1), own_quarter, width)
-    part_b = plus(keep, across(send, "core"))
+    part_b = plus_gathered(keep, lax.all_gather(send, "core"))
     parts = (part_a, part_b)
     other = across(parts[0], "xh")
     weights_out = averaged(v2, v1, weights)
@@ -590,8 +628,7 @@
     sums = lax.all_to_all(sums, ALL, 0, 0)
     near, far, sums = lax.optimization_barrier((near, far, sums))
     far_near = across(near, "core")
-    duals_out = joined((far_near, near, far, quarter), width)
-    sums, duals_out = lax.optimization_barrier((sums, duals_out))
+    duals_out = completed(joined((near, far, quarter), width), far_near, width)
     tail_risk, lam_out = finished(sums, t_out, lam1, lam0, goal, total_cols, total_rows)
     return (weights_out, t_out.reshape(K), duals_out, lam_out.reshape(K), tail_risk.reshape(K))
 

time: 173 us -> 165 us (0.954)
  waiting for transfers between devices: 26.7 us -> 13.3 us
  blocking collectives: 95.5 us -> 98.9 us
    ppermute x15 -> x13, waiting for transfers between devices: 26.7 us -> 13.3 us  [across(): return lax.ppermute(values, axis, [(0, 1), (1, 0)])]
    all_gather x0 -> x2, blocking collectives: none -> 5.2 us  [local(): part_b = plus_gathered(keep, lax.all_gather(send, 'core'))]
    all_to_all x4, blocking collectives: 62.6 us -> 60.8 us  [exchanged(): received = lax.all_to_all(payload, SCEN, 0, 0)]
    pallas_call x26 -> x28, Pallas kernels: 30.9 us -> 31.8 us  [call(): pl.pallas_call(body, in_specs=in_specs or [VMEM] * len(operands), out_spe...]
    ppermute x15 -> x13, starting transfers between devices: 18.9 us -> 19.3 us  [across(): return lax.ppermute(values, axis, [(0, 1), (1, 0)])]
  transfers between devices with their start and end apart: 15 -> 13, of which waited for: 5 -> 4; matrix products, arithmetic and copies ran while one was open for 0% -> 0% of each run, Pallas kernels for 5% -> 10%
where the time goes in v3:
time: 165 us; the launch traced here: 164 us
  blocking collectives  98.9 us (60%)
  Pallas kernels  31.8 us (19%)
  starting transfers between devices  19.3 us (12%)
  waiting for transfers between devices  13.3 us (8%)
    all_to_all x4, blocking collectives, exchanged(): received = lax.all_to_all(payload, SCEN, 0, 0)  60.8 us
    pallas_call x28, Pallas kernels, call(): pl.pallas_call(body, in_specs=in_specs or [VMEM] * len(operands), out_spe...  31.8 us
    ppermute x13, starting transfers between devices, across(): return lax.ppermute(values, axis, [(0, 1), (1, 0)])  19.3 us
    ppermute x13, waiting for transfers between devices, across(): return lax.ppermute(values, axis, [(0, 1), (1, 0)])  13.3 us
    all_to_all x1, blocking collectives, local(): sums = lax.all_to_all(sums, ALL, 0, 0)  12.7 us
    all_gather x1, blocking collectives, local(): gathered = lax.all_gather(own, ASSET)  11.6 us
    all_gather x1, blocking collectives, local(): gathered_first = lax.all_gather(own_first, ASSET)  8.54 us
    all_gather x2, blocking collectives, local(): part_b = plus_gathered(keep, lax.all_gather(send, 'core'))  5.2 us
  transfers between devices with their start and end apart: 13, of which 4 were waited for; matrix products, arithmetic and copies ran while one was open for 0% of the time, Pallas kernels for 10%

profile of v3, /device:TPU:1, one launch (start us, length us, event | category | flops | bytes accessed | tf_op | source)
XLA Modules:
  0.0 164.3 jit_solution(11836064630046444506)
XLA Ops:
  0.7 7.8 %first_gradient.1 = (f32[32,24,128]{2,1,0:T(8,128)S(1)}, f32[1,64]{1,0:T(1,128)S(1)}, bf16[6144,1536]{1,0:T(8,128)(2,1)S(1)}, f32[64,6144]{1,0:T(8,128)S(1)}) custom-call(f32[64,6144]{1,0:T(8,128)} %u.1, bf16[6144,1536]{1,0:T(8,128)(2,1)} %r.1), custom_call_target="tpu_custom_call" | custom-call | flops 12079595 | bytes 188743 | tf_op jit(solution)/shard_map/first_gradient/pallas_call | solution.py:96
  8.5 19.6 %all_to_all.25.got = f32[32,24,128]{2,1,0:T(8,128)S(1)} all-to-all(f32[32,24,128]{2,1,0:T(8,128)S(1)} %get-tuple-element.171), channel_id=1, replica_groups=mesh['z'=4,'y'=4,'xl'=2,'xh'=2,'core'=2] {'z','y','xl'}, dimensions={0} | all-to-all | bytes 786432 | tf_op jit(solution)/shard_map/all_to_all | solution.py:534
  28.2 8.5 %all-gather = f32[192,128]{1,0:T(8,128)S(1)} all-gather(f32[48,128]{1,0:T(8,128)S(1)} %get-tuple-element.263.mine.mean), channel_id=2, replica_groups=mesh['z'=4,'y'=4,'xl'=2,'xh'=2,'core'=2] {'xh','core'}, dimensions={0}, use_global_device_ids=true | all-gather | bytes 122880 | tf_op jit(solution)/shard_map/all_gather | solution.py:555
  36.7 1.7 %projected.2 = (f32[32,13,2,128]{3,2,1,0:T(2,128)S(1)}, f32[1,64]{1,0:T(1,128)S(1)}) custom-call(f32[4,48,128]{2,1,0:T(8,128)S(1)} %bitcast.12, f32[48,128]{1,0:T(8,128)S(1)} %get-tuple-element.263.mine.mean, f32[4,48,128]{2,1,0:T(8,128)S(1)} %bitcast.13, f32[48,128]{1,0:T(8,128)S(1)} %get-tuple-element.263.mine.mean, f32[1,64]{1,0:T(1,128)S(1)} %bitcast.21, ...), custom_call_target="tpu_custom_call" | custom-call | bytes 5242 | tf_op jit(solution)/shard_map/projected/pallas_call | solution.py:96
  38.5 13.8 %all_to_all.26.got = f32[32,13,2,128]{3,2,1,0:T(2,128)S(1)} all-to-all(f32[32,13,2,128]{3,2,1,0:T(2,128)S(1)} %get-tuple-element.193), channel_id=1, replica_groups=mesh['z'=4,'y'=4,'xl'=2,'xh'=2,'core'=2] {'z','y','xl'}, dimensions={0} | all-to-all | bytes 851968 | tf_op jit(solution)/shard_map/all_to_all | solution.py:534
  54.1 1.7 %collective-permute-start = (f32[64,1536]{1,0:T(8,128)S(1)}, f32[64,1536]{1,0:T(8,128)S(1)}, u32[]{:S(2)}, u32[]{:S(2)}) collective-permute-start(f32[64,1536]{1,0:T(8,128)S(1)} %get-tuple-element.210), channel_id=1, source_target_pairs={{0,1},{1,0},{2,3},{3,2},{4,5},{5,4},{6,7},{7,6},{8,9},{9,8},{10,11... | collective-permute-start | bytes 1179656 | tf_op jit(solution)/shard_map/ppermute | solution.py:521
  57.6 2.4 %collective-permute-start.5 = (f32[64,1536]{1,0:T(8,128)S(1)}, f32[64,1536]{1,0:T(8,128)S(1)}, u32[]{:S(2)}, u32[]{:S(2)}) collective-permute-start(f32[64,1536]{1,0:T(8,128)S(1)} %plus.4.p), channel_id=1, source_target_pairs={{0,2},{2,0},{1,3},{3,1},{4,6},{6,4},{5,7},{7,5},{8,10},{10,8},{9,1... | collective-permute-start | bytes 1179656 | tf_op jit(solution)/shard_map/ppermute | solution.py:521
  60.1 2.7 %loss_part.8 = (f32[64,1536]{1,0:T(8,128)S(1)}, f32[64,1536]{1,0:T(8,128)S(1)}, f32[64,1536]{1,0:T(8,128)S(1)}, f32[64,1536]{1,0:T(8,128)S(1)}) custom-call(bf16[128,1536]{1,0:T(8,128)(2,1)S(1)} %get-tuple-element.212.b, bf16[6144,1536]{1,0:T(8,128)(2,1)S(1)} %get-tuple-element.300.r), custom_call_target="tpu_custom_call" | custom-call | flops 12079595 | bytes 94371 | tf_op jit(solution)/shard_map/loss_part/pallas_call | solution.py:96
  62.8 2.7 %all-gather.1 = f32[128,1536]{1,0:T(8,128)S(1)} all-gather(f32[64,1536]{1,0:T(8,128)S(1)} %get-tuple-element.214), channel_id=3, replica_groups=mesh['z'=4,'y'=4,'xl'=2,'xh'=2,'core'=2] {'core'}, dimensions={0}, use_global_device_ids=true | all-gather | bytes 1179648 | tf_op jit(solution)/shard_map/all_gather | solution.py:574
  66.7 2.7 %collective-permute-done.5.o = f32[64,1536]{1,0:T(8,128)S(1)} collective-permute-done((f32[64,1536]{1,0:T(8,128)S(1)}, f32[64,1536]{1,0:T(8,128)S(1)}, u32[]{:S(2)}, u32[]{:S(2)}) %collective-permute-start.5) | collective-permute-done | bytes 393248 | tf_op jit(solution)/shard_map/ppermute | solution.py:521
  69.6 1.7 %collective-permute-start.6 = (f32[64,1536]{1,0:T(8,128)S(1)}, f32[64,1536]{1,0:T(8,128)S(1)}, u32[]{:S(2)}, u32[]{:S(2)}) collective-permute-start(f32[64,1536]{1,0:T(8,128)S(1)} %dual_row.3.refs_0_.ua), channel_id=1, source_target_pairs={{0,1},{1,0},{2,3},{3,2},{4,5},{5,4},{6,7},{7,6},{8,9},{9,8},{10,11... | collective-permute-start | bytes 1179656 | tf_op jit(solution)/shard_map/ppermute | solution.py:521
  71.3 6.9 %collective-permute-done.2.o = f32[64,1536]{1,0:T(8,128)S(1)} collective-permute-done((f32[64,1536]{1,0:T(8,128)S(1)}, f32[64,1536]{1,0:T(8,128)S(1)}, u32[]{:S(2)}, u32[]{:S(2)}) %collective-permute-start.2) | collective-permute-done | bytes 393248 | tf_op jit(solution)/shard_map/ppermute | solution.py:521
  79.4 1.7 %gradient_part.2 = (f32[64,1536]{1,0:T(8,128)S(1)}, f32[64,128]{1,0:T(8,128)S(1)}) custom-call(bf16[6144,1536]{1,0:T(8,128)(2,1)S(1)} %get-tuple-element.300.r, f32[64,1536]{1,0:T(8,128)S(1)} %dual_row.3.refs_0_.ua, f32[64,1536]{1,0:T(8,128)S(1)} %dual_row.2.refs_1_.ub), custom_call_target="tpu_custom_call" | custom-call | flops 6039797 | bytes 94371 | tf_op jit(solution)/shard_map/gradient_part/pallas_call | solution.py:96
  83.3 13.6 %all_to_all.27.got = f32[32,24,128]{2,1,0:T(8,128)S(1)} all-to-all(f32[32,24,128]{2,1,0:T(8,128)S(1)} %get-tuple-element.239), channel_id=1, replica_groups=mesh['z'=4,'y'=4,'xl'=2,'xh'=2,'core'=2] {'z','y','xl'}, dimensions={0} | all-to-all | bytes 786432 | tf_op jit(solution)/shard_map/all_to_all | solution.py:534
  96.9 2.5 %collective-permute-start.7 = (f32[64,1536]{1,0:T(8,128)S(1)}, f32[64,1536]{1,0:T(8,128)S(1)}, u32[]{:S(2)}, u32[]{:S(2)}) collective-permute-start(f32[64,1536]{1,0:T(8,128)S(1)} %get-tuple-element.278), channel_id=1, source_target_pairs={{0,2},{2,0},{1,3},{3,1},{4,6},{6,4},{5,7},{7,5},{8,10},{10,8},{9,1... | collective-permute-start | bytes 1179656 | tf_op jit(solution)/shard_map/ppermute | solution.py:521
  99.5 11.6 %all-gather.2 = f32[128,128]{1,0:T(8,128)S(1)} all-gather(f32[32,128]{1,0:T(8,128)S(1)} %get-tuple-element.261.mine), channel_id=4, replica_groups=mesh['z'=4,'y'=4,'xl'=2,'xh'=2,'core'=2] {'xh','core'}, dimensions={0}, use_global_device_ids=true | all-gather | bytes 81920 | tf_op jit(solution)/shard_map/all_gather | solution.py:595
  111.0 1.7 %projected.3 = (f32[32,13,2,128]{3,2,1,0:T(2,128)S(1)}, f32[1,64]{1,0:T(1,128)S(1)}) custom-call(f32[4,32,128]{2,1,0:T(8,128)S(1)} %bitcast.15, f32[32,128]{1,0:T(8,128)S(1)} %get-tuple-element.261.mine, f32[4,48,128]{2,1,0:T(8,128)S(1)} %bitcast.14, f32[48,128]{1,0:T(8,128)S(1)} %get-tuple-element.263.mine.mean, ...), custom_call_target="tpu_custom_call" | custom-call | bytes 5242 | tf_op jit(solution)/shard_map/projected/pallas_call | solution.py:96
  112.8 13.8 %all_to_all.28.got = f32[32,13,2,128]{3,2,1,0:T(2,128)S(1)} all-to-all(f32[32,13,2,128]{3,2,1,0:T(2,128)S(1)} %get-tuple-element.279), channel_id=1, replica_groups=mesh['z'=4,'y'=4,'xl'=2,'xh'=2,'core'=2] {'z','y','xl'}, dimensions={0} | all-to-all | bytes 851968 | tf_op jit(solution)/shard_map/all_to_all | solution.py:534
  131.6 2.5 %collective-permute-start.9 = (f32[64,1536]{1,0:T(8,128)S(1)}, f32[64,1536]{1,0:T(8,128)S(1)}, u32[]{:S(2)}, u32[]{:S(2)}) collective-permute-start(f32[64,1536]{1,0:T(8,128)S(1)} %plus.6), channel_id=1, source_target_pairs={{0,2},{2,0},{1,3},{3,1},{4,6},{6,4},{5,7},{7,5},{8,10},{10,8},{9,1... | collective-permute-start | bytes 1179656 | tf_op jit(solution)/shard_map/ppermute | solution.py:521
  135.0 2.7 %loss_part.11 = (f32[64,1536]{1,0:T(8,128)S(1)}, f32[64,1536]{1,0:T(8,128)S(1)}) custom-call(bf16[64,1536]{1,0:T(8,128)(2,1)S(1)} %get-tuple-element.302.b, bf16[6144,1536]{1,0:T(8,128)(2,1)S(1)} %get-tuple-element.300.r), custom_call_target="tpu_custom_call" | custom-call | flops 6039797 | bytes 94371 | tf_op jit(solution)/shard_map/loss_part/pallas_call | solution.py:96
  137.6 2.5 %all-gather.3 = f32[128,1536]{1,0:T(8,128)S(1)} all-gather(f32[64,1536]{1,0:T(8,128)S(1)} %get-tuple-element.304), channel_id=5, replica_groups=mesh['z'=4,'y'=4,'xl'=2,'xh'=2,'core'=2] {'core'}, dimensions={0}, use_global_device_ids=true | all-gather | bytes 1179648 | tf_op jit(solution)/shard_map/all_gather | solution.py:617
  140.2 3.4 %collective-permute-done.9.o = f32[64,1536]{1,0:T(8,128)S(1)} collective-permute-done((f32[64,1536]{1,0:T(8,128)S(1)}, f32[64,1536]{1,0:T(8,128)S(1)}, u32[]{:S(2)}, u32[]{:S(2)}) %collective-permute-start.9) | collective-permute-done | bytes 393248 | tf_op jit(solution)/shard_map/ppermute | solution.py:521
  144.5 2.5 %collective-permute-start.10 = (f32[64,1536]{1,0:T(8,128)S(1)}, f32[64,1536]{1,0:T(8,128)S(1)}, u32[]{:S(2)}, u32[]{:S(2)}) collective-permute-start(f32[64,1536]{1,0:T(8,128)S(1)} %get-tuple-element.319.own), channel_id=1, source_target_pairs={{0,2},{2,0},{1,3},{3,1},{4,6},{6,4},{5,7},{7,5},{8,10},{10,8},{9,1... | collective-permute-start | bytes 1179656 | tf_op jit(solution)/shard_map/ppermute | solution.py:521
  148.3 12.7 %all_to_all.29.got = f32[128,1,128]{2,1,0:T(1,128)S(1)} all-to-all(f32[128,1,128]{2,1,0:T(1,128)S(1)} %get-tuple-element.320), channel_id=1, replica_groups=mesh['z'=4,'y'=4,'xl'=2,'xh'=2,'core'=2] {'z','y','xl','xh','core'}, dimensions={0} | all-to-all | bytes 131072 | tf_op jit(solution)/shard_map/all_to_all | solution.py:628
  (51 shorter events, 19.8 us)
Async XLA Ops:
  0.6 27.5 %copy-start = (f32[64,1536]{1,0:T(8,128)S(1)}, f32[64,1536]{1,0:T(8,128)}, u32[]{:S(2)}) copy-start(f32[64,1536]{1,0:T(8,128)} %w.2) | copy-start | bytes 1179652
  0.6 27.5 %copy-start.1 = (f32[1536]{0:T(1024)S(1)}, f32[1536]{0:T(1024)}, u32[]{:S(2)}) copy-start(f32[1536]{0:T(1024)} %more) | copy-start | bytes 18436
  8.4 28.3 %copy-start.2 = (f32[64]{0:T(128)S(1)}, f32[64]{0:T(128)}, u32[]{:S(2)}) copy-start(f32[64]{0:T(128)} %param.9) | copy-start | bytes 772
  8.4 28.3 %copy-start.4 = (f32[64]{0:T(128)S(1)}, f32[64]{0:T(128)}, u32[]{:S(2)}) copy-start(f32[64]{0:T(128)} %param.13) | copy-start | bytes 772
  8.4 43.8 %copy-start.3 = (f32[64]{0:T(128)S(1)}, f32[64]{0:T(128)}, u32[]{:S(2)}) copy-start(f32[64]{0:T(128)} %param.11) | copy-start | bytes 772
  54.1 3.2 %collective-permute-start = (f32[64,1536]{1,0:T(8,128)S(1)}, f32[64,1536]{1,0:T(8,128)S(1)}, u32[]{:S(2)}, u32[]{:S(2)}) collective-permute-start(f32[64,1536]{1,0:T(8,128)S(1)} %get-tuple-element.210), channel_id=1, source_target_pairs={{0,1},{1,0},{2,3},{3,2},{4,5},{5,4},{6,7},{7,6},{8,9},{9,8},{10,11... | collective-permute-start | bytes 1179656 | tf_op jit(solution)/shard_map/ppermute | solution.py:521
  55.7 1.9 %collective-permute-start.1 = (f32[64,1536]{1,0:T(8,128)S(1)}, f32[64,1536]{1,0:T(8,128)S(1)}, u32[]{:S(2)}, u32[]{:S(2)}) collective-permute-start(f32[64,1536]{1,0:T(8,128)S(1)} %get-tuple-element.211), channel_id=1, source_target_pairs={{0,1},{1,0},{2,3},{3,2},{4,5},{5,4},{6,7},{7,6},{8,9},{9,8},{10,11... | collective-permute-start | bytes 1179656 | tf_op jit(solution)/shard_map/ppermute | solution.py:521
  57.6 11.8 %collective-permute-start.5 = (f32[64,1536]{1,0:T(8,128)S(1)}, f32[64,1536]{1,0:T(8,128)S(1)}, u32[]{:S(2)}, u32[]{:S(2)}) collective-permute-start(f32[64,1536]{1,0:T(8,128)S(1)} %plus.4.p), channel_id=1, source_target_pairs={{0,2},{2,0},{1,3},{3,1},{4,6},{6,4},{5,7},{7,5},{8,10},{10,8},{9,1... | collective-permute-start | bytes 1179656 | tf_op jit(solution)/shard_map/ppermute | solution.py:521
  65.5 12.8 %collective-permute-start.2 = (f32[64,1536]{1,0:T(8,128)S(1)}, f32[64,1536]{1,0:T(8,128)S(1)}, u32[]{:S(2)}, u32[]{:S(2)}) collective-permute-start(f32[64,1536]{1,0:T(8,128)S(1)} %plus.5.p), channel_id=1, source_target_pairs={{0,2},{2,0},{1,3},{3,1},{4,6},{6,4},{5,7},{7,5},{8,10},{10,8},{9,1... | collective-permute-start | bytes 1179656 | tf_op jit(solution)/shard_map/ppermute | solution.py:521
  66.1 12.3 %collective-permute-start.3 = (f32[64,1536]{1,0:T(8,128)S(1)}, f32[64,1536]{1,0:T(8,128)S(1)}, u32[]{:S(2)}, u32[]{:S(2)}) collective-permute-start(f32[64,1536]{1,0:T(8,128)S(1)} %get-tuple-element.220), channel_id=1, source_target_pairs={{0,1},{1,0},{2,3},{3,2},{4,5},{5,4},{6,7},{7,6},{8,9},{9,8},{10,11... | collective-permute-start | bytes 1179656 | tf_op jit(solution)/shard_map/ppermute | solution.py:521
  69.6 11.6 %collective-permute-start.6 = (f32[64,1536]{1,0:T(8,128)S(1)}, f32[64,1536]{1,0:T(8,128)S(1)}, u32[]{:S(2)}, u32[]{:S(2)}) collective-permute-start(f32[64,1536]{1,0:T(8,128)S(1)} %dual_row.3.refs_0_.ua), channel_id=1, source_target_pairs={{0,1},{1,0},{2,3},{3,2},{4,5},{5,4},{6,7},{7,6},{8,9},{9,8},{10,11... | collective-permute-start | bytes 1179656 | tf_op jit(solution)/shard_map/ppermute | solution.py:521
  78.5 3.6 %collective-permute-start.4 = (f32[64,1536]{1,0:T(8,128)S(1)}, f32[64,1536]{1,0:T(8,128)S(1)}, u32[]{:S(2)}, u32[]{:S(2)}) collective-permute-start(f32[64,1536]{1,0:T(8,128)S(1)} %dual_row.2.refs_1_.ub), channel_id=1, source_target_pairs={{0,1},{1,0},{2,3},{3,2},{4,5},{5,4},{6,7},{7,6},{8,9},{9,8},{10,11... | collective-permute-start | bytes 1179656 | tf_op jit(solution)/shard_map/ppermute | solution.py:521
  96.9 15.8 %collective-permute-start.7 = (f32[64,1536]{1,0:T(8,128)S(1)}, f32[64,1536]{1,0:T(8,128)S(1)}, u32[]{:S(2)}, u32[]{:S(2)}) collective-permute-start(f32[64,1536]{1,0:T(8,128)S(1)} %get-tuple-element.278), channel_id=1, source_target_pairs={{0,2},{2,0},{1,3},{3,1},{4,6},{6,4},{5,7},{7,5},{8,10},{10,8},{9,1... | collective-permute-start | bytes 1179656 | tf_op jit(solution)/shard_map/ppermute | solution.py:521
  128.4 3.1 %collective-permute-start.8 = (f32[64,1536]{1,0:T(8,128)S(1)}, f32[64,1536]{1,0:T(8,128)S(1)}, u32[]{:S(2)}, u32[]{:S(2)}) collective-permute-start(f32[64,1536]{1,0:T(8,128)S(1)} %loss_part.10), channel_id=1, source_target_pairs={{0,1},{1,0},{2,3},{3,2},{4,5},{5,4},{6,7},{7,6},{8,9},{9,8},{10,11... | collective-permute-start | bytes 1179656 | tf_op jit(solution)/shard_map/ppermute | solution.py:521
  131.6 12.0 %collective-permute-start.9 = (f32[64,1536]{1,0:T(8,128)S(1)}, f32[64,1536]{1,0:T(8,128)S(1)}, u32[]{:S(2)}, u32[]{:S(2)}) collective-permute-start(f32[64,1536]{1,0:T(8,128)S(1)} %plus.6), channel_id=1, source_target_pairs={{0,2},{2,0},{1,3},{3,1},{4,6},{6,4},{5,7},{7,5},{8,10},{10,8},{9,1... | collective-permute-start | bytes 1179656 | tf_op jit(solution)/shard_map/ppermute | solution.py:521
  144.5 18.2 %copy-start.5 = (f32[1,64]{1,0:T(1,128)S(1)}, f32[1,64]{1,0:T(1,128)}, u32[]{:S(2)}) copy-start(f32[1,64]{1,0:T(1,128)} %get-tuple-element.318.end) | copy-start | bytes 772
  144.5 16.5 %collective-permute-start.10 = (f32[64,1536]{1,0:T(8,128)S(1)}, f32[64,1536]{1,0:T(8,128)S(1)}, u32[]{:S(2)}, u32[]{:S(2)}) collective-permute-start(f32[64,1536]{1,0:T(8,128)S(1)} %get-tuple-element.319.own), channel_id=1, source_target_pairs={{0,2},{2,0},{1,3},{3,1},{4,6},{6,4},{5,7},{7,5},{8,10},{10,8},{9,1... | collective-permute-start | bytes 1179656 | tf_op jit(solution)/shard_map/ppermute | solution.py:521
  146.9 14.1 %collective-permute-start.11 = (f32[64,1536]{1,0:T(8,128)S(1)}, f32[64,1536]{1,0:T(8,128)S(1)}, u32[]{:S(2)}, u32[]{:S(2)}) collective-permute-start(f32[64,1536]{1,0:T(8,128)S(1)} %get-tuple-element.319.own), channel_id=1, source_target_pairs={{0,1},{1,0},{2,3},{3,2},{4,5},{5,4},{6,7},{7,6},{8,9},{9,8},{10,11... | collective-permute-start | bytes 1179656 | tf_op jit(solution)/shard_map/ppermute | solution.py:521
  161.0 2.4 %collective-permute-start.12 = (f32[64,1536]{1,0:T(8,128)S(1)}, f32[64,1536]{1,0:T(8,128)S(1)}, u32[]{:S(2)}, u32[]{:S(2)}) collective-permute-start(f32[64,1536]{1,0:T(8,128)S(1)} %collective-permute-done.10.near), channel_id=1, source_target_pairs={{0,1},{1,0},{2,3},{3,2},{4,5},{5,4},{6,7},{7,6},{8,9},{9,8},{10,11... | collective-permute-start | bytes 1179656 | tf_op jit(solution)/shard_map/ppermute | solution.py:521

commit v4 on v3

--- a/solution.py
+++ b/solution.py
@@ -9,6 +9,7 @@
 from jax.sharding import PartitionSpec as P
 
 BISECT = 6
+AHEAD = 3
 TAIL = 0.2
 STEP_V = 1.0
 STEP_T = 0.5
@@ -206,9 +207,9 @@
         s = scen_index()
         first_row = lax.broadcasted_iota(jnp.int32, (lines, LANES), 0) < blocks
 
-        def sums(values):
-            a = jnp.sum(jnp.where(first_row, values, 0.0), (0, 1), keepdims=True)
-            b = jnp.sum(jnp.where(first_row, 0.0, values), (0, 1), keepdims=True)
+        def folded(values):
+            a = jnp.sum(jnp.where(first_row, values, 0.0), 0, keepdims=True)
+            b = jnp.sum(jnp.where(first_row, 0.0, values), 0, keepdims=True)
             return jnp.concatenate([a, b], 0)
 
         def spread(pair):
@@ -231,29 +232,70 @@
         for part in parts[1:]:
             total = total + part
             top = jnp.maximum(top, part)
-        low = jnp.min(top, (0, 1), keepdims=True)
-        top_a = jnp.max(jnp.where(first_row, top, low), (0, 1), keepdims=True)
-        top_b = jnp.max(jnp.where(first_row, low, top), (0, 1), keepdims=True)
-        upper = jnp.concatenate([top_a, top_b], 0)
-        lower = sums(total) / total_cols - 1.0
-
-        def excess_at(level):
-            wide = spread(level)
-            over = jnp.maximum(parts[0] - wide, 0.0)
-            for part in parts[1:]:
-                over = over + jnp.maximum(part - wide, 0.0)
-            return sums(over) - total_cols
-
-        f_low = excess_at(lower)
+        low = jnp.min(top, 0, keepdims=True)
+        top_a = jnp.max(jnp.where(first_row, top, low), 0, keepdims=True)
+        top_b = jnp.max(jnp.where(first_row, low, top), 0, keepdims=True)
+        upper = jnp.max(jnp.concatenate([top_a, top_b], 0), 1, keepdims=True)
+        lower = jnp.sum(folded(total), 1, keepdims=True) / total_cols - 1.0
+
+        def excesses(levels):
+            found = []
+            for level in levels:
+                wide = spread(level)
+                over = jnp.maximum(parts[0] - wide, 0.0)
+                for part in parts[1:]:
+                    over = over + jnp.maximum(part - wide, 0.0)
+                found.append(folded(over))
+            whole = jnp.sum(jnp.concatenate(found, 0), 1, keepdims=True) - total_cols
+            return [whole[2 * i : 2 * i + 2, :] for i in range(len(levels))]
+
+        def middles(bounds, depth):
+            if depth == 0:
+                return None
+            low_end, high_end = bounds
+            middle = (low_end + high_end) * 0.5
+            return (
+                middle,
+                middles((low_end, middle), depth - 1),
+                middles((middle, high_end), depth - 1),
+            )
+
+        def listed(tree):
+            return [] if tree is None else [tree[0]] + listed(tree[1]) + listed(tree[2])
+
+        def with_values(tree, values):
+            if tree is None:
+                return None
+            return ((tree[0], values.pop(0)), with_values(tree[1], values), with_values(tree[2], values))
+
+        def picked_tree(raise_low, above, below):
+            if above is None:
+                return None
+            node = tuple(jnp.where(raise_low, a, b) for a, b in zip(above[0], below[0]))
+            return (
+                node,
+                picked_tree(raise_low, above[1], below[1]),
+                picked_tree(raise_low, above[2], below[2]),
+            )
+
+        f_low = None
         f_up = jnp.zeros_like(lower) - total_cols
-        for _ in range(BISECT):
-            middle = (lower + upper) * 0.5
-            excess = excess_at(middle)
-            raise_low = excess >= 0
-            lower = jnp.where(raise_low, middle, lower)
-            upper = jnp.where(raise_low, upper, middle)
-            f_low = jnp.where(raise_low, excess, f_low)
-            f_up = jnp.where(raise_low, f_up, excess)
+        for _ in range(BISECT // AHEAD):
+            tree = middles((lower, upper), AHEAD)
+            levels = listed(tree)
+            if f_low is None:
+                f_low, *values = excesses([lower] + levels)
+            else:
+                values = excesses(levels)
+            tree = with_values(tree, values)
+            while tree is not None:
+                (middle, excess), below, above = tree
+                raise_low = excess >= 0
+                lower = jnp.where(raise_low, middle, lower)
+                upper = jnp.where(raise_low, upper, middle)
+                f_low = jnp.where(raise_low, excess, f_low)
+                f_up = jnp.where(raise_low, f_up, excess)
+                tree = picked_tree(raise_low, above, below)
         theta = lower + f_low * (upper - lower) / (f_low - f_up)
         x = mine[0:lines, :] + slope * mean[lines : 2 * lines, :]
         fresh = jnp.maximum(x - spread(theta), 0.0)
@@ -303,11 +345,19 @@
     )
 
 
-def averaged(fresh, old, start):
-    def body(new, v, w, out):
-        out[...] = (2.0 / 3.0) * (2.0 * new[...] - v[...]) + w[...] / 3.0
-
-    return call(body, "averaged", (fresh, old, start), shape(*start.shape), nbytes=16 * start.size)
+def mixed(fresh, old, start):
+    return (2.0 / 3.0) * (2.0 * fresh - old) + start / 3.0
+
+
+def averaged(weights, thresholds):
+    def body(v2, v1, v0, t2, t1, t0, v_out, t_out):
+        v_out[...] = mixed(v2[...], v1[...], v0[...])
+        t_out[...] = mixed(t2[...], t1[...], t0[...])
+
+    outs = [shape(*weights[0].shape), shape(1, K)]
+    return call(
+        body, "averaged", (*weights, *thresholds), outs, nbytes=16 * weights[0].size
+    )
 
 
 def loss_part(bars, returns, sides, quarter, width):
@@ -429,15 +479,14 @@
 def final_duals(part, other, tails, held, start, t_new, t_old, t_start, t_bar, ret, width):
     devices = 128
 
-    def body(p, o, la, lb, ua, ub, u0, tn, t, ts, tb, er, duals_out, t_out, sums):
+    def body(p, o, la, lb, ua, ub, u0, tn, t, ts, tb, er, duals_out, sums):
         mine = lax.axis_index("xh")
         base = row_base(1, mine, width)
         loss = p[...] + o[...]
         old = jnp.where(mine == 0, ua[...], ub[...])
         fresh = dual_step(loss, old, tb[...])
-        duals_out[...] = (2.0 / 3.0) * (2.0 * fresh - old) + u0[:, pl.ds(base, width)] / 3.0
-        end = (2.0 / 3.0) * (2.0 * tn[...] - t[...]) + ts[...] / 3.0
-        t_out[...] = end
+        duals_out[...] = mixed(fresh, old, u0[:, pl.ds(base, width)])
+        end = mixed(tn[...], t[...], ts[...])
         tail = (2.0 / 3.0) * loss + (la[...] + lb[...]) / 3.0
         over = jnp.maximum(tail - in_rows(end), 0.0)
         line = jnp.concatenate([in_lanes(row_total(lane_folded(over))), er[...]], 1)
@@ -448,13 +497,18 @@
         body,
         "final_duals",
         operands,
-        [shape(K, width), shape(1, K), shape(devices, 1, LANES)],
+        [shape(K, width), shape(devices, 1, LANES)],
         nbytes=24 * K * width,
     )
 
 
-def joined(pieces, width):
-    def body(near, far, own, out, sems):
+def joined(pieces, width, ends, total_cols, total_rows):
+    devices = ends[0].shape[0]
+    copies_of_ret = devices // 4
+
+    def body(
+        near, far, own, got, t2, t1, t0, lam_1, lam_0, target, out, tail_out, lam_out, tail, lam, sems
+    ):
         mine = lax.axis_index("xh")
         places = ((1, 1 - mine, near), (0, mine, far), (1, mine, own))
         copies = []
@@ -463,17 +517,30 @@
             copies.append(pltpu.make_async_copy(ref, to, sems.at[i]))
         for copy in copies:
             copy.start()
+        total = jnp.sum(got[...], 0)
+        end = mixed(t2[...], t1[...], t0[...])
+        tail[...] = end + total[:, 0:K] / (TAIL * total_rows)
+        ret = total[:, K : 2 * K] / copies_of_ret
+        fresh = jnp.maximum(lam_1[...] + STEP_L * (target[...] - ret / total_cols), 0.0)
+        lam[...] = mixed(fresh, lam_1[...], lam_0[...])
+        for ref, to in ((tail, tail_out), (lam, lam_out)):
+            copies.append(pltpu.make_async_copy(ref, to, sems.at[len(copies)]))
+            copies[-1].start()
         for copy in copies:
             copy.wait()
 
     return call(
         body,
         "joined",
-        pieces,
-        pltpu.HBM((K, 4 * width), F32),
+        (*pieces, *ends),
+        [pltpu.HBM((K, 4 * width), F32), pltpu.HBM((1, K), F32), pltpu.HBM((1, K), F32)],
         nbytes=24 * K * width,
-        scratch=(pltpu.SemaphoreType.DMA((3,)),),
-        out_specs=ANY,
+        scratch=(
+            pltpu.VMEM((1, K), F32),
+            pltpu.VMEM((1, K), F32),
+            pltpu.SemaphoreType.DMA((5,)),
+        ),
+        out_specs=[ANY] * 3,
     )
 
 
@@ -497,22 +564,6 @@
     )
 
 
-def finished(sums, t_out, lam, lam_start, goal, total_cols, total_rows):
-    devices = sums.shape[0]
-    copies = devices // 4
-
-    def body(got, end, lam_old, lam_0, target, tail, lam_out):
-        total = jnp.sum(got[...], 0)
-        tail[...] = end[...] + total[:, 0:K] / (TAIL * total_rows)
-        ret = total[:, K : 2 * K] / copies
-        fresh = jnp.maximum(lam_old[...] + STEP_L * (target[...] - ret / total_cols), 0.0)
-        lam_out[...] = (2.0 / 3.0) * (2.0 * fresh - lam_old[...]) + lam_0[...] / 3.0
-
-    return call(
-        body, "finished", (sums, t_out, lam, lam_start, goal), [shape(1, K)] * 2, nbytes=devices * 512
-    )
-
-
 def pinned(a):
     return pltpu.with_memory_space_constraint(a, pltpu.VMEM)
 
@@ -569,7 +620,7 @@
     keep, keep_tail_a = loss_part(bars, returns, (1,), lambda: 0, width)
     part_a = plus(keep, take)
     take_tail_a = across(send_tail_a, "core")
-    part_a, bars, take_tail_a = lax.optimization_barrier((part_a, bars, take_tail_a))
+    part_a, bars = lax.optimization_barrier((part_a, bars))
     send, send_tail_b, keep, keep_tail_b = loss_part(bars, returns, (0, 1), lambda: 1, width)
     part_b = plus_gathered(keep, lax.all_gather(send, "core"))
     take_tail_b = across(send_tail_b, "core")
@@ -617,10 +668,10 @@
     part_b = plus_gathered(keep, lax.all_gather(send, "core"))
     parts = (part_a, part_b)
     other = across(parts[0], "xh")
-    weights_out = averaged(v2, v1, weights)
+    weights_out, threshold_out = averaged((v2, v1, weights), (t2, t1, t0))
     part, weights_out = lax.optimization_barrier((parts[1], weights_out))
 
-    quarter, t_out, sums = final_duals(
+    quarter, sums = final_duals(
         part, other, (tail_a, tail_b), (ua, ub), duals, t2, t1, t0, bar2, ret2, width
     )
     near = across(quarter, "xh")
@@ -628,9 +679,12 @@
     sums = lax.all_to_all(sums, ALL, 0, 0)
     near, far, sums = lax.optimization_barrier((near, far, sums))
     far_near = across(near, "core")
-    duals_out = completed(joined((near, far, quarter), width), far_near, width)
-    tail_risk, lam_out = finished(sums, t_out, lam1, lam0, goal, total_cols, total_rows)
-    return (weights_out, t_out.reshape(K), duals_out, lam_out.reshape(K), tail_risk.reshape(K))
+    ends = (sums, t2, t1, t0, lam1, lam0, goal)
+    duals_out, tail_risk, lam_out = joined(
+        (near, far, quarter), width, ends, total_cols, total_rows
+    )
+    duals_out = completed(duals_out, far_near, width)
+    return (weights_out, threshold_out.reshape(K), duals_out, lam_out.reshape(K), tail_risk.reshape(K))
 
 
 def solution(mesh):

time: 165 us -> 162 us (0.982)
  Pallas kernels: 31.8 us -> 28.9 us
    pallas_call x28 -> x27, Pallas kernels: 31.8 us -> 28.9 us  [call(): pl.pallas_call(body, in_specs=in_specs or [VMEM] * len(operands), out_spe...]
  transfers between devices with their start and end apart: 13 -> 13, of which waited for: 4 -> 4; matrix products, arithmetic and copies ran while one was open for 0% -> 0% of each run, Pallas kernels for 10% -> 9%
where the time goes in v4:
time: 162 us; the launch traced here: 161 us
  blocking collectives  98.7 us (61%)
  Pallas kernels  28.9 us (18%)
  starting transfers between devices  19.5 us (12%)
  waiting for transfers between devices  13.2 us (8%)
    all_to_all x4, blocking collectives, exchanged(): received = lax.all_to_all(payload, SCEN, 0, 0)  60.8 us
    pallas_call x27, Pallas kernels, call(): pl.pallas_call(body, in_specs=in_specs or [VMEM] * len(operands), out_spe...  28.9 us
    ppermute x13, starting transfers between devices, across(): return lax.ppermute(values, axis, [(0, 1), (1, 0)])  19.5 us
    ppermute x13, waiting for transfers between devices, across(): return lax.ppermute(values, axis, [(0, 1), (1, 0)])  13.2 us
    all_to_all x1, blocking collectives, local(): sums = lax.all_to_all(sums, ALL, 0, 0)  12.7 us
    all_gather x1, blocking collectives, local(): gathered = lax.all_gather(own, ASSET)  11.6 us
    all_gather x1, blocking collectives, local(): gathered_first = lax.all_gather(own_first, ASSET)  8.54 us
    all_gather x2, blocking collectives, local(): part_b = plus_gathered(keep, lax.all_gather(send, 'core'))  5.04 us
  transfers between devices with their start and end apart: 13, of which 4 were waited for; matrix products, arithmetic and copies ran while one was open for 0% of the time, Pallas kernels for 9%

profile of v4, /device:TPU:1, one launch (start us, length us, event | category | flops | bytes accessed | tf_op | source)
XLA Modules:
  0.0 161.4 jit_solution(1985504222377891918)
XLA Ops:
  0.7 7.8 %first_gradient.1 = (f32[32,24,128]{2,1,0:T(8,128)S(1)}, f32[1,64]{1,0:T(1,128)S(1)}, bf16[6144,1536]{1,0:T(8,128)(2,1)S(1)}, f32[64,6144]{1,0:T(8,128)S(1)}) custom-call(f32[64,6144]{1,0:T(8,128)} %u.1, bf16[6144,1536]{1,0:T(8,128)(2,1)} %r.1), custom_call_target="tpu_custom_call" | custom-call | flops 12079595 | bytes 188743 | tf_op jit(solution)/shard_map/first_gradient/pallas_call | solution.py:97
  8.5 19.6 %all_to_all.25.got = f32[32,24,128]{2,1,0:T(8,128)S(1)} all-to-all(f32[32,24,128]{2,1,0:T(8,128)S(1)} %get-tuple-element.172), channel_id=1, replica_groups=mesh['z'=4,'y'=4,'xl'=2,'xh'=2,'core'=2] {'z','y','xl'}, dimensions={0} | all-to-all | bytes 786432 | tf_op jit(solution)/shard_map/all_to_all | solution.py:585
  28.2 8.5 %all-gather = f32[192,128]{1,0:T(8,128)S(1)} all-gather(f32[48,128]{1,0:T(8,128)S(1)} %get-tuple-element.263.mine.mean), channel_id=2, replica_groups=mesh['z'=4,'y'=4,'xl'=2,'xh'=2,'core'=2] {'xh','core'}, dimensions={0}, use_global_device_ids=true | all-gather | bytes 122880 | tf_op jit(solution)/shard_map/all_gather | solution.py:606
  37.5 13.8 %all_to_all.26.got = f32[32,13,2,128]{3,2,1,0:T(2,128)S(1)} all-to-all(f32[32,13,2,128]{3,2,1,0:T(2,128)S(1)} %get-tuple-element.194), channel_id=1, replica_groups=mesh['z'=4,'y'=4,'xl'=2,'xh'=2,'core'=2] {'z','y','xl'}, dimensions={0} | all-to-all | bytes 851968 | tf_op jit(solution)/shard_map/all_to_all | solution.py:585
  51.7 1.5 loss_part.7
  53.1 1.7 %collective-permute-start = (f32[64,1536]{1,0:T(8,128)S(1)}, f32[64,1536]{1,0:T(8,128)S(1)}, u32[]{:S(2)}, u32[]{:S(2)}) collective-permute-start(f32[64,1536]{1,0:T(8,128)S(1)} %get-tuple-element.211), channel_id=1, source_target_pairs={{0,1},{1,0},{2,3},{3,2},{4,5},{5,4},{6,7},{7,6},{8,9},{9,8},{10,11... | collective-permute-start | bytes 1179656 | tf_op jit(solution)/shard_map/ppermute | solution.py:572
  56.3 2.5 %collective-permute-start.5 = (f32[64,1536]{1,0:T(8,128)S(1)}, f32[64,1536]{1,0:T(8,128)S(1)}, u32[]{:S(2)}, u32[]{:S(2)}) collective-permute-start(f32[64,1536]{1,0:T(8,128)S(1)} %plus.4.p), channel_id=1, source_target_pairs={{0,2},{2,0},{1,3},{3,1},{4,6},{6,4},{5,7},{7,5},{8,10},{10,8},{9,1... | collective-permute-start | bytes 1179656 | tf_op jit(solution)/shard_map/ppermute | solution.py:572
  58.9 2.7 %loss_part.8 = (f32[64,1536]{1,0:T(8,128)S(1)}, f32[64,1536]{1,0:T(8,128)S(1)}, f32[64,1536]{1,0:T(8,128)S(1)}, f32[64,1536]{1,0:T(8,128)S(1)}) custom-call(bf16[128,1536]{1,0:T(8,128)(2,1)S(1)} %get-tuple-element.212.b, bf16[6144,1536]{1,0:T(8,128)(2,1)S(1)} %get-tuple-element.300.r), custom_call_target="tpu_custom_call" | custom-call | flops 12079595 | bytes 94371 | tf_op jit(solution)/shard_map/loss_part/pallas_call | solution.py:97
  61.6 2.5 %all-gather.1 = f32[128,1536]{1,0:T(8,128)S(1)} all-gather(f32[64,1536]{1,0:T(8,128)S(1)} %get-tuple-element.214), channel_id=3, replica_groups=mesh['z'=4,'y'=4,'xl'=2,'xh'=2,'core'=2] {'core'}, dimensions={0}, use_global_device_ids=true | all-gather | bytes 1179648 | tf_op jit(solution)/shard_map/all_gather | solution.py:625
  65.4 3.0 %collective-permute-done.5.o = f32[64,1536]{1,0:T(8,128)S(1)} collective-permute-done((f32[64,1536]{1,0:T(8,128)S(1)}, f32[64,1536]{1,0:T(8,128)S(1)}, u32[]{:S(2)}, u32[]{:S(2)}) %collective-permute-start.5) | collective-permute-done | bytes 393248 | tf_op jit(solution)/shard_map/ppermute | solution.py:572
  68.5 1.8 %collective-permute-start.6 = (f32[64,1536]{1,0:T(8,128)S(1)}, f32[64,1536]{1,0:T(8,128)S(1)}, u32[]{:S(2)}, u32[]{:S(2)}) collective-permute-start(f32[64,1536]{1,0:T(8,128)S(1)} %dual_row.3.refs_0_.ua), channel_id=1, source_target_pairs={{0,1},{1,0},{2,3},{3,2},{4,5},{5,4},{6,7},{7,6},{8,9},{9,8},{10,11... | collective-permute-start | bytes 1179656 | tf_op jit(solution)/shard_map/ppermute | solution.py:572
  70.3 6.5 %collective-permute-done.1.o = f32[64,1536]{1,0:T(8,128)S(1)} collective-permute-done((f32[64,1536]{1,0:T(8,128)S(1)}, f32[64,1536]{1,0:T(8,128)S(1)}, u32[]{:S(2)}, u32[]{:S(2)}) %collective-permute-start.1) | collective-permute-done | bytes 393248 | tf_op jit(solution)/shard_map/ppermute | solution.py:572
  78.2 1.7 %gradient_part.2 = (f32[64,1536]{1,0:T(8,128)S(1)}, f32[64,128]{1,0:T(8,128)S(1)}) custom-call(bf16[6144,1536]{1,0:T(8,128)(2,1)S(1)} %get-tuple-element.300.r, f32[64,1536]{1,0:T(8,128)S(1)} %dual_row.3.refs_0_.ua, f32[64,1536]{1,0:T(8,128)S(1)} %dual_row.2.refs_1_.ub), custom_call_target="tpu_custom_call" | custom-call | flops 6039797 | bytes 94371 | tf_op jit(solution)/shard_map/gradient_part/pallas_call | solution.py:97
  82.0 13.6 %all_to_all.27.got = f32[32,24,128]{2,1,0:T(8,128)S(1)} all-to-all(f32[32,24,128]{2,1,0:T(8,128)S(1)} %get-tuple-element.239), channel_id=1, replica_groups=mesh['z'=4,'y'=4,'xl'=2,'xh'=2,'core'=2] {'z','y','xl'}, dimensions={0} | all-to-all | bytes 786432 | tf_op jit(solution)/shard_map/all_to_all | solution.py:585
  95.7 2.5 %collective-permute-start.7 = (f32[64,1536]{1,0:T(8,128)S(1)}, f32[64,1536]{1,0:T(8,128)S(1)}, u32[]{:S(2)}, u32[]{:S(2)}) collective-permute-start(f32[64,1536]{1,0:T(8,128)S(1)} %get-tuple-element.278), channel_id=1, source_target_pairs={{0,2},{2,0},{1,3},{3,1},{4,6},{6,4},{5,7},{7,5},{8,10},{10,8},{9,1... | collective-permute-start | bytes 1179656 | tf_op jit(solution)/shard_map/ppermute | solution.py:572
  98.3 11.6 %all-gather.2 = f32[128,128]{1,0:T(8,128)S(1)} all-gather(f32[32,128]{1,0:T(8,128)S(1)} %get-tuple-element.261.mine), channel_id=4, replica_groups=mesh['z'=4,'y'=4,'xl'=2,'xh'=2,'core'=2] {'xh','core'}, dimensions={0}, use_global_device_ids=true | all-gather | bytes 81920 | tf_op jit(solution)/shard_map/all_gather | solution.py:646
  110.7 13.8 %all_to_all.28.got = f32[32,13,2,128]{3,2,1,0:T(2,128)S(1)} all-to-all(f32[32,13,2,128]{3,2,1,0:T(2,128)S(1)} %get-tuple-element.279), channel_id=1, replica_groups=mesh['z'=4,'y'=4,'xl'=2,'xh'=2,'core'=2] {'z','y','xl'}, dimensions={0} | all-to-all | bytes 851968 | tf_op jit(solution)/shard_map/all_to_all | solution.py:585
  126.3 1.7 %collective-permute-start.8 = (f32[64,1536]{1,0:T(8,128)S(1)}, f32[64,1536]{1,0:T(8,128)S(1)}, u32[]{:S(2)}, u32[]{:S(2)}) collective-permute-start(f32[64,1536]{1,0:T(8,128)S(1)} %loss_part.10), channel_id=1, source_target_pairs={{0,1},{1,0},{2,3},{3,2},{4,5},{5,4},{6,7},{7,6},{8,9},{9,8},{10,11... | collective-permute-start | bytes 1179656 | tf_op jit(solution)/shard_map/ppermute | solution.py:572
  129.4 2.5 %collective-permute-start.9 = (f32[64,1536]{1,0:T(8,128)S(1)}, f32[64,1536]{1,0:T(8,128)S(1)}, u32[]{:S(2)}, u32[]{:S(2)}) collective-permute-start(f32[64,1536]{1,0:T(8,128)S(1)} %plus.6), channel_id=1, source_target_pairs={{0,2},{2,0},{1,3},{3,1},{4,6},{6,4},{5,7},{7,5},{8,10},{10,8},{9,1... | collective-permute-start | bytes 1179656 | tf_op jit(solution)/shard_map/ppermute | solution.py:572
  132.0 2.7 %loss_part.11 = (f32[64,1536]{1,0:T(8,128)S(1)}, f32[64,1536]{1,0:T(8,128)S(1)}) custom-call(bf16[64,1536]{1,0:T(8,128)(2,1)S(1)} %get-tuple-element.302.b, bf16[6144,1536]{1,0:T(8,128)(2,1)S(1)} %get-tuple-element.300.r), custom_call_target="tpu_custom_call" | custom-call | flops 6039797 | bytes 94371 | tf_op jit(solution)/shard_map/loss_part/pallas_call | solution.py:97
  134.6 2.5 %all-gather.3 = f32[128,1536]{1,0:T(8,128)S(1)} all-gather(f32[64,1536]{1,0:T(8,128)S(1)} %get-tuple-element.304), channel_id=5, replica_groups=mesh['z'=4,'y'=4,'xl'=2,'xh'=2,'core'=2] {'core'}, dimensions={0}, use_global_device_ids=true | all-gather | bytes 1179648 | tf_op jit(solution)/shard_map/all_gather | solution.py:668
  138.1 3.4 %collective-permute-done.9.o = f32[64,1536]{1,0:T(8,128)S(1)} collective-permute-done((f32[64,1536]{1,0:T(8,128)S(1)}, f32[64,1536]{1,0:T(8,128)S(1)}, u32[]{:S(2)}, u32[]{:S(2)}) %collective-permute-start.9) | collective-permute-done | bytes 393248 | tf_op jit(solution)/shard_map/ppermute | solution.py:572
  141.9 2.5 %collective-permute-start.10 = (f32[64,1536]{1,0:T(8,128)S(1)}, f32[64,1536]{1,0:T(8,128)S(1)}, u32[]{:S(2)}, u32[]{:S(2)}) collective-permute-start(f32[64,1536]{1,0:T(8,128)S(1)} %get-tuple-element.320.own), channel_id=1, source_target_pairs={{0,2},{2,0},{1,3},{3,1},{4,6},{6,4},{5,7},{7,5},{8,10},{10,8},{9,1... | collective-permute-start | bytes 1179656 | tf_op jit(solution)/shard_map/ppermute | solution.py:572
  145.8 12.7 %all_to_all.29.got = f32[128,1,128]{2,1,0:T(1,128)S(1)} all-to-all(f32[128,1,128]{2,1,0:T(1,128)S(1)} %get-tuple-element.321), channel_id=1, replica_groups=mesh['z'=4,'y'=4,'xl'=2,'xh'=2,'core'=2] {'z','y','xl','xh','core'}, dimensions={0} | all-to-all | bytes 131072 | tf_op jit(solution)/shard_map/all_to_all | solution.py:679
  (48 shorter events, 17.1 us)
Async XLA Ops:
  0.6 27.5 %copy-start = (f32[64,1536]{1,0:T(8,128)S(1)}, f32[64,1536]{1,0:T(8,128)}, u32[]{:S(2)}) copy-start(f32[64,1536]{1,0:T(8,128)} %v0) | copy-start | bytes 1179652
  0.6 27.5 %copy-start.2 = (f32[1536]{0:T(1024)S(1)}, f32[1536]{0:T(1024)}, u32[]{:S(2)}) copy-start(f32[1536]{0:T(1024)} %more) | copy-start | bytes 18436
  8.4 28.3 %copy-start.3 = (f32[64]{0:T(128)S(1)}, f32[64]{0:T(128)}, u32[]{:S(2)}) copy-start(f32[64]{0:T(128)} %param.9) | copy-start | bytes 772
  8.4 28.3 %copy-start.4 = (f32[64]{0:T(128)S(1)}, f32[64]{0:T(128)}, u32[]{:S(2)}) copy-start(f32[64]{0:T(128)} %param.13) | copy-start | bytes 772
  8.4 42.9 %copy-start.1 = (f32[64]{0:T(128)S(1)}, f32[64]{0:T(128)}, u32[]{:S(2)}) copy-start(f32[64]{0:T(128)} %param.11) | copy-start | bytes 772
  53.1 3.1 %collective-permute-start = (f32[64,1536]{1,0:T(8,128)S(1)}, f32[64,1536]{1,0:T(8,128)S(1)}, u32[]{:S(2)}, u32[]{:S(2)}) collective-permute-start(f32[64,1536]{1,0:T(8,128)S(1)} %get-tuple-element.211), channel_id=1, source_target_pairs={{0,1},{1,0},{2,3},{3,2},{4,5},{5,4},{6,7},{7,6},{8,9},{9,8},{10,11... | collective-permute-start | bytes 1179656 | tf_op jit(solution)/shard_map/ppermute | solution.py:572
  56.3 12.1 %collective-permute-start.5 = (f32[64,1536]{1,0:T(8,128)S(1)}, f32[64,1536]{1,0:T(8,128)S(1)}, u32[]{:S(2)}, u32[]{:S(2)}) collective-permute-start(f32[64,1536]{1,0:T(8,128)S(1)} %plus.4.p), channel_id=1, source_target_pairs={{0,2},{2,0},{1,3},{3,1},{4,6},{6,4},{5,7},{7,5},{8,10},{10,8},{9,1... | collective-permute-start | bytes 1179656 | tf_op jit(solution)/shard_map/ppermute | solution.py:572
  64.1 12.7 %collective-permute-start.1 = (f32[64,1536]{1,0:T(8,128)S(1)}, f32[64,1536]{1,0:T(8,128)S(1)}, u32[]{:S(2)}, u32[]{:S(2)}) collective-permute-start(f32[64,1536]{1,0:T(8,128)S(1)} %plus.5.p), channel_id=1, source_target_pairs={{0,2},{2,0},{1,3},{3,1},{4,6},{6,4},{5,7},{7,5},{8,10},{10,8},{9,1... | collective-permute-start | bytes 1179656 | tf_op jit(solution)/shard_map/ppermute | solution.py:572
  64.7 12.3 %collective-permute-start.2 = (f32[64,1536]{1,0:T(8,128)S(1)}, f32[64,1536]{1,0:T(8,128)S(1)}, u32[]{:S(2)}, u32[]{:S(2)}) collective-permute-start(f32[64,1536]{1,0:T(8,128)S(1)} %get-tuple-element.218), channel_id=1, source_target_pairs={{0,1},{1,0},{2,3},{3,2},{4,5},{5,4},{6,7},{7,6},{8,9},{9,8},{10,11... | collective-permute-start | bytes 1179656 | tf_op jit(solution)/shard_map/ppermute | solution.py:572
  65.4 11.6 %collective-permute-start.3 = (f32[64,1536]{1,0:T(8,128)S(1)}, f32[64,1536]{1,0:T(8,128)S(1)}, u32[]{:S(2)}, u32[]{:S(2)}) collective-permute-start(f32[64,1536]{1,0:T(8,128)S(1)} %get-tuple-element.220), channel_id=1, source_target_pairs={{0,1},{1,0},{2,3},{3,2},{4,5},{5,4},{6,7},{7,6},{8,9},{9,8},{10,11... | collective-permute-start | bytes 1179656 | tf_op jit(solution)/shard_map/ppermute | solution.py:572
  68.5 11.4 %collective-permute-start.6 = (f32[64,1536]{1,0:T(8,128)S(1)}, f32[64,1536]{1,0:T(8,128)S(1)}, u32[]{:S(2)}, u32[]{:S(2)}) collective-permute-start(f32[64,1536]{1,0:T(8,128)S(1)} %dual_row.3.refs_0_.ua), channel_id=1, source_target_pairs={{0,1},{1,0},{2,3},{3,2},{4,5},{5,4},{6,7},{7,6},{8,9},{9,8},{10,11... | collective-permute-start | bytes 1179656 | tf_op jit(solution)/shard_map/ppermute | solution.py:572
  77.1 3.9 %collective-permute-start.4 = (f32[64,1536]{1,0:T(8,128)S(1)}, f32[64,1536]{1,0:T(8,128)S(1)}, u32[]{:S(2)}, u32[]{:S(2)}) collective-permute-start(f32[64,1536]{1,0:T(8,128)S(1)} %dual_row.2.refs_1_.ub), channel_id=1, source_target_pairs={{0,1},{1,0},{2,3},{3,2},{4,5},{5,4},{6,7},{7,6},{8,9},{9,8},{10,11... | collective-permute-start | bytes 1179656 | tf_op jit(solution)/shard_map/ppermute | solution.py:572
  95.7 14.9 %collective-permute-start.7 = (f32[64,1536]{1,0:T(8,128)S(1)}, f32[64,1536]{1,0:T(8,128)S(1)}, u32[]{:S(2)}, u32[]{:S(2)}) collective-permute-start(f32[64,1536]{1,0:T(8,128)S(1)} %get-tuple-element.278), channel_id=1, source_target_pairs={{0,2},{2,0},{1,3},{3,1},{4,6},{6,4},{5,7},{7,5},{8,10},{10,8},{9,1... | collective-permute-start | bytes 1179656 | tf_op jit(solution)/shard_map/ppermute | solution.py:572
  126.3 3.1 %collective-permute-start.8 = (f32[64,1536]{1,0:T(8,128)S(1)}, f32[64,1536]{1,0:T(8,128)S(1)}, u32[]{:S(2)}, u32[]{:S(2)}) collective-permute-start(f32[64,1536]{1,0:T(8,128)S(1)} %loss_part.10), channel_id=1, source_target_pairs={{0,1},{1,0},{2,3},{3,2},{4,5},{5,4},{6,7},{7,6},{8,9},{9,8},{10,11... | collective-permute-start | bytes 1179656 | tf_op jit(solution)/shard_map/ppermute | solution.py:572
  129.4 12.0 %collective-permute-start.9 = (f32[64,1536]{1,0:T(8,128)S(1)}, f32[64,1536]{1,0:T(8,128)S(1)}, u32[]{:S(2)}, u32[]{:S(2)}) collective-permute-start(f32[64,1536]{1,0:T(8,128)S(1)} %plus.6), channel_id=1, source_target_pairs={{0,2},{2,0},{1,3},{3,1},{4,6},{6,4},{5,7},{7,5},{8,10},{10,8},{9,1... | collective-permute-start | bytes 1179656 | tf_op jit(solution)/shard_map/ppermute | solution.py:572
  141.9 16.6 %collective-permute-start.10 = (f32[64,1536]{1,0:T(8,128)S(1)}, f32[64,1536]{1,0:T(8,128)S(1)}, u32[]{:S(2)}, u32[]{:S(2)}) collective-permute-start(f32[64,1536]{1,0:T(8,128)S(1)} %get-tuple-element.320.own), channel_id=1, source_target_pairs={{0,2},{2,0},{1,3},{3,1},{4,6},{6,4},{5,7},{7,5},{8,10},{10,8},{9,1... | collective-permute-start | bytes 1179656 | tf_op jit(solution)/shard_map/ppermute | solution.py:572
  144.4 14.1 %collective-permute-start.11 = (f32[64,1536]{1,0:T(8,128)S(1)}, f32[64,1536]{1,0:T(8,128)S(1)}, u32[]{:S(2)}, u32[]{:S(2)}) collective-permute-start(f32[64,1536]{1,0:T(8,128)S(1)} %get-tuple-element.320.own), channel_id=1, source_target_pairs={{0,1},{1,0},{2,3},{3,2},{4,5},{5,4},{6,7},{7,6},{8,9},{9,8},{10,11... | collective-permute-start | bytes 1179656 | tf_op jit(solution)/shard_map/ppermute | solution.py:572
  158.5 2.0 %collective-permute-start.12 = (f32[64,1536]{1,0:T(8,128)S(1)}, f32[64,1536]{1,0:T(8,128)S(1)}, u32[]{:S(2)}, u32[]{:S(2)}) collective-permute-start(f32[64,1536]{1,0:T(8,128)S(1)} %collective-permute-done.10.near), channel_id=1, source_target_pairs={{0,1},{1,0},{2,3},{3,2},{4,5},{5,4},{6,7},{7,6},{8,9},{9,8},{10,11... | collective-permute-start | bytes 1179656 | tf_op jit(solution)/shard_map/ppermute | solution.py:572

commit v5 on v4

--- a/solution.py
+++ b/solution.py
@@ -24,6 +24,7 @@
 HALF = 32
 LANES = 128
 TILE = 768
+FIRST_TILE = 384
 
 F32 = jnp.float32
 BF16 = jnp.bfloat16
@@ -120,12 +121,12 @@
 
 def first_gradient(duals, returns):
     rows, cols = returns.shape
-    steps = rows // TILE
+    steps = rows // FIRST_TILE
 
     def body(u, r, out, mass, held, kept, acc, sems, dual_sems):
         copies = []
         for i in range(steps):
-            at = pl.ds(i * TILE, TILE)
+            at = pl.ds(i * FIRST_TILE, FIRST_TILE)
             mine = pltpu.make_async_copy(u.at[:, at], kept.at[:, at], dual_sems.at[i])
             block = pltpu.make_async_copy(r.at[at], held.at[at], sems.at[i])
             mine.start()
@@ -134,11 +135,11 @@
         folded = jnp.zeros((K, LANES), F32)
         for i in range(steps):
             copies[i][0].wait()
-            part = kept[:, i * TILE : (i + 1) * TILE]
+            part = kept[:, i * FIRST_TILE : (i + 1) * FIRST_TILE]
             folded = folded + lane_folded(part)
             copies[i][1].wait()
             term = jnp.dot(
-                part.astype(BF16), held[pl.ds(i * TILE, TILE), :], preferred_element_type=F32
+                part.astype(BF16), held[pl.ds(i * FIRST_TILE, FIRST_TILE), :], preferred_element_type=F32
             )
             acc[...] = term if i == 0 else acc[...] + term
         pack(acc[...], out)

time: 162 us -> 162 us (level)
  no operation moved by 1% of the time
where the time goes in v5:
time: 162 us; the launch traced here: 161 us
  blocking collectives  98.9 us (61%)
  Pallas kernels  28.7 us (18%)
  starting transfers between devices  19.5 us (12%)
  waiting for transfers between devices  13.3 us (8%)
    all_to_all x4, blocking collectives, exchanged(): received = lax.all_to_all(payload, SCEN, 0, 0)  61 us
    pallas_call x27, Pallas kernels, call(): pl.pallas_call(body, in_specs=in_specs or [VMEM] * len(operands), out_spe...  28.7 us
    ppermute x13, starting transfers between devices, across(): return lax.ppermute(values, axis, [(0, 1), (1, 0)])  19.5 us
    ppermute x13, waiting for transfers between devices, across(): return lax.ppermute(values, axis, [(0, 1), (1, 0)])  13.3 us
    all_to_all x1, blocking collectives, local(): sums = lax.all_to_all(sums, ALL, 0, 0)  12.7 us
    all_gather x1, blocking collectives, local(): gathered = lax.all_gather(own, ASSET)  11.6 us
    all_gather x1, blocking collectives, local(): gathered_first = lax.all_gather(own_first, ASSET)  8.54 us
    all_gather x2, blocking collectives, local(): part_b = plus_gathered(keep, lax.all_gather(send, 'core'))  5.04 us
  transfers between devices with their start and end apart: 13, of which 4 were waited for; matrix products, arithmetic and copies ran while one was open for 0% of the time, Pallas kernels for 9%

profile of v5, /device:TPU:1, one launch (start us, length us, event | category | flops | bytes accessed | tf_op | source)
XLA Modules:
  0.0 161.4 jit_solution(11662947003250810897)
XLA Ops:
  0.7 7.6 %first_gradient.1 = (f32[32,24,128]{2,1,0:T(8,128)S(1)}, f32[1,64]{1,0:T(1,128)S(1)}, bf16[6144,1536]{1,0:T(8,128)(2,1)S(1)}, f32[64,6144]{1,0:T(8,128)S(1)}) custom-call(f32[64,6144]{1,0:T(8,128)} %u.1, bf16[6144,1536]{1,0:T(8,128)(2,1)} %r.1), custom_call_target="tpu_custom_call" | custom-call | flops 12079595 | bytes 188743 | tf_op jit(solution)/shard_map/first_gradient/pallas_call | solution.py:98
  8.3 19.6 %all_to_all.25.got = f32[32,24,128]{2,1,0:T(8,128)S(1)} all-to-all(f32[32,24,128]{2,1,0:T(8,128)S(1)} %get-tuple-element.172), channel_id=1, replica_groups=mesh['z'=4,'y'=4,'xl'=2,'xh'=2,'core'=2] {'z','y','xl'}, dimensions={0} | all-to-all | bytes 786432 | tf_op jit(solution)/shard_map/all_to_all | solution.py:586
  28.1 8.5 %all-gather = f32[192,128]{1,0:T(8,128)S(1)} all-gather(f32[48,128]{1,0:T(8,128)S(1)} %get-tuple-element.263.mine.mean), channel_id=2, replica_groups=mesh['z'=4,'y'=4,'xl'=2,'xh'=2,'core'=2] {'xh','core'}, dimensions={0}, use_global_device_ids=true | all-gather | bytes 122880 | tf_op jit(solution)/shard_map/all_gather | solution.py:607
  37.4 13.8 %all_to_all.26.got = f32[32,13,2,128]{3,2,1,0:T(2,128)S(1)} all-to-all(f32[32,13,2,128]{3,2,1,0:T(2,128)S(1)} %get-tuple-element.194), channel_id=1, replica_groups=mesh['z'=4,'y'=4,'xl'=2,'xh'=2,'core'=2] {'z','y','xl'}, dimensions={0} | all-to-all | bytes 851968 | tf_op jit(solution)/shard_map/all_to_all | solution.py:586
  51.5 1.5 loss_part.7
  53.0 1.7 %collective-permute-start = (f32[64,1536]{1,0:T(8,128)S(1)}, f32[64,1536]{1,0:T(8,128)S(1)}, u32[]{:S(2)}, u32[]{:S(2)}) collective-permute-start(f32[64,1536]{1,0:T(8,128)S(1)} %get-tuple-element.211), channel_id=1, source_target_pairs={{0,1},{1,0},{2,3},{3,2},{4,5},{5,4},{6,7},{7,6},{8,9},{9,8},{10,11... | collective-permute-start | bytes 1179656 | tf_op jit(solution)/shard_map/ppermute | solution.py:573
  56.2 2.5 %collective-permute-start.5 = (f32[64,1536]{1,0:T(8,128)S(1)}, f32[64,1536]{1,0:T(8,128)S(1)}, u32[]{:S(2)}, u32[]{:S(2)}) collective-permute-start(f32[64,1536]{1,0:T(8,128)S(1)} %plus.4.p), channel_id=1, source_target_pairs={{0,2},{2,0},{1,3},{3,1},{4,6},{6,4},{5,7},{7,5},{8,10},{10,8},{9,1... | collective-permute-start | bytes 1179656 | tf_op jit(solution)/shard_map/ppermute | solution.py:573
  58.8 2.7 %loss_part.8 = (f32[64,1536]{1,0:T(8,128)S(1)}, f32[64,1536]{1,0:T(8,128)S(1)}, f32[64,1536]{1,0:T(8,128)S(1)}, f32[64,1536]{1,0:T(8,128)S(1)}) custom-call(bf16[128,1536]{1,0:T(8,128)(2,1)S(1)} %get-tuple-element.212.b, bf16[6144,1536]{1,0:T(8,128)(2,1)S(1)} %get-tuple-element.300.r), custom_call_target="tpu_custom_call" | custom-call | flops 12079595 | bytes 94371 | tf_op jit(solution)/shard_map/loss_part/pallas_call | solution.py:98
  61.5 2.5 %all-gather.1 = f32[128,1536]{1,0:T(8,128)S(1)} all-gather(f32[64,1536]{1,0:T(8,128)S(1)} %get-tuple-element.214), channel_id=3, replica_groups=mesh['z'=4,'y'=4,'xl'=2,'xh'=2,'core'=2] {'core'}, dimensions={0}, use_global_device_ids=true | all-gather | bytes 1179648 | tf_op jit(solution)/shard_map/all_gather | solution.py:626
  65.3 3.0 %collective-permute-done.5.o = f32[64,1536]{1,0:T(8,128)S(1)} collective-permute-done((f32[64,1536]{1,0:T(8,128)S(1)}, f32[64,1536]{1,0:T(8,128)S(1)}, u32[]{:S(2)}, u32[]{:S(2)}) %collective-permute-start.5) | collective-permute-done | bytes 393248 | tf_op jit(solution)/shard_map/ppermute | solution.py:573
  68.4 1.7 %collective-permute-start.6 = (f32[64,1536]{1,0:T(8,128)S(1)}, f32[64,1536]{1,0:T(8,128)S(1)}, u32[]{:S(2)}, u32[]{:S(2)}) collective-permute-start(f32[64,1536]{1,0:T(8,128)S(1)} %dual_row.3.refs_0_.ua), channel_id=1, source_target_pairs={{0,1},{1,0},{2,3},{3,2},{4,5},{5,4},{6,7},{7,6},{8,9},{9,8},{10,11... | collective-permute-start | bytes 1179656 | tf_op jit(solution)/shard_map/ppermute | solution.py:573
  70.1 6.7 %collective-permute-done.1.o = f32[64,1536]{1,0:T(8,128)S(1)} collective-permute-done((f32[64,1536]{1,0:T(8,128)S(1)}, f32[64,1536]{1,0:T(8,128)S(1)}, u32[]{:S(2)}, u32[]{:S(2)}) %collective-permute-start.1) | collective-permute-done | bytes 393248 | tf_op jit(solution)/shard_map/ppermute | solution.py:573
  78.1 1.7 %gradient_part.2 = (f32[64,1536]{1,0:T(8,128)S(1)}, f32[64,128]{1,0:T(8,128)S(1)}) custom-call(bf16[6144,1536]{1,0:T(8,128)(2,1)S(1)} %get-tuple-element.300.r, f32[64,1536]{1,0:T(8,128)S(1)} %dual_row.3.refs_0_.ua, f32[64,1536]{1,0:T(8,128)S(1)} %dual_row.2.refs_1_.ub), custom_call_target="tpu_custom_call" | custom-call | flops 6039797 | bytes 94371 | tf_op jit(solution)/shard_map/gradient_part/pallas_call | solution.py:98
  81.9 13.8 %all_to_all.27.got = f32[32,24,128]{2,1,0:T(8,128)S(1)} all-to-all(f32[32,24,128]{2,1,0:T(8,128)S(1)} %get-tuple-element.239), channel_id=1, replica_groups=mesh['z'=4,'y'=4,'xl'=2,'xh'=2,'core'=2] {'z','y','xl'}, dimensions={0} | all-to-all | bytes 786432 | tf_op jit(solution)/shard_map/all_to_all | solution.py:586
  95.8 2.5 %collective-permute-start.7 = (f32[64,1536]{1,0:T(8,128)S(1)}, f32[64,1536]{1,0:T(8,128)S(1)}, u32[]{:S(2)}, u32[]{:S(2)}) collective-permute-start(f32[64,1536]{1,0:T(8,128)S(1)} %get-tuple-element.278), channel_id=1, source_target_pairs={{0,2},{2,0},{1,3},{3,1},{4,6},{6,4},{5,7},{7,5},{8,10},{10,8},{9,1... | collective-permute-start | bytes 1179656 | tf_op jit(solution)/shard_map/ppermute | solution.py:573
  98.3 11.6 %all-gather.2 = f32[128,128]{1,0:T(8,128)S(1)} all-gather(f32[32,128]{1,0:T(8,128)S(1)} %get-tuple-element.261.mine), channel_id=4, replica_groups=mesh['z'=4,'y'=4,'xl'=2,'xh'=2,'core'=2] {'xh','core'}, dimensions={0}, use_global_device_ids=true | all-gather | bytes 81920 | tf_op jit(solution)/shard_map/all_gather | solution.py:647
  110.7 13.8 %all_to_all.28.got = f32[32,13,2,128]{3,2,1,0:T(2,128)S(1)} all-to-all(f32[32,13,2,128]{3,2,1,0:T(2,128)S(1)} %get-tuple-element.279), channel_id=1, replica_groups=mesh['z'=4,'y'=4,'xl'=2,'xh'=2,'core'=2] {'z','y','xl'}, dimensions={0} | all-to-all | bytes 851968 | tf_op jit(solution)/shard_map/all_to_all | solution.py:586
  126.3 1.7 %collective-permute-start.8 = (f32[64,1536]{1,0:T(8,128)S(1)}, f32[64,1536]{1,0:T(8,128)S(1)}, u32[]{:S(2)}, u32[]{:S(2)}) collective-permute-start(f32[64,1536]{1,0:T(8,128)S(1)} %loss_part.10), channel_id=1, source_target_pairs={{0,1},{1,0},{2,3},{3,2},{4,5},{5,4},{6,7},{7,6},{8,9},{9,8},{10,11... | collective-permute-start | bytes 1179656 | tf_op jit(solution)/shard_map/ppermute | solution.py:573
  129.5 2.5 %collective-permute-start.9 = (f32[64,1536]{1,0:T(8,128)S(1)}, f32[64,1536]{1,0:T(8,128)S(1)}, u32[]{:S(2)}, u32[]{:S(2)}) collective-permute-start(f32[64,1536]{1,0:T(8,128)S(1)} %plus.6), channel_id=1, source_target_pairs={{0,2},{2,0},{1,3},{3,1},{4,6},{6,4},{5,7},{7,5},{8,10},{10,8},{9,1... | collective-permute-start | bytes 1179656 | tf_op jit(solution)/shard_map/ppermute | solution.py:573
  132.0 2.7 %loss_part.11 = (f32[64,1536]{1,0:T(8,128)S(1)}, f32[64,1536]{1,0:T(8,128)S(1)}) custom-call(bf16[64,1536]{1,0:T(8,128)(2,1)S(1)} %get-tuple-element.302.b, bf16[6144,1536]{1,0:T(8,128)(2,1)S(1)} %get-tuple-element.300.r), custom_call_target="tpu_custom_call" | custom-call | flops 6039797 | bytes 94371 | tf_op jit(solution)/shard_map/loss_part/pallas_call | solution.py:98
  134.7 2.5 %all-gather.3 = f32[128,1536]{1,0:T(8,128)S(1)} all-gather(f32[64,1536]{1,0:T(8,128)S(1)} %get-tuple-element.304), channel_id=5, replica_groups=mesh['z'=4,'y'=4,'xl'=2,'xh'=2,'core'=2] {'core'}, dimensions={0}, use_global_device_ids=true | all-gather | bytes 1179648 | tf_op jit(solution)/shard_map/all_gather | solution.py:669
  138.1 3.4 %collective-permute-done.9.o = f32[64,1536]{1,0:T(8,128)S(1)} collective-permute-done((f32[64,1536]{1,0:T(8,128)S(1)}, f32[64,1536]{1,0:T(8,128)S(1)}, u32[]{:S(2)}, u32[]{:S(2)}) %collective-permute-start.9) | collective-permute-done | bytes 393248 | tf_op jit(solution)/shard_map/ppermute | solution.py:573
  141.9 2.5 %collective-permute-start.10 = (f32[64,1536]{1,0:T(8,128)S(1)}, f32[64,1536]{1,0:T(8,128)S(1)}, u32[]{:S(2)}, u32[]{:S(2)}) collective-permute-start(f32[64,1536]{1,0:T(8,128)S(1)} %get-tuple-element.320.own), channel_id=1, source_target_pairs={{0,2},{2,0},{1,3},{3,1},{4,6},{6,4},{5,7},{7,5},{8,10},{10,8},{9,1... | collective-permute-start | bytes 1179656 | tf_op jit(solution)/shard_map/ppermute | solution.py:573
  145.8 12.7 %all_to_all.29.got = f32[128,1,128]{2,1,0:T(1,128)S(1)} all-to-all(f32[128,1,128]{2,1,0:T(1,128)S(1)} %get-tuple-element.321), channel_id=1, replica_groups=mesh['z'=4,'y'=4,'xl'=2,'xh'=2,'core'=2] {'z','y','xl','xh','core'}, dimensions={0} | all-to-all | bytes 131072 | tf_op jit(solution)/shard_map/all_to_all | solution.py:680
  (48 shorter events, 17.1 us)
Async XLA Ops:
  0.6 27.3 %copy-start = (f32[64,1536]{1,0:T(8,128)S(1)}, f32[64,1536]{1,0:T(8,128)}, u32[]{:S(2)}) copy-start(f32[64,1536]{1,0:T(8,128)} %v0) | copy-start | bytes 1179652
  0.6 27.3 %copy-start.2 = (f32[1536]{0:T(1024)S(1)}, f32[1536]{0:T(1024)}, u32[]{:S(2)}) copy-start(f32[1536]{0:T(1024)} %more) | copy-start | bytes 18436
  8.3 28.3 %copy-start.3 = (f32[64]{0:T(128)S(1)}, f32[64]{0:T(128)}, u32[]{:S(2)}) copy-start(f32[64]{0:T(128)} %param.9) | copy-start | bytes 772
  8.3 28.3 %copy-start.4 = (f32[64]{0:T(128)S(1)}, f32[64]{0:T(128)}, u32[]{:S(2)}) copy-start(f32[64]{0:T(128)} %param.13) | copy-start | bytes 772
  8.3 42.9 %copy-start.1 = (f32[64]{0:T(128)S(1)}, f32[64]{0:T(128)}, u32[]{:S(2)}) copy-start(f32[64]{0:T(128)} %param.11) | copy-start | bytes 772
  53.0 3.1 %collective-permute-start = (f32[64,1536]{1,0:T(8,128)S(1)}, f32[64,1536]{1,0:T(8,128)S(1)}, u32[]{:S(2)}, u32[]{:S(2)}) collective-permute-start(f32[64,1536]{1,0:T(8,128)S(1)} %get-tuple-element.211), channel_id=1, source_target_pairs={{0,1},{1,0},{2,3},{3,2},{4,5},{5,4},{6,7},{7,6},{8,9},{9,8},{10,11... | collective-permute-start | bytes 1179656 | tf_op jit(solution)/shard_map/ppermute | solution.py:573
  56.2 12.1 %collective-permute-start.5 = (f32[64,1536]{1,0:T(8,128)S(1)}, f32[64,1536]{1,0:T(8,128)S(1)}, u32[]{:S(2)}, u32[]{:S(2)}) collective-permute-start(f32[64,1536]{1,0:T(8,128)S(1)} %plus.4.p), channel_id=1, source_target_pairs={{0,2},{2,0},{1,3},{3,1},{4,6},{6,4},{5,7},{7,5},{8,10},{10,8},{9,1... | collective-permute-start | bytes 1179656 | tf_op jit(solution)/shard_map/ppermute | solution.py:573
  64.0 12.8 %collective-permute-start.1 = (f32[64,1536]{1,0:T(8,128)S(1)}, f32[64,1536]{1,0:T(8,128)S(1)}, u32[]{:S(2)}, u32[]{:S(2)}) collective-permute-start(f32[64,1536]{1,0:T(8,128)S(1)} %plus.5.p), channel_id=1, source_target_pairs={{0,2},{2,0},{1,3},{3,1},{4,6},{6,4},{5,7},{7,5},{8,10},{10,8},{9,1... | collective-permute-start | bytes 1179656 | tf_op jit(solution)/shard_map/ppermute | solution.py:573
  64.6 12.3 %collective-permute-start.2 = (f32[64,1536]{1,0:T(8,128)S(1)}, f32[64,1536]{1,0:T(8,128)S(1)}, u32[]{:S(2)}, u32[]{:S(2)}) collective-permute-start(f32[64,1536]{1,0:T(8,128)S(1)} %get-tuple-element.218), channel_id=1, source_target_pairs={{0,1},{1,0},{2,3},{3,2},{4,5},{5,4},{6,7},{7,6},{8,9},{9,8},{10,11... | collective-permute-start | bytes 1179656 | tf_op jit(solution)/shard_map/ppermute | solution.py:573
  65.2 11.7 %collective-permute-start.3 = (f32[64,1536]{1,0:T(8,128)S(1)}, f32[64,1536]{1,0:T(8,128)S(1)}, u32[]{:S(2)}, u32[]{:S(2)}) collective-permute-start(f32[64,1536]{1,0:T(8,128)S(1)} %get-tuple-element.220), channel_id=1, source_target_pairs={{0,1},{1,0},{2,3},{3,2},{4,5},{5,4},{6,7},{7,6},{8,9},{9,8},{10,11... | collective-permute-start | bytes 1179656 | tf_op jit(solution)/shard_map/ppermute | solution.py:573
  68.4 11.4 %collective-permute-start.6 = (f32[64,1536]{1,0:T(8,128)S(1)}, f32[64,1536]{1,0:T(8,128)S(1)}, u32[]{:S(2)}, u32[]{:S(2)}) collective-permute-start(f32[64,1536]{1,0:T(8,128)S(1)} %dual_row.3.refs_0_.ua), channel_id=1, source_target_pairs={{0,1},{1,0},{2,3},{3,2},{4,5},{5,4},{6,7},{7,6},{8,9},{9,8},{10,11... | collective-permute-start | bytes 1179656 | tf_op jit(solution)/shard_map/ppermute | solution.py:573
  77.0 3.8 %collective-permute-start.4 = (f32[64,1536]{1,0:T(8,128)S(1)}, f32[64,1536]{1,0:T(8,128)S(1)}, u32[]{:S(2)}, u32[]{:S(2)}) collective-permute-start(f32[64,1536]{1,0:T(8,128)S(1)} %dual_row.2.refs_1_.ub), channel_id=1, source_target_pairs={{0,1},{1,0},{2,3},{3,2},{4,5},{5,4},{6,7},{7,6},{8,9},{9,8},{10,11... | collective-permute-start | bytes 1179656 | tf_op jit(solution)/shard_map/ppermute | solution.py:573
  95.8 14.9 %collective-permute-start.7 = (f32[64,1536]{1,0:T(8,128)S(1)}, f32[64,1536]{1,0:T(8,128)S(1)}, u32[]{:S(2)}, u32[]{:S(2)}) collective-permute-start(f32[64,1536]{1,0:T(8,128)S(1)} %get-tuple-element.278), channel_id=1, source_target_pairs={{0,2},{2,0},{1,3},{3,1},{4,6},{6,4},{5,7},{7,5},{8,10},{10,8},{9,1... | collective-permute-start | bytes 1179656 | tf_op jit(solution)/shard_map/ppermute | solution.py:573
  126.3 3.1 %collective-permute-start.8 = (f32[64,1536]{1,0:T(8,128)S(1)}, f32[64,1536]{1,0:T(8,128)S(1)}, u32[]{:S(2)}, u32[]{:S(2)}) collective-permute-start(f32[64,1536]{1,0:T(8,128)S(1)} %loss_part.10), channel_id=1, source_target_pairs={{0,1},{1,0},{2,3},{3,2},{4,5},{5,4},{6,7},{7,6},{8,9},{9,8},{10,11... | collective-permute-start | bytes 1179656 | tf_op jit(solution)/shard_map/ppermute | solution.py:573
  129.5 12.0 %collective-permute-start.9 = (f32[64,1536]{1,0:T(8,128)S(1)}, f32[64,1536]{1,0:T(8,128)S(1)}, u32[]{:S(2)}, u32[]{:S(2)}) collective-permute-start(f32[64,1536]{1,0:T(8,128)S(1)} %plus.6), channel_id=1, source_target_pairs={{0,2},{2,0},{1,3},{3,1},{4,6},{6,4},{5,7},{7,5},{8,10},{10,8},{9,1... | collective-permute-start | bytes 1179656 | tf_op jit(solution)/shard_map/ppermute | solution.py:573
  141.9 16.6 %collective-permute-start.10 = (f32[64,1536]{1,0:T(8,128)S(1)}, f32[64,1536]{1,0:T(8,128)S(1)}, u32[]{:S(2)}, u32[]{:S(2)}) collective-permute-start(f32[64,1536]{1,0:T(8,128)S(1)} %get-tuple-element.320.own), channel_id=1, source_target_pairs={{0,2},{2,0},{1,3},{3,1},{4,6},{6,4},{5,7},{7,5},{8,10},{10,8},{9,1... | collective-permute-start | bytes 1179656 | tf_op jit(solution)/shard_map/ppermute | solution.py:573
  144.4 14.1 %collective-permute-start.11 = (f32[64,1536]{1,0:T(8,128)S(1)}, f32[64,1536]{1,0:T(8,128)S(1)}, u32[]{:S(2)}, u32[]{:S(2)}) collective-permute-start(f32[64,1536]{1,0:T(8,128)S(1)} %get-tuple-element.320.own), channel_id=1, source_target_pairs={{0,1},{1,0},{2,3},{3,2},{4,5},{5,4},{6,7},{7,6},{8,9},{9,8},{10,11... | collective-permute-start | bytes 1179656 | tf_op jit(solution)/shard_map/ppermute | solution.py:573
  158.5 2.0 %collective-permute-start.12 = (f32[64,1536]{1,0:T(8,128)S(1)}, f32[64,1536]{1,0:T(8,128)S(1)}, u32[]{:S(2)}, u32[]{:S(2)}) collective-permute-start(f32[64,1536]{1,0:T(8,128)S(1)} %collective-permute-done.10.near), channel_id=1, source_target_pairs={{0,1},{1,0},{2,3},{3,2},{4,5},{5,4},{6,7},{7,6},{8,9},{9,8},{10,11... | collective-permute-start | bytes 1179656 | tf_op jit(solution)/shard_map/ppermute | solution.py:573

commit v6 on v4

--- a/solution.py
+++ b/solution.py
@@ -387,11 +387,16 @@
     )
 
 
-def plus(a, b):
-    def body(x, y, out):
-        out[...] = x[...] + y[...]
-
-    return call(body, "plus", (a, b), shape(*a.shape), nbytes=12 * a.size)
+def plus(a, b, pieces=1):
+    rows = a.shape[0] // pieces
+
+    def body(x, y, *outs):
+        for i, out in enumerate(outs):
+            at = slice(i * rows, (i + 1) * rows)
+            out[...] = x[at, :] + y[at, :]
+
+    outs = [shape(rows, a.shape[1])] * pieces
+    return call(body, "plus", (a, b), outs, nbytes=12 * a.size)
 
 
 def own_and_other(keeps, takes):
@@ -415,12 +420,20 @@
     return jnp.clip(duals + STEP_U * (loss - t_bar[:, 0:1]), 0.0, 1.0)
 
 
-def dual_row(part, other, duals, t_bar, quarter, width):
-    def body(p, o, u, t, fresh):
+def dual_row(parts, others, duals, t_bar, quarter, width):
+    count = len(parts)
+    rows = K // count
+
+    def body(*refs):
+        u, t, fresh = refs[2 * count :]
         base = row_base(1, quarter, width)
-        fresh[...] = dual_step(p[...] + o[...], u[:, pl.ds(base, width)], t[...])
-
-    return call(body, "dual_row", (part, other, duals, t_bar), shape(K, width), nbytes=16 * K * width)
+        for i in range(count):
+            at = slice(i * rows, (i + 1) * rows)
+            loss = refs[i][...] + refs[count + i][...]
+            fresh[at, :] = dual_step(loss, u[at, pl.ds(base, width)], t[at, :])
+
+    operands = (*parts, *others, duals, t_bar)
+    return call(body, "dual_row", operands, shape(K, width), nbytes=16 * K * width)
 
 
 def gradient_part(terms, returns, before, width):
@@ -572,12 +585,17 @@
     return lax.ppermute(values, axis, [(0, 1), (1, 0)])
 
 
-def plus_gathered(a, both):
-    def body(x, y, out):
-        core = lax.axis_index("core")
-        out[...] = x[...] + y[1 - core]
-
-    return call(body, "plus", (a, both), shape(*a.shape), nbytes=12 * a.size)
+def plus_gathered(a, both, pieces=1):
+    rows = a.shape[0] // pieces
+
+    def body(x, y, *outs):
+        other = 1 - lax.axis_index("core")
+        for i, out in enumerate(outs):
+            at = slice(i * rows, (i + 1) * rows)
+            out[...] = x[at, :] + y[other, at, :]
+
+    outs = [shape(rows, a.shape[1])] * pieces
+    return call(body, "plus", (a, both), outs, nbytes=12 * a.size)
 
 
 def exchanged(payload, others):
@@ -618,13 +636,13 @@
     send, send_tail_a = loss_part(bars, returns, (0,), lambda: 0, width)
     take = across(send, "core")
     keep, keep_tail_a = loss_part(bars, returns, (1,), lambda: 0, width)
-    part_a = plus(keep, take)
+    part_a = plus(keep, take, 1)
     take_tail_a = across(send_tail_a, "core")
     part_a, bars = lax.optimization_barrier((part_a, bars))
     send, send_tail_b, keep, keep_tail_b = loss_part(bars, returns, (0, 1), lambda: 1, width)
-    part_b = plus_gathered(keep, lax.all_gather(send, "core"))
+    part_b = plus_gathered(keep, lax.all_gather(send, "core"), 2)
     take_tail_b = across(send_tail_b, "core")
-    others = (across(part_a, "xh"), across(part_b, "xh"))
+    others = [[across(piece, "xh") for piece in part] for part in (part_a, part_b)]
     send_tail, tail_a = own_and_other((keep_tail_a, keep_tail_b), (take_tail_a, take_tail_b))
 
     ua = dual_row(part_a, others[0], duals, bar1, 0, width)
@@ -662,10 +680,10 @@
     (send,) = loss_part(bars, returns, (0,), far_quarter, width)
     take = across(send, "core")
     (keep,) = loss_part(bars, returns, (1,), far_quarter, width)
-    part_a = plus(keep, take)
+    (part_a,) = plus(keep, take)
     part_a, bars, v2 = lax.optimization_barrier((part_a, bars, v2))
     send, keep = loss_part(bars, returns, (0, 1), own_quarter, width)
-    part_b = plus_gathered(keep, lax.all_gather(send, "core"))
+    (part_b,) = plus_gathered(keep, lax.all_gather(send, "core"))
     parts = (part_a, part_b)
     other = across(parts[0], "xh")
     weights_out, threshold_out = averaged((v2, v1, weights), (t2, t1, t0))

time: 162 us -> 162 us (level)
    ppermute x13 -> x14, starting transfers between devices: 19.5 us -> 20.6 us  [across(): return lax.ppermute(values, axis, [(0, 1), (1, 0)])]
    ppermute x13 -> x14, waiting for transfers between devices: 13.2 us -> 12.8 us  [across(): return lax.ppermute(values, axis, [(0, 1), (1, 0)])]
  transfers between devices with their start and end apart: 13 -> 14, of which waited for: 4 -> 4; matrix products, arithmetic and copies ran while one was open for 0% -> 0% of each run, Pallas kernels for 9% -> 9%
where the time goes in v6:
time: 162 us; the launch traced here: 161 us
  blocking collectives  98.2 us (61%)
  Pallas kernels  28.9 us (18%)
  starting transfers between devices  20.6 us (13%)
  waiting for transfers between devices  12.8 us (8%)
    all_to_all x4, blocking collectives, exchanged(): received = lax.all_to_all(payload, SCEN, 0, 0)  60.4 us
    pallas_call x27, Pallas kernels, call(): pl.pallas_call(body, in_specs=in_specs or [VMEM] * len(operands), out_spe...  28.9 us
    ppermute x14, starting transfers between devices, across(): return lax.ppermute(values, axis, [(0, 1), (1, 0)])  20.6 us
    ppermute x14, waiting for transfers between devices, across(): return lax.ppermute(values, axis, [(0, 1), (1, 0)])  12.8 us
    all_to_all x1, blocking collectives, local(): sums = lax.all_to_all(sums, ALL, 0, 0)  12.7 us
    all_gather x1, blocking collectives, local(): gathered = lax.all_gather(own, ASSET)  11.6 us
    all_gather x1, blocking collectives, local(): gathered_first = lax.all_gather(own_first, ASSET)  8.54 us
  transfers between devices with their start and end apart: 14, of which 4 were waited for; matrix products, arithmetic and copies ran while one was open for 0% of the time, Pallas kernels for 9%

profile of v6, /device:TPU:1, one launch (start us, length us, event | category | flops | bytes accessed | tf_op | source)
XLA Modules:
  0.0 161.5 jit_solution(648077230281443551)
XLA Ops:
  0.7 7.8 %first_gradient.1 = (f32[32,24,128]{2,1,0:T(8,128)S(1)}, f32[1,64]{1,0:T(1,128)S(1)}, bf16[6144,1536]{1,0:T(8,128)(2,1)S(1)}, f32[64,6144]{1,0:T(8,128)S(1)}) custom-call(f32[64,6144]{1,0:T(8,128)} %u.1, bf16[6144,1536]{1,0:T(8,128)(2,1)} %r.1), custom_call_target="tpu_custom_call" | custom-call | flops 12079595 | bytes 188743 | tf_op jit(solution)/shard_map/first_gradient/pallas_call | solution.py:97
  8.5 19.6 %all_to_all.25.got = f32[32,24,128]{2,1,0:T(8,128)S(1)} all-to-all(f32[32,24,128]{2,1,0:T(8,128)S(1)} %get-tuple-element.174), channel_id=1, replica_groups=mesh['z'=4,'y'=4,'xl'=2,'xh'=2,'core'=2] {'z','y','xl'}, dimensions={0} | all-to-all | bytes 786432 | tf_op jit(solution)/shard_map/all_to_all | solution.py:603
  28.2 8.5 %all-gather = f32[192,128]{1,0:T(8,128)S(1)} all-gather(f32[48,128]{1,0:T(8,128)S(1)} %get-tuple-element.267.mine.mean), channel_id=2, replica_groups=mesh['z'=4,'y'=4,'xl'=2,'xh'=2,'core'=2] {'xh','core'}, dimensions={0}, use_global_device_ids=true | all-gather | bytes 122880 | tf_op jit(solution)/shard_map/all_gather | solution.py:624
  37.5 13.8 %all_to_all.26.got = f32[32,13,2,128]{3,2,1,0:T(2,128)S(1)} all-to-all(f32[32,13,2,128]{3,2,1,0:T(2,128)S(1)} %get-tuple-element.196), channel_id=1, replica_groups=mesh['z'=4,'y'=4,'xl'=2,'xh'=2,'core'=2] {'z','y','xl'}, dimensions={0} | all-to-all | bytes 851968 | tf_op jit(solution)/shard_map/all_to_all | solution.py:603
  51.7 1.5 loss_part.7
  53.1 1.7 %collective-permute-start = (f32[64,1536]{1,0:T(8,128)S(1)}, f32[64,1536]{1,0:T(8,128)S(1)}, u32[]{:S(2)}, u32[]{:S(2)}) collective-permute-start(f32[64,1536]{1,0:T(8,128)S(1)} %get-tuple-element.213), channel_id=1, source_target_pairs={{0,1},{1,0},{2,3},{3,2},{4,5},{5,4},{6,7},{7,6},{8,9},{9,8},{10,11... | collective-permute-start | bytes 1179656 | tf_op jit(solution)/shard_map/ppermute | solution.py:585
  56.4 2.5 %collective-permute-start.6 = (f32[64,1536]{1,0:T(8,128)S(1)}, f32[64,1536]{1,0:T(8,128)S(1)}, u32[]{:S(2)}, u32[]{:S(2)}) collective-permute-start(f32[64,1536]{1,0:T(8,128)S(1)} %plus.4.refs_0_), channel_id=1, source_target_pairs={{0,2},{2,0},{1,3},{3,1},{4,6},{6,4},{5,7},{7,5},{8,10},{10,8},{9,1... | collective-permute-start | bytes 1179656 | tf_op jit(solution)/shard_map/ppermute | solution.py:585
  59.0 2.7 %loss_part.8 = (f32[64,1536]{1,0:T(8,128)S(1)}, f32[64,1536]{1,0:T(8,128)S(1)}, f32[64,1536]{1,0:T(8,128)S(1)}, f32[64,1536]{1,0:T(8,128)S(1)}) custom-call(bf16[128,1536]{1,0:T(8,128)(2,1)S(1)} %get-tuple-element.214.b, bf16[6144,1536]{1,0:T(8,128)(2,1)S(1)} %get-tuple-element.304.r), custom_call_target="tpu_custom_call" | custom-call | flops 12079595 | bytes 94371 | tf_op jit(solution)/shard_map/loss_part/pallas_call | solution.py:97
  62.4 2.4 %all-gather.1 = f32[128,1536]{1,0:T(8,128)S(1)} all-gather(f32[64,1536]{1,0:T(8,128)S(1)} %get-tuple-element.216), channel_id=3, replica_groups=mesh['z'=4,'y'=4,'xl'=2,'xh'=2,'core'=2] {'core'}, dimensions={0}, use_global_device_ids=true | all-gather | bytes 1179648 | tf_op jit(solution)/shard_map/all_gather | solution.py:643
  65.4 2.4 %collective-permute-start.2 = (f32[32,1536]{1,0:T(8,128)S(1)}, f32[32,1536]{1,0:T(8,128)S(1)}, u32[]{:S(2)}, u32[]{:S(2)}) collective-permute-start(f32[32,1536]{1,0:T(8,128)S(1)} %get-tuple-element.218.refs_1_), channel_id=1, source_target_pairs={{0,2},{2,0},{1,3},{3,1},{4,6},{6,4},{5,7},{7,5},{8,10},{10,8},{9,1... | collective-permute-start | bytes 589832 | tf_op jit(solution)/shard_map/ppermute | solution.py:585
  67.9 5.0 %collective-permute-done.1.refs_2_ = f32[32,1536]{1,0:T(8,128)S(1)} collective-permute-done((f32[32,1536]{1,0:T(8,128)S(1)}, f32[32,1536]{1,0:T(8,128)S(1)}, u32[]{:S(2)}, u32[]{:S(2)}) %collective-permute-start.1) | collective-permute-done | bytes 196640 | tf_op jit(solution)/shard_map/ppermute | solution.py:585
  72.8 4.2 %collective-permute-done.2.refs_3_ = f32[32,1536]{1,0:T(8,128)S(1)} collective-permute-done((f32[32,1536]{1,0:T(8,128)S(1)}, f32[32,1536]{1,0:T(8,128)S(1)}, u32[]{:S(2)}, u32[]{:S(2)}) %collective-permute-start.2) | collective-permute-done | bytes 196640 | tf_op jit(solution)/shard_map/ppermute | solution.py:585
  78.7 1.7 %gradient_part.2 = (f32[64,1536]{1,0:T(8,128)S(1)}, f32[64,128]{1,0:T(8,128)S(1)}) custom-call(bf16[6144,1536]{1,0:T(8,128)(2,1)S(1)} %get-tuple-element.304.r, f32[64,1536]{1,0:T(8,128)S(1)} %dual_row.3.refs_0_.ua, f32[64,1536]{1,0:T(8,128)S(1)} %dual_row.2.refs_1_.ub), custom_call_target="tpu_custom_call" | custom-call | flops 6039797 | bytes 94371 | tf_op jit(solution)/shard_map/gradient_part/pallas_call | solution.py:97
  82.6 13.2 %all_to_all.27.got = f32[32,24,128]{2,1,0:T(8,128)S(1)} all-to-all(f32[32,24,128]{2,1,0:T(8,128)S(1)} %get-tuple-element.243), channel_id=1, replica_groups=mesh['z'=4,'y'=4,'xl'=2,'xh'=2,'core'=2] {'z','y','xl'}, dimensions={0} | all-to-all | bytes 786432 | tf_op jit(solution)/shard_map/all_to_all | solution.py:603
  95.8 2.5 %collective-permute-start.8 = (f32[64,1536]{1,0:T(8,128)S(1)}, f32[64,1536]{1,0:T(8,128)S(1)}, u32[]{:S(2)}, u32[]{:S(2)}) collective-permute-start(f32[64,1536]{1,0:T(8,128)S(1)} %get-tuple-element.282), channel_id=1, source_target_pairs={{0,2},{2,0},{1,3},{3,1},{4,6},{6,4},{5,7},{7,5},{8,10},{10,8},{9,1... | collective-permute-start | bytes 1179656 | tf_op jit(solution)/shard_map/ppermute | solution.py:585
  98.4 11.6 %all-gather.2 = f32[128,128]{1,0:T(8,128)S(1)} all-gather(f32[32,128]{1,0:T(8,128)S(1)} %get-tuple-element.265.mine), channel_id=4, replica_groups=mesh['z'=4,'y'=4,'xl'=2,'xh'=2,'core'=2] {'xh','core'}, dimensions={0}, use_global_device_ids=true | all-gather | bytes 81920 | tf_op jit(solution)/shard_map/all_gather | solution.py:664
  110.7 13.9 %all_to_all.28.got = f32[32,13,2,128]{3,2,1,0:T(2,128)S(1)} all-to-all(f32[32,13,2,128]{3,2,1,0:T(2,128)S(1)} %get-tuple-element.283), channel_id=1, replica_groups=mesh['z'=4,'y'=4,'xl'=2,'xh'=2,'core'=2] {'z','y','xl'}, dimensions={0} | all-to-all | bytes 851968 | tf_op jit(solution)/shard_map/all_to_all | solution.py:603
  126.4 1.7 %collective-permute-start.9 = (f32[64,1536]{1,0:T(8,128)S(1)}, f32[64,1536]{1,0:T(8,128)S(1)}, u32[]{:S(2)}, u32[]{:S(2)}) collective-permute-start(f32[64,1536]{1,0:T(8,128)S(1)} %loss_part.10), channel_id=1, source_target_pairs={{0,1},{1,0},{2,3},{3,2},{4,5},{5,4},{6,7},{7,6},{8,9},{9,8},{10,11... | collective-permute-start | bytes 1179656 | tf_op jit(solution)/shard_map/ppermute | solution.py:585
  129.6 2.5 %collective-permute-start.10 = (f32[64,1536]{1,0:T(8,128)S(1)}, f32[64,1536]{1,0:T(8,128)S(1)}, u32[]{:S(2)}, u32[]{:S(2)}) collective-permute-start(f32[64,1536]{1,0:T(8,128)S(1)} %plus.6), channel_id=1, source_target_pairs={{0,2},{2,0},{1,3},{3,1},{4,6},{6,4},{5,7},{7,5},{8,10},{10,8},{9,1... | collective-permute-start | bytes 1179656 | tf_op jit(solution)/shard_map/ppermute | solution.py:585
  132.1 2.7 %loss_part.11 = (f32[64,1536]{1,0:T(8,128)S(1)}, f32[64,1536]{1,0:T(8,128)S(1)}) custom-call(bf16[64,1536]{1,0:T(8,128)(2,1)S(1)} %get-tuple-element.306.b, bf16[6144,1536]{1,0:T(8,128)(2,1)S(1)} %get-tuple-element.304.r), custom_call_target="tpu_custom_call" | custom-call | flops 6039797 | bytes 94371 | tf_op jit(solution)/shard_map/loss_part/pallas_call | solution.py:97
  134.7 2.5 %all-gather.3 = f32[128,1536]{1,0:T(8,128)S(1)} all-gather(f32[64,1536]{1,0:T(8,128)S(1)} %get-tuple-element.308), channel_id=5, replica_groups=mesh['z'=4,'y'=4,'xl'=2,'xh'=2,'core'=2] {'core'}, dimensions={0}, use_global_device_ids=true | all-gather | bytes 1179648 | tf_op jit(solution)/shard_map/all_gather | solution.py:686
  138.2 3.4 %collective-permute-done.10.o = f32[64,1536]{1,0:T(8,128)S(1)} collective-permute-done((f32[64,1536]{1,0:T(8,128)S(1)}, f32[64,1536]{1,0:T(8,128)S(1)}, u32[]{:S(2)}, u32[]{:S(2)}) %collective-permute-start.10) | collective-permute-done | bytes 393248 | tf_op jit(solution)/shard_map/ppermute | solution.py:585
  142.0 2.5 %collective-permute-start.11 = (f32[64,1536]{1,0:T(8,128)S(1)}, f32[64,1536]{1,0:T(8,128)S(1)}, u32[]{:S(2)}, u32[]{:S(2)}) collective-permute-start(f32[64,1536]{1,0:T(8,128)S(1)} %get-tuple-element.324.own), channel_id=1, source_target_pairs={{0,2},{2,0},{1,3},{3,1},{4,6},{6,4},{5,7},{7,5},{8,10},{10,8},{9,1... | collective-permute-start | bytes 1179656 | tf_op jit(solution)/shard_map/ppermute | solution.py:585
  145.9 12.7 %all_to_all.29.got = f32[128,1,128]{2,1,0:T(1,128)S(1)} all-to-all(f32[128,1,128]{2,1,0:T(1,128)S(1)} %get-tuple-element.325), channel_id=1, replica_groups=mesh['z'=4,'y'=4,'xl'=2,'xh'=2,'core'=2] {'z','y','xl','xh','core'}, dimensions={0} | all-to-all | bytes 131072 | tf_op jit(solution)/shard_map/all_to_all | solution.py:697
  (50 shorter events, 17.5 us)
Async XLA Ops:
  0.6 27.5 %copy-start = (f32[64,1536]{1,0:T(8,128)S(1)}, f32[64,1536]{1,0:T(8,128)}, u32[]{:S(2)}) copy-start(f32[64,1536]{1,0:T(8,128)} %v0) | copy-start | bytes 1179652
  0.6 27.5 %copy-start.2 = (f32[1536]{0:T(1024)S(1)}, f32[1536]{0:T(1024)}, u32[]{:S(2)}) copy-start(f32[1536]{0:T(1024)} %more) | copy-start | bytes 18436
  8.4 28.3 %copy-start.3 = (f32[64]{0:T(128)S(1)}, f32[64]{0:T(128)}, u32[]{:S(2)}) copy-start(f32[64]{0:T(128)} %param.9) | copy-start | bytes 772
  8.4 28.3 %copy-start.4 = (f32[64]{0:T(128)S(1)}, f32[64]{0:T(128)}, u32[]{:S(2)}) copy-start(f32[64]{0:T(128)} %param.13) | copy-start | bytes 772
  8.4 42.9 %copy-start.1 = (f32[64]{0:T(128)S(1)}, f32[64]{0:T(128)}, u32[]{:S(2)}) copy-start(f32[64]{0:T(128)} %param.11) | copy-start | bytes 772
  53.1 3.2 %collective-permute-start = (f32[64,1536]{1,0:T(8,128)S(1)}, f32[64,1536]{1,0:T(8,128)S(1)}, u32[]{:S(2)}, u32[]{:S(2)}) collective-permute-start(f32[64,1536]{1,0:T(8,128)S(1)} %get-tuple-element.213), channel_id=1, source_target_pairs={{0,1},{1,0},{2,3},{3,2},{4,5},{5,4},{6,7},{7,6},{8,9},{9,8},{10,11... | collective-permute-start | bytes 1179656 | tf_op jit(solution)/shard_map/ppermute | solution.py:585
  54.8 23.5 %collective-permute-start.3 = (f32[64,1536]{1,0:T(8,128)S(1)}, f32[64,1536]{1,0:T(8,128)S(1)}, u32[]{:S(2)}, u32[]{:S(2)}) collective-permute-start(f32[64,1536]{1,0:T(8,128)S(1)} %get-tuple-element.222), channel_id=1, source_target_pairs={{0,1},{1,0},{2,3},{3,2},{4,5},{5,4},{6,7},{7,6},{8,9},{9,8},{10,11... | collective-permute-start | bytes 1179656 | tf_op jit(solution)/shard_map/ppermute | solution.py:585
  56.4 20.7 %collective-permute-start.6 = (f32[64,1536]{1,0:T(8,128)S(1)}, f32[64,1536]{1,0:T(8,128)S(1)}, u32[]{:S(2)}, u32[]{:S(2)}) collective-permute-start(f32[64,1536]{1,0:T(8,128)S(1)} %plus.4.refs_0_), channel_id=1, source_target_pairs={{0,2},{2,0},{1,3},{3,1},{4,6},{6,4},{5,7},{7,5},{8,10},{10,8},{9,1... | collective-permute-start | bytes 1179656 | tf_op jit(solution)/shard_map/ppermute | solution.py:585
  61.6 16.7 %collective-permute-start.4 = (f32[64,1536]{1,0:T(8,128)S(1)}, f32[64,1536]{1,0:T(8,128)S(1)}, u32[]{:S(2)}, u32[]{:S(2)}) collective-permute-start(f32[64,1536]{1,0:T(8,128)S(1)} %get-tuple-element.224), channel_id=1, source_target_pairs={{0,1},{1,0},{2,3},{3,2},{4,5},{5,4},{6,7},{7,6},{8,9},{9,8},{10,11... | collective-permute-start | bytes 1179656 | tf_op jit(solution)/shard_map/ppermute | solution.py:585
  64.8 8.0 %collective-permute-start.1 = (f32[32,1536]{1,0:T(8,128)S(1)}, f32[32,1536]{1,0:T(8,128)S(1)}, u32[]{:S(2)}, u32[]{:S(2)}) collective-permute-start(f32[32,1536]{1,0:T(8,128)S(1)} %get-tuple-element.217.refs_0_), channel_id=1, source_target_pairs={{0,2},{2,0},{1,3},{3,1},{4,6},{6,4},{5,7},{7,5},{8,10},{10,8},{9,1... | collective-permute-start | bytes 589832 | tf_op jit(solution)/shard_map/ppermute | solution.py:585
  65.4 11.6 %collective-permute-start.2 = (f32[32,1536]{1,0:T(8,128)S(1)}, f32[32,1536]{1,0:T(8,128)S(1)}, u32[]{:S(2)}, u32[]{:S(2)}) collective-permute-start(f32[32,1536]{1,0:T(8,128)S(1)} %get-tuple-element.218.refs_1_), channel_id=1, source_target_pairs={{0,2},{2,0},{1,3},{3,1},{4,6},{6,4},{5,7},{7,5},{8,10},{10,8},{9,1... | collective-permute-start | bytes 589832 | tf_op jit(solution)/shard_map/ppermute | solution.py:585
  77.3 3.2 %collective-permute-start.7 = (f32[64,1536]{1,0:T(8,128)S(1)}, f32[64,1536]{1,0:T(8,128)S(1)}, u32[]{:S(2)}, u32[]{:S(2)}) collective-permute-start(f32[64,1536]{1,0:T(8,128)S(1)} %dual_row.3.refs_0_.ua), channel_id=1, source_target_pairs={{0,1},{1,0},{2,3},{3,2},{4,5},{5,4},{6,7},{7,6},{8,9},{9,8},{10,11... | collective-permute-start | bytes 1179656 | tf_op jit(solution)/shard_map/ppermute | solution.py:585
  78.4 3.0 %collective-permute-start.5 = (f32[64,1536]{1,0:T(8,128)S(1)}, f32[64,1536]{1,0:T(8,128)S(1)}, u32[]{:S(2)}, u32[]{:S(2)}) collective-permute-start(f32[64,1536]{1,0:T(8,128)S(1)} %dual_row.2.refs_1_.ub), channel_id=1, source_target_pairs={{0,1},{1,0},{2,3},{3,2},{4,5},{5,4},{6,7},{7,6},{8,9},{9,8},{10,11... | collective-permute-start | bytes 1179656 | tf_op jit(solution)/shard_map/ppermute | solution.py:585
  95.8 14.9 %collective-permute-start.8 = (f32[64,1536]{1,0:T(8,128)S(1)}, f32[64,1536]{1,0:T(8,128)S(1)}, u32[]{:S(2)}, u32[]{:S(2)}) collective-permute-start(f32[64,1536]{1,0:T(8,128)S(1)} %get-tuple-element.282), channel_id=1, source_target_pairs={{0,2},{2,0},{1,3},{3,1},{4,6},{6,4},{5,7},{7,5},{8,10},{10,8},{9,1... | collective-permute-start | bytes 1179656 | tf_op jit(solution)/shard_map/ppermute | solution.py:585
  126.4 3.1 %collective-permute-start.9 = (f32[64,1536]{1,0:T(8,128)S(1)}, f32[64,1536]{1,0:T(8,128)S(1)}, u32[]{:S(2)}, u32[]{:S(2)}) collective-permute-start(f32[64,1536]{1,0:T(8,128)S(1)} %loss_part.10), channel_id=1, source_target_pairs={{0,1},{1,0},{2,3},{3,2},{4,5},{5,4},{6,7},{7,6},{8,9},{9,8},{10,11... | collective-permute-start | bytes 1179656 | tf_op jit(solution)/shard_map/ppermute | solution.py:585
  129.6 12.0 %collective-permute-start.10 = (f32[64,1536]{1,0:T(8,128)S(1)}, f32[64,1536]{1,0:T(8,128)S(1)}, u32[]{:S(2)}, u32[]{:S(2)}) collective-permute-start(f32[64,1536]{1,0:T(8,128)S(1)} %plus.6), channel_id=1, source_target_pairs={{0,2},{2,0},{1,3},{3,1},{4,6},{6,4},{5,7},{7,5},{8,10},{10,8},{9,1... | collective-permute-start | bytes 1179656 | tf_op jit(solution)/shard_map/ppermute | solution.py:585
  142.0 16.6 %collective-permute-start.11 = (f32[64,1536]{1,0:T(8,128)S(1)}, f32[64,1536]{1,0:T(8,128)S(1)}, u32[]{:S(2)}, u32[]{:S(2)}) collective-permute-start(f32[64,1536]{1,0:T(8,128)S(1)} %get-tuple-element.324.own), channel_id=1, source_target_pairs={{0,2},{2,0},{1,3},{3,1},{4,6},{6,4},{5,7},{7,5},{8,10},{10,8},{9,1... | collective-permute-start | bytes 1179656 | tf_op jit(solution)/shard_map/ppermute | solution.py:585
  144.5 14.1 %collective-permute-start.12 = (f32[64,1536]{1,0:T(8,128)S(1)}, f32[64,1536]{1,0:T(8,128)S(1)}, u32[]{:S(2)}, u32[]{:S(2)}) collective-permute-start(f32[64,1536]{1,0:T(8,128)S(1)} %get-tuple-element.324.own), channel_id=1, source_target_pairs={{0,1},{1,0},{2,3},{3,2},{4,5},{5,4},{6,7},{7,6},{8,9},{9,8},{10,11... | collective-permute-start | bytes 1179656 | tf_op jit(solution)/shard_map/ppermute | solution.py:585
  158.6 2.0 %collective-permute-start.13 = (f32[64,1536]{1,0:T(8,128)S(1)}, f32[64,1536]{1,0:T(8,128)S(1)}, u32[]{:S(2)}, u32[]{:S(2)}) collective-permute-start(f32[64,1536]{1,0:T(8,128)S(1)} %collective-permute-done.11.near), channel_id=1, source_target_pairs={{0,1},{1,0},{2,3},{3,2},{4,5},{5,4},{6,7},{7,6},{8,9},{9,8},{10,11... | collective-permute-start | bytes 1179656 | tf_op jit(solution)/shard_map/ppermute | solution.py:585
